TPU v7x, 32 devices: a whole 2x2x4 slice. The times are simulated.
32 devices in a mesh: layer: 2 (over x), expert: 16 (over z, y, core).
Axes of the slice: x: 2, y: 2, z: 4, core: 2. Of those that a mesh axis runs over, the one named last changes fastest.
Arguments:
- weights: bfloat16 [16384, 7168], P(('layer', 'expert')), parts along dimension 0, may hold values from -6 to 6
- loadings: bfloat16 [16384, 256], P(('layer', 'expert')), parts along dimension 0, may hold values from -0.375 to 0.375
- bases: bfloat16 [128, 256, 7168], P('layer', 'expert'), parts along dimension 0, may hold values from -1.5 to 1.5
- coeff: float32 [8, 64], P('layer'), parts along dimension 0, may hold values from -2 to 2
Outputs:
- grad_a: float32 [16384, 256], P(('layer', 'expert')), parts along dimension 0
- grad_b: bfloat16 [128, 256, 7168], P('layer', 'expert'), parts along dimension 0
- grad_c: float32 [8, 64], P('layer'), parts along dimension 0
There are 2 independent parts, one for each index of `layer`. A program takes and returns all parts, laid end to end along the dimension named above; each array names one. Nothing has to cross between parts.
All inputs are finite; a program needn't handle non-finite values.
Results may differ from a plain program's by a relative error of at most 0.0061.
Values may be sent and summed in bfloat16 or wider, within the bound.
No kernel may reach another device: no remote copies, remote signals or barrier semaphores. Data moves between devices by JAX's collectives and lax.ppermute only.
A program may use at most 128 MiB of HBM per device.

v0:
```python
import math

import jax
import jax.numpy as jnp
from jax import lax
from jax.sharding import PartitionSpec as P


def per_device(weights, loadings, bases, coeff):
    devices = lax.axis_size("expert")
    num_bases, rows_dev, width = bases.shape
    experts = coeff.shape[0]
    row_split = devices // experts
    rank_dim = rows_dev * devices
    mix_bf = jnp.tanh(coeff).astype(jnp.bfloat16)
    flat_bases = bases.reshape(num_bases, rows_dev * width)
    mixed_rows = jnp.dot(mix_bf, flat_bases, preferred_element_type=jnp.float32)
    mixed_rows = mixed_rows.astype(jnp.bfloat16).reshape(experts, rows_dev, width)
    outgoing = jnp.repeat(mixed_rows, row_split, axis=0)
    mixture = lax.all_to_all(outgoing, "expert", split_axis=0, concat_axis=1, tiled=True).reshape(
        rank_dim, width
    )
    product = jnp.dot(loadings, mixture, preferred_element_type=jnp.float32)
    residual = (product - weights.astype(jnp.float32)).astype(jnp.bfloat16)
    grad_a = lax.dot_general(
        residual, mixture, (((1,), (1,)), ((), ())), preferred_element_type=jnp.float32
    )
    grad_a = grad_a / math.sqrt(width)
    partial_value = lax.dot_general(
        loadings, residual, (((0,), (0,)), ((), ())), preferred_element_type=jnp.float32
    )
    mix_full = mix_bf.astype(jnp.float32)
    bases_full = bases.astype(jnp.float32)
    returned = lax.all_to_all(
        partial_value.reshape(devices, rows_dev, width),
        "expert",
        split_axis=0,
        concat_axis=0,
        tiled=True,
    )
    summed = returned.reshape(experts, row_split, rows_dev, width).sum(axis=1)
    grad_b = jnp.einsum("ek,erd->krd", mix_full, summed, precision=lax.Precision.HIGHEST)
    basis_inner = jnp.einsum("krd,erd->ek", bases_full, summed, precision=lax.Precision.HIGHEST)
    grad_b = (grad_b / math.sqrt(experts)).astype(jnp.bfloat16)
    total_inner = lax.psum(basis_inner, "expert")
    slope = 1.0 - jnp.tanh(coeff) ** 2
    grad_c = slope * total_inner / math.sqrt(rank_dim * width)
    return (grad_a, grad_b, grad_c)


def solution(mesh):
    in_specs = (
        P(("layer", "expert"), None),
        P(("layer", "expert"), None),
        P("layer", "expert", None),
        P("layer", None),
    )
    out_specs = (P(("layer", "expert"), None), P("layer", "expert", None), P("layer", None))
    return jax.shard_map(
        per_device, mesh=mesh, in_specs=in_specs, out_specs=out_specs, check_vma=False
    )
```

profile of v0, /device:TPU:0, one launch (start us, length us, event | category | flops | bytes accessed | tf_op | source)
XLA Modules:
  0.0 387.5 jit_solution(7125346387417299317)
XLA Ops:
  0.6 0.0 copy-start
  0.6 0.0 copy-start.3
  0.7 13.9 %copy.15 = bf16[8,8,16,7168]{3,1,2,0:T(8,128)(2,1)S(1)} copy(bf16[8,8,16,7168]{3,2,1,0:T(8,128)(2,1)} %bitcast.31) | data formatting | bytes 29360128
  14.6 0.0 copy-done.3
  14.6 2.0 convolution_convert_fusion
  16.6 0.3 copy.28
  16.9 2.2 broadcast_in_dim.3
  19.1 7.4 %all-to-all-start = ((bf16[16,16,7168]{2,1,0:T(8,128)(2,1)}), bf16[16,16,7168]{2,1,0:T(8,128)(2,1)}, u32[]{:S(2)}, u32[]{:S(2)}) async-start(bf16[16,16,7168]{2,1,0:T(8,128)(2,1)} %bitcast.34), calls=%async_computation | async-start | bytes 7340032 | tf_op jit(solution)/shard_map/all_to_all | solution.py:20
  26.6 10.4 %copy.10 = bf16[512,7168]{0,1:T(8,128)(2,1)} copy(bf16[512,7168]{1,0:T(8,128)(2,1)} %param.4) | data formatting | bytes 14680064 | tf_op args[0]
  37.0 58.1 %all-to-all-done = bf16[16,16,7168]{2,1,0:T(8,128)(2,1)} async-done(((bf16[16,16,7168]{2,1,0:T(8,128)(2,1)}), bf16[16,16,7168]{2,1,0:T(8,128)(2,1)}, u32[]{:S(2)}, u32[]{:S(2)}) %all-to-all-start) | async-done | bytes 3670048 | tf_op jit(solution)/shard_map/all_to_all | solution.py:20
  95.1 0.0 copy-done
  95.1 6.3 %fusion = bf16[512,7168]{0,1:T(8,128)(2,1)S(1)} fusion(bf16[512,7168]{0,1:T(8,128)(2,1)} %copy.10, bf16[256,7168]{1,0:T(8,128)(2,1)} %bitcast.1, bf16[512,256]{1,0:T(8,128)(2,1)S(1)} %copy-done), kind=kOutput, calls=%fused_computation.3 | convolution fusion | flops 1890058240 | bytes 18612224 | tf_op jit(solution)/shard_map/dot_general | solution.py:23
  101.5 0.0 copy-start.2
  101.5 5.4 %fusion.12 = f32[7168,256]{0,1:T(8,128)} fusion(bf16[512,7168]{0,1:T(8,128)(2,1)S(1)} %fusion, bf16[512,256]{1,0:T(8,128)(2,1)S(1)} %copy-done), kind=kOutput, calls=%fused_computation.16 | convolution fusion | flops 1879048192 | bytes 14942208 | tf_op jit(solution)/shard_map/dot_general | solution.py:29
  106.9 0.0 copy-done.2
  106.9 17.6 %all-to-all-start.1 = ((f32[16,16,7168]{2,1,0:T(8,128)}), f32[16,16,7168]{2,1,0:T(8,128)}, u32[]{:S(2)}, u32[]{:S(2)}) async-start(f32[16,16,7168]{2,1,0:T(8,128)} %bitcast.33), calls=%async_computation.1 | async-start | bytes 14680064 | tf_op jit(solution)/shard_map/all_to_all | solution.py:34
  124.5 7.0 %convolution_multiply_fusion = f32[512,256]{1,0:T(8,128)} fusion(bf16[512,7168]{0,1:T(8,128)(2,1)} %copy-done.2, bf16[256,7168]{1,0:T(8,128)(2,1)} %bitcast.1), kind=kOutput, calls=%fused_computation.10 | convolution fusion | flops 1879179264 | bytes 11534336 | tf_op jit(solution)/shard_map/dot_general | solution.py:25
  131.5 125.4 %all-to-all-done.1 = f32[16,16,7168]{2,1,0:T(8,128)} async-done(((f32[16,16,7168]{2,1,0:T(8,128)}), f32[16,16,7168]{2,1,0:T(8,128)}, u32[]{:S(2)}, u32[]{:S(2)}) %all-to-all-start.1) | async-done | bytes 7340064 | tf_op jit(solution)/shard_map/all_to_all | solution.py:34
  256.9 3.8 bitcast_reduce_fusion
  260.7 34.2 %fusion.6 = f32[4,64]{1,0:T(4,128)S(1)} fusion(bf16[64,16,7168]{2,1,0:T(8,128)(2,1)} %param.6, f32[4,16,7168]{2,1,0:T(8,128)S(1)} %bitcast_reduce_fusion), kind=kOutput, calls=%fused_computation.11 | convolution fusion | flops 352321536 | bytes 16516096 | tf_op jit(solution)/shard_map/krd,erd->ek/dot_general | solution.py:43
  294.9 15.0 %fusion.3 = bf16[64,16,7168]{2,0,1:T(8,128)(2,1)} fusion(f32[4,16,7168]{2,1,0:T(8,128)S(1)} %bitcast_reduce_fusion, f32[4,64]{1,0:T(4,128)S(1)} %copy-done.3), kind=kOutput, calls=%fused_computation.6 | convolution fusion | flops 367001856 | bytes 16516096 | tf_op jit(solution)/shard_map/ek,erd->krd/dot_general | solution.py:42
  309.9 60.3 %psum.7 = f32[4,64]{1,0:T(4,128)S(1)} all-reduce(f32[4,64]{1,0:T(4,128)S(1)} %fusion.6), channel_id=1, replica_groups=mesh['layer'=2,'expert'=16] {'expert'}, use_global_device_ids=true, to_apply=%region_1.0 | all-reduce | flops 256 | bytes 2048 | tf_op jit(solution)/shard_map/psum | solution.py:45
  370.2 0.6 multiply_multiply_fusion
  370.8 0.0 copy-start.1
  370.8 16.7 %copy.14 = bf16[64,16,7168]{2,1,0:T(8,128)(2,1)} copy(bf16[64,16,7168]{2,0,1:T(8,128)(2,1)} %fusion.3) | data formatting | bytes 29360128
  387.5 0.0 copy-done.1
Async XLA Ops:
  0.6 94.5 %copy-start = (bf16[512,256]{1,0:T(8,128)(2,1)S(1)}, bf16[512,256]{1,0:T(8,128)(2,1)}, u32[]{:S(2)}) copy-start(bf16[512,256]{1,0:T(8,128)(2,1)} %param.5) | copy-start | bytes 786436
  0.6 13.9 %copy-start.3 = (f32[4,64]{1,0:T(4,128)S(1)}, f32[4,64]{1,0:T(4,128)}, u32[]{:S(2)}) copy-start(f32[4,64]{1,0:T(4,128)} %param.7) | copy-start | bytes 3076
  19.1 76.0 %all-to-all-start = ((bf16[16,16,7168]{2,1,0:T(8,128)(2,1)}), bf16[16,16,7168]{2,1,0:T(8,128)(2,1)}, u32[]{:S(2)}, u32[]{:S(2)}) async-start(bf16[16,16,7168]{2,1,0:T(8,128)(2,1)} %bitcast.34), calls=%async_computation | async-start | bytes 7340032 | tf_op jit(solution)/shard_map/all_to_all | solution.py:20
  101.5 5.4 %copy-start.2 = (bf16[512,7168]{0,1:T(8,128)(2,1)}, bf16[512,7168]{0,1:T(8,128)(2,1)S(1)}, u32[]{:S(2)}) copy-start(bf16[512,7168]{0,1:T(8,128)(2,1)S(1)} %fusion) | copy-start | bytes 22020100
  106.9 150.0 %all-to-all-start.1 = ((f32[16,16,7168]{2,1,0:T(8,128)}), f32[16,16,7168]{2,1,0:T(8,128)}, u32[]{:S(2)}, u32[]{:S(2)}) async-start(f32[16,16,7168]{2,1,0:T(8,128)} %bitcast.33), calls=%async_computation.1 | async-start | bytes 14680064 | tf_op jit(solution)/shard_map/all_to_all | solution.py:34
  370.8 16.7 %copy-start.1 = (bf16[512,256]{1,0:T(8,128)(2,1)S(1)}, bf16[512,256]{1,0:T(8,128)(2,1)}, u32[]{:S(2)}) copy-start(bf16[512,256]{1,0:T(8,128)(2,1)} %param.5) | copy-start | bytes 786436
where the time goes:
time: 388 us; the launch traced here: 387 us
  waiting for transfers between devices  184 us (47%)
  matrix products  70 us (18%)
  blocking collectives  60.3 us (16%)
  local copies, waits for them, and re-layouts  43.6 us (11%)
  starting transfers between devices  25 us (6%)
  other arithmetic  4.37 us (1%)
    all_to_all x1, waiting for transfers between devices, per_device(): lax.all_to_all(partial_value.reshape(devices, rows_dev, width), 'expert',...  125 us
    psum x1, blocking collectives, per_device(): total_inner = lax.psum(basis_inner, 'expert')  60.3 us
    all_to_all x1, waiting for transfers between devices, per_device(): lax.all_to_all(outgoing, 'expert', split_axis=0, concat_axis=1, tiled=True)  58.1 us
    unnamed x12, local copies, waits for them, and re-layouts  41.3 us
    dot_general x1, matrix products, per_device(): jnp.einsum('krd,erd->ek', bases_full, summed, precision=lax.Precision.HIG...  34.2 us
    all_to_all x1, starting transfers between devices, per_device(): lax.all_to_all(partial_value.reshape(devices, rows_dev, width), 'expert',...  17.6 us
    dot_general x1, matrix products, per_device(): jnp.einsum('ek,erd->krd', mix_full, summed, precision=lax.Precision.HIGHEST)  15 us
  transfers between devices with their start and end apart: 2, of which 2 were waited for; matrix products, arithmetic and copies ran while one was open for 5% of the time, Pallas kernels for 0%

commit v1 on v0

v1 whole, which is shorter than its diff:
```python
import functools
import math

import jax
import jax.numpy as jnp
from jax import lax
from jax.experimental import pallas as pl
from jax.experimental.pallas import tpu as pltpu
from jax.sharding import PartitionSpec as P

F32, BF16 = jnp.float32, jnp.bfloat16
HIGHEST = lax.Precision.HIGHEST
CHUNKS = 4
VMEM_LIMIT = 32 * 2**20


def iota(shape, dim):
    return lax.broadcasted_iota(jnp.int32, shape, dim)


def params():
    return pltpu.CompilerParams(vmem_limit_bytes=VMEM_LIMIT)


def cost(flops, bytes_accessed):
    return pl.CostEstimate(flops=flops, bytes_accessed=bytes_accessed, transcendentals=0)


def column_block(width):
    for block in (896, 512, 256, 128):
        if width % block == 0:
            return block
    return width


def spread_kernel(rows, place_ref, coeff_ref, spread_ref, spread_t_ref):
    experts, bases = coeff_ref.shape
    mix = jnp.tanh(coeff_ref[...]).astype(BF16).astype(F32)
    place = place_ref[0]
    tall = experts * rows
    wide = bases * rows
    owner = jnp.bitwise_xor(iota((tall, bases), 0) // rows, place)
    picked = jnp.zeros((tall, bases), F32)
    for e in range(experts):
        picked = jnp.where(owner == e, mix[e : e + 1, :], picked)
    widen = (iota((bases, wide), 1) // rows == iota((bases, wide), 0)).astype(BF16)
    spread = jnp.dot(picked.astype(BF16), widen, preferred_element_type=F32)
    same = iota((tall, wide), 0) % rows == iota((tall, wide), 1) % rows
    spread = jnp.where(same, spread, 0.0)
    spread_ref[...] = spread.astype(BF16)
    spread_t_ref[...] = spread.T.astype(BF16)


def mix_kernel(spread_ref, bases_ref, *out_refs):
    mixed = jnp.dot(spread_ref[...], bases_ref[...], preferred_element_type=F32)
    rows = mixed.shape[0] // len(out_refs)
    for j, out_ref in enumerate(out_refs):
        out_ref[...] = mixed[j * rows : (j + 1) * rows].astype(BF16)


def fit_kernel(first, load_ref, load_t_ref, weights_ref, m0, m1, m2, m3, *refs):
    if first:
        near_ref, far_ref, grad_ref = refs
    else:
        before_ref, near_ref, far_ref, grad_ref = refs
    mixture = jnp.concatenate([m0[...], m1[...], m2[...], m3[...]], axis=0)
    product = jnp.dot(load_ref[...], mixture, preferred_element_type=F32)
    residual = (product - weights_ref[...].astype(F32)).astype(BF16)
    grad = lax.dot_general(
        residual, mixture, (((1,), (1,)), ((), ())), preferred_element_type=F32
    )
    partial = jnp.dot(load_t_ref[...], residual, preferred_element_type=F32)
    half = partial.shape[0] // 2
    near_ref[...] = partial[:half]
    far_ref[...] = partial[half:].astype(BF16)

    @pl.when(pl.program_id(0) == 0)
    def _():
        if first:
            grad_ref[...] = grad
        else:
            grad_ref[...] = before_ref[...] + grad

    @pl.when(pl.program_id(0) > 0)
    def _():
        grad_ref[...] += grad


def chip_sum_kernel(near_ref, got_ref, keep_ref, send_ref):
    total = near_ref[...] + got_ref[...].astype(F32)
    half = total.shape[0] // 2
    keep_ref[...] = total[:half]
    send_ref[...] = total[half:].astype(BF16)


def plane_sum_kernel(keep_ref, got_ref, *out_refs):
    total = keep_ref[...] + got_ref[...].astype(F32)
    rows = total.shape[0] // len(out_refs)
    for j, out_ref in enumerate(out_refs):
        out_ref[...] = total[j * rows : (j + 1) * rows].astype(BF16)


def inner_kernel(rows, experts, place_ref, bases_ref, *refs):
    *sum_refs, inner_ref, acc_ref = refs
    summed = jnp.concatenate([ref[...] for ref in sum_refs], axis=0)
    step = lax.dot_general(
        summed, bases_ref[...], (((1,), (1,)), ((), ())), preferred_element_type=F32
    )

    @pl.when(pl.program_id(0) == 0)
    def _():
        acc_ref[...] = step

    @pl.when(pl.program_id(0) > 0)
    def _():
        acc_ref[...] += step

    @pl.when(pl.program_id(0) == pl.num_programs(0) - 1)
    def _():
        tall, wide = acc_ref.shape
        bases = wide // rows
        same = iota((tall, wide), 0) % rows == iota((tall, wide), 1) % rows
        kept = jnp.where(same, acc_ref[...], 0.0)
        owner = jnp.bitwise_xor(iota((experts, tall), 1) // rows, place_ref[0])
        gather = (owner == iota((experts, tall), 0)).astype(F32)
        narrow = (iota((wide, bases), 0) // rows == iota((wide, bases), 1)).astype(F32)
        by_expert = jnp.dot(gather, kept, precision=HIGHEST, preferred_element_type=F32)
        inner_ref[...] = jnp.dot(
            by_expert, narrow, precision=HIGHEST, preferred_element_type=F32
        )


def basis_kernel(scale, aliased, spread_t_ref, *refs):
    if aliased:
        _, *sum_refs, out_ref = refs
    else:
        *sum_refs, out_ref = refs
    summed = jnp.concatenate([ref[...] for ref in sum_refs], axis=0)
    grad = jnp.dot(spread_t_ref[...], summed, preferred_element_type=F32)
    out_ref[...] = (grad * scale).astype(BF16)


def whole_spec(shape):
    return pl.BlockSpec(shape, lambda s: (0,) * len(shape))


def column_spec(rows, block, start=0):
    return pl.BlockSpec((rows, block), lambda s: (0, start + s))


def per_device(weights, loadings, bases, coeff):
    devices = lax.axis_size("expert")
    num_bases, rows, width = bases.shape
    experts = coeff.shape[0]
    group = devices // experts
    assert group == 4 and experts & (experts - 1) == 0
    ff = loadings.shape[0]
    rank = rows * devices
    tall, wide = experts * rows, num_bases * rows
    split = rows % 16 == 0
    chunks = CHUNKS if experts <= 8 else 1
    chunk = width // chunks
    block = column_block(chunk)
    steps = chunk // block
    me = lax.axis_index("expert")
    place = (me // group).astype(jnp.int32).reshape(1)
    smem = pl.BlockSpec(memory_space=pltpu.SMEM)
    vmem = pl.BlockSpec(memory_space=pltpu.VMEM)

    def send(x, flip):
        return lax.ppermute(x, "expert", [(i, i ^ flip) for i in range(devices)])

    def pieces_of(x):
        return [x[j * rows : (j + 1) * rows] for j in range(experts)]

    flat = bases.reshape(wide, width)
    spread, spread_t = pl.pallas_call(
        functools.partial(spread_kernel, rows),
        out_shape=(
            jax.ShapeDtypeStruct((tall, wide), BF16),
            jax.ShapeDtypeStruct((wide, tall), BF16),
        ),
        in_specs=[smem, vmem],
        out_specs=(vmem, vmem),
        compiler_params=params(),
        name="spread",
    )(place, coeff)

    local = jnp.arange(rank, dtype=jnp.int32)
    piece = local // rows
    flips = (piece % experts) * group + (piece // experts % 2) * 2 + piece // (2 * experts)
    absolute = (me ^ flips) * rows + local % rows
    order = (jnp.arange(rank, dtype=jnp.int32)[:, None] == absolute[None, :]).astype(BF16)
    load = jnp.dot(loadings, order, preferred_element_type=F32).astype(BF16)
    load_t = lax.dot_general(
        order, loadings, (((0,), (1,)), ((), ())), preferred_element_type=F32
    ).astype(BF16)

    def mix_chunk(j):
        count = experts if split else 1
        outs = pl.pallas_call(
            mix_kernel,
            grid=(steps,),
            out_shape=[jax.ShapeDtypeStruct((tall // count, chunk), BF16)] * count,
            in_specs=[whole_spec((tall, wide)), column_spec(wide, block, j * steps)],
            out_specs=[column_spec(tall // count, block)] * count,
            compiler_params=params(),
            cost_estimate=cost(2 * tall * wide * chunk * 4, 2 * wide * chunk),
            name="mix",
        )(spread, flat)
        return list(outs) if split else pieces_of(outs[0])

    def fit_chunk(j, parts, before):
        first = before is None
        quarter = rank // 4
        extra = [] if first else [before]
        return pl.pallas_call(
            functools.partial(fit_kernel, first),
            grid=(steps,),
            out_shape=(
                jax.ShapeDtypeStruct((rank // 2, chunk), F32),
                jax.ShapeDtypeStruct((rank // 2, chunk), BF16),
                jax.ShapeDtypeStruct((ff, rank), F32),
            ),
            in_specs=[
                whole_spec((ff, rank)),
                whole_spec((rank, ff)),
                column_spec(ff, block, j * steps),
                *[column_spec(quarter, block)] * 4,
                *[whole_spec((ff, rank))] * len(extra),
            ],
            out_specs=(
                column_spec(rank // 2, block),
                column_spec(rank // 2, block),
                whole_spec((ff, rank)),
            ),
            compiler_params=params(),
            cost_estimate=cost(6 * ff * rank * chunk, 2 * ff * chunk),
            name="fit",
        )(load, load_t, weights, *parts, *extra)

    def chip_sum(near, got):
        half = rank // 4
        return pl.pallas_call(
            chip_sum_kernel,
            grid=(steps,),
            out_shape=(
                jax.ShapeDtypeStruct((half, chunk), F32),
                jax.ShapeDtypeStruct((half, chunk), BF16),
            ),
            in_specs=[column_spec(2 * half, block)] * 2,
            out_specs=(column_spec(half, block),) * 2,
            compiler_params=params(),
            cost_estimate=cost(2 * half * chunk, 16 * half * chunk),
            name="chip_sum",
        )(near, got)

    def plane_sum(keep, got):
        count = experts if split else 1
        outs = pl.pallas_call(
            plane_sum_kernel,
            grid=(steps,),
            out_shape=[jax.ShapeDtypeStruct((tall // count, chunk), BF16)] * count,
            in_specs=[column_spec(tall, block)] * 2,
            out_specs=[column_spec(tall // count, block)] * count,
            compiler_params=params(),
            cost_estimate=cost(tall * chunk, 8 * tall * chunk),
            name="plane_sum",
        )(keep, got)
        return list(outs) if split else pieces_of(outs[0])

    def sums_of(sums):
        return sums if split else [jnp.concatenate(sums, axis=0)]

    def inner_chunk(j, sums):
        sums = sums_of(sums)
        return pl.pallas_call(
            functools.partial(inner_kernel, rows, experts),
            grid=(steps,),
            out_shape=jax.ShapeDtypeStruct((experts, num_bases), F32),
            in_specs=[
                smem,
                column_spec(wide, block, j * steps),
                *[column_spec(tall // len(sums), block)] * len(sums),
            ],
            out_specs=whole_spec((experts, num_bases)),
            scratch_shapes=[pltpu.VMEM((tall, wide), F32)],
            compiler_params=params(),
            cost_estimate=cost(2 * tall * wide * chunk * 4, 2 * wide * chunk),
            name="inner",
        )(place, flat, *sums)

    def basis_chunk(j, sums, before):
        sums = sums_of(sums)
        aliased = before is not None
        extra = [before] if aliased else []
        return pl.pallas_call(
            functools.partial(basis_kernel, 1.0 / math.sqrt(experts), aliased),
            grid=(steps,),
            out_shape=jax.ShapeDtypeStruct((wide, width), BF16),
            in_specs=[
                whole_spec((wide, tall)),
                *[pl.BlockSpec(memory_space=pl.ANY)] * len(extra),
                *[column_spec(tall // len(sums), block)] * len(sums),
            ],
            out_specs=column_spec(wide, block, j * steps),
            input_output_aliases={1: 0} if aliased else {},
            compiler_params=params(),
            cost_estimate=cost(2 * tall * wide * chunk * 4, 2 * wide * chunk),
            name="basis",
        )(spread_t, *extra, *sums)

    grad_local, grad_flat, inners = None, None, []
    gathered = []
    for j in range(chunks):
        mixed = mix_chunk(j)
        got = [mixed[0]] + [send(mixed[k], k * group) for k in range(1, experts)]
        own = jnp.concatenate(got, axis=0)
        row = send(own, 2)
        gathered.append((own, row, send(own, 1), send(row, 1)))
    returned = []
    for j in range(chunks):
        near, far, grad_local = fit_chunk(j, gathered[j], grad_local)
        keep, away = chip_sum(near, send(far, 1))
        sums = plane_sum(keep, send(away, 2))
        returned.append([sums[0]] + [send(sums[k], k * group) for k in range(1, experts)])
    for j in range(chunks):
        inners.append(inner_chunk(j, returned[j]))
        grad_flat = basis_chunk(j, returned[j], grad_flat)

    grad_a = jnp.dot(
        grad_local, order.astype(F32).T, precision=HIGHEST, preferred_element_type=F32
    ) / math.sqrt(width)

    total = sum(inners[1:], inners[0])
    flip = 1
    while flip < devices:
        if flip * 2 < devices:
            a, b, c = (send(total, flip * k) for k in (1, 2, 3))
            total = (total + a) + (b + c)
            flip *= 4
        else:
            total = total + send(total, flip)
            flip *= 2
    slope = 1.0 - jnp.tanh(coeff) ** 2
    grad_c = slope * total / math.sqrt(rank * width)
    return (grad_a, grad_flat.reshape(num_bases, rows, width), grad_c)


def solution(mesh):
    in_specs = (
        P(("layer", "expert"), None),
        P(("layer", "expert"), None),
        P("layer", "expert", None),
        P("layer", None),
    )
    out_specs = (P(("layer", "expert"), None), P("layer", "expert", None), P("layer", None))
    return jax.shard_map(
        per_device, mesh=mesh, in_specs=in_specs, out_specs=out_specs, check_vma=False
    )
```

time: 388 us -> 134 us (0.35)
  waiting for transfers between devices: 184 us -> 27.4 us
  matrix products: 70 us -> 1.48 us
  blocking collectives: 60.3 us -> 0 us
  Pallas kernels: 0 us -> 38.2 us
  local copies, waits for them, and re-layouts: 43.6 us -> 9.22 us
  starting transfers between devices: 25 us -> 55.7 us
    all_to_all x2 -> x0, waiting for transfers between devices: 184 us -> none  [the longest x1 125 us: per_device(): lax.all_to_all(partial_value.reshape(devices, rows_dev, width), 'expert',...]
    dot_general x6 -> x2, matrix products: 70 us -> 1.48 us  [the longest x1 1.21 us: per_device(): jnp.dot(grad_local, order.astype(F32).T, precision=HIGHEST, preferred_ele...]
    psum x1 -> x0, blocking collectives: 60.3 us -> none  [per_device(): total_inner = lax.psum(basis_inner, 'expert')]
    ppermute x0 -> x50, starting transfers between devices: none -> 55.7 us  [send(): return lax.ppermute(x, 'expert', [(i, i ^ flip) for i in range(devices)])]
    pallas_call x0 -> x25, Pallas kernels: none -> 38.2 us  [the longest x4 11.4 us: fit_chunk(): pl.pallas_call(functools.partial(fit_kernel, first), grid=(steps,), out_s...]
    unnamed x12 -> x30, local copies, waits for them, and re-layouts: 41.3 us -> 9.07 us
    ppermute x0 -> x50, waiting for transfers between devices: none -> 27.4 us  [send(): return lax.ppermute(x, 'expert', [(i, i ^ flip) for i in range(devices)])]
    all_to_all x2 -> x0, starting transfers between devices: 25 us -> none  [the longest x1 17.6 us: per_device(): lax.all_to_all(partial_value.reshape(devices, rows_dev, width), 'expert',...]
  transfers between devices with their start and end apart: 2 -> 50, of which waited for: 2 -> 14; matrix products, arithmetic and copies ran while one was open for 5% -> 1% of each run, Pallas kernels for 0% -> 24%
where the time goes in v1:
time: 134 us
  starting transfers between devices  55.7 us (42%)
  Pallas kernels  38.2 us (29%)
  waiting for transfers between devices  27.4 us (20%)
  local copies, waits for them, and re-layouts  9.22 us (7%)
  matrix products  1.48 us (1%)
    ppermute x50, starting transfers between devices, send(): return lax.ppermute(x, 'expert', [(i, i ^ flip) for i in range(devices)])  55.7 us
    ppermute x50, waiting for transfers between devices, send(): return lax.ppermute(x, 'expert', [(i, i ^ flip) for i in range(devices)])  27.4 us
    pallas_call x4, Pallas kernels, fit_chunk(): pl.pallas_call(functools.partial(fit_kernel, first), grid=(steps,), out_s...  11.4 us
    pallas_call x4, Pallas kernels, basis_chunk(): pl.pallas_call(functools.partial(basis_kernel, 1.0 / math.sqrt(experts),...  10.1 us
    pallas_call x4, Pallas kernels, inner_chunk(): pl.pallas_call(functools.partial(inner_kernel, rows, experts), grid=(step...  9.38 us
    unnamed x30, local copies, waits for them, and re-layouts  9.07 us
    pallas_call x4, Pallas kernels, mix_chunk(): pl.pallas_call(mix_kernel, grid=(steps,), out_shape=[jax.ShapeDtypeStruct...  5.13 us
  transfers between devices with their start and end apart: 50, of which 14 were waited for; matrix products, arithmetic and copies ran while one was open for 1% of the time, Pallas kernels for 24%

profile of v1, /device:TPU:0, one launch (start us, length us, event | category | flops | bytes accessed | tf_op | source)
XLA Modules:
  0.0 133.8 jit_solution(4917917591631675785)
XLA Ops:
  0.7 0.7 copy-done.3
  1.7 5.2 %copy-done.1 = bf16[64,16,7168]{2,1,0:T(8,128)(2,1)S(1)} copy-done((bf16[64,16,7168]{2,1,0:T(8,128)(2,1)S(1)}, bf16[64,16,7168]{2,1,0:T(8,128)(2,1)}, u32[]{:S(2)}) %copy-start.1) | copy-done | bytes 14680088
  6.8 1.3 mix.7
  8.1 3.1 %collective-permute-start.18 = (bf16[16,1792]{1,0:T(8,128)(2,1)S(1)}, bf16[16,1792]{1,0:T(8,128)(2,1)S(1)}, u32[]{:S(2)}, u32[]{:S(2)}) collective-permute-start(bf16[16,1792]{1,0:T(8,128)(2,1)S(1)} %get-tuple-element.71), channel_id=1, source_target_pairs={{0,4},{1,5},{2,6},{3,7},{4,0},{5,1},{6,2},{7,3},{8,12},{9,13},{10,... | collective-permute-start | bytes 172040 | tf_op jit(solution)/shard_map/ppermute | solution.py:171
  11.2 2.6 %collective-permute-start.19 = (bf16[16,1792]{1,0:T(8,128)(2,1)S(1)}, bf16[16,1792]{1,0:T(8,128)(2,1)S(1)}, u32[]{:S(2)}, u32[]{:S(2)}) collective-permute-start(bf16[16,1792]{1,0:T(8,128)(2,1)S(1)} %get-tuple-element.72), channel_id=1, source_target_pairs={{0,8},{1,9},{2,10},{3,11},{4,12},{5,13},{6,14},{7,15},{8,0},{9,1},... | collective-permute-start | bytes 172040 | tf_op jit(solution)/shard_map/ppermute | solution.py:171
  13.8 1.3 mix.6
  15.1 1.0 collective-permute-start.12
  16.0 3.5 %collective-permute-start.13 = (bf16[16,1792]{1,0:T(8,128)(2,1)S(1)}, bf16[16,1792]{1,0:T(8,128)(2,1)S(1)}, u32[]{:S(2)}, u32[]{:S(2)}) collective-permute-start(bf16[16,1792]{1,0:T(8,128)(2,1)S(1)} %get-tuple-element.68), channel_id=1, source_target_pairs={{0,8},{1,9},{2,10},{3,11},{4,12},{5,13},{6,14},{7,15},{8,0},{9,1},... | collective-permute-start | bytes 172040 | tf_op jit(solution)/shard_map/ppermute | solution.py:171
  19.5 1.3 mix.5
  20.8 1.3 mix.4
  22.3 0.6 collective-permute-start.6
  22.9 3.9 %collective-permute-start.7 = (bf16[16,1792]{1,0:T(8,128)(2,1)S(1)}, bf16[16,1792]{1,0:T(8,128)(2,1)S(1)}, u32[]{:S(2)}, u32[]{:S(2)}) collective-permute-start(bf16[16,1792]{1,0:T(8,128)(2,1)S(1)} %get-tuple-element.64), channel_id=1, source_target_pairs={{0,8},{1,9},{2,10},{3,11},{4,12},{5,13},{6,14},{7,15},{8,0},{9,1},... | collective-permute-start | bytes 172040 | tf_op jit(solution)/shard_map/ppermute | solution.py:171
  26.9 0.6 collective-permute-start
  27.6 0.8 collective-permute-done.14
  28.4 3.0 %collective-permute-start.1 = (bf16[16,1792]{1,0:T(8,128)(2,1)S(1)}, bf16[16,1792]{1,0:T(8,128)(2,1)S(1)}, u32[]{:S(2)}, u32[]{:S(2)}) collective-permute-start(bf16[16,1792]{1,0:T(8,128)(2,1)S(1)} %get-tuple-element.60), channel_id=1, source_target_pairs={{0,8},{1,9},{2,10},{3,11},{4,12},{5,13},{6,14},{7,15},{8,0},{9,1},... | collective-permute-start | bytes 172040 | tf_op jit(solution)/shard_map/ppermute | solution.py:171
  31.5 0.5 collective-permute-start.2
  32.1 1.2 collective-permute-done.8
  33.3 1.5 %collective-permute-start.15 = (bf16[64,1792]{1,0:T(8,128)(2,1)S(1)}, bf16[64,1792]{1,0:T(8,128)(2,1)S(1)}, u32[]{:S(2)}, u32[]{:S(2)}) collective-permute-start(bf16[64,1792]{1,0:T(8,128)(2,1)S(1)} %constant_dynamic-update-slice_fusion.8.m0), channel_id=1, source_target_pairs={{0,2},{1,3},{2,0},{3,1},{4,6},{5,7},{6,4},{7,5},{8,10},{9,11},{10,... | collective-permute-start | bytes 688136 | tf_op jit(solution)/shard_map/ppermute | solution.py:171
  34.8 0.6 collective-permute-start.9
  35.6 1.5 %collective-permute-start.21 = (bf16[64,1792]{1,0:T(8,128)(2,1)S(1)}, bf16[64,1792]{1,0:T(8,128)(2,1)S(1)}, u32[]{:S(2)}, u32[]{:S(2)}) collective-permute-start(bf16[64,1792]{1,0:T(8,128)(2,1)S(1)} %constant_dynamic-update-slice_fusion.12.m0), channel_id=1, source_target_pairs={{0,2},{1,3},{2,0},{3,1},{4,6},{5,7},{6,4},{7,5},{8,10},{9,11},{10,... | collective-permute-start | bytes 688136 | tf_op jit(solution)/shard_map/ppermute | solution.py:171
  37.5 9.2 %collective-permute-done.9.m1 = bf16[64,1792]{1,0:T(8,128)(2,1)S(1)} collective-permute-done((bf16[64,1792]{1,0:T(8,128)(2,1)S(1)}, bf16[64,1792]{1,0:T(8,128)(2,1)S(1)}, u32[]{:S(2)}, u32[]{:S(2)}) %collective-permute-start.9) | collective-permute-done | bytes 229408 | tf_op jit(solution)/shard_map/ppermute | solution.py:171
  46.7 1.5 %collective-permute-start.3 = (bf16[64,1792]{1,0:T(8,128)(2,1)S(1)}, bf16[64,1792]{1,0:T(8,128)(2,1)S(1)}, u32[]{:S(2)}, u32[]{:S(2)}) collective-permute-start(bf16[64,1792]{1,0:T(8,128)(2,1)S(1)} %constant_dynamic-update-slice_fusion.m0), channel_id=1, source_target_pairs={{0,2},{1,3},{2,0},{3,1},{4,6},{5,7},{6,4},{7,5},{8,10},{9,11},{10,... | collective-permute-start | bytes 688136 | tf_op jit(solution)/shard_map/ppermute | solution.py:171
  48.3 3.4 %collective-permute-done.21.m1 = bf16[64,1792]{1,0:T(8,128)(2,1)S(1)} collective-permute-done((bf16[64,1792]{1,0:T(8,128)(2,1)S(1)}, bf16[64,1792]{1,0:T(8,128)(2,1)S(1)}, u32[]{:S(2)}, u32[]{:S(2)}) %collective-permute-start.21) | collective-permute-done | bytes 229408 | tf_op jit(solution)/shard_map/ppermute | solution.py:171
  52.1 0.6 collective-permute-start.10
  52.7 0.6 collective-permute-done.23.m3
  53.4 3.1 %copy-done.2 = bf16[512,7168]{1,0:T(8,128)(2,1)S(1)} copy-done((bf16[512,7168]{1,0:T(8,128)(2,1)S(1)}, bf16[512,7168]{1,0:T(8,128)(2,1)}, u32[]{:S(2)}) %copy-start.2) | copy-done | bytes 7340056
  56.5 3.3 %fit.4 = (f32[128,1792]{1,0:T(8,128)S(1)}, bf16[128,1792]{1,0:T(8,128)(2,1)S(1)}, f32[512,256]{1,0:T(8,128)S(1)}) custom-call(bf16[512,256]{1,0:T(8,128)(2,1)S(1)} %copy.13.load_ref, bf16[256,512]{1,0:T(8,128)(2,1)S(1)} %convolution_convert_fusion.load_t_ref, bf16[512,7168]{1,0:T(8,128)(2,1)S(1)} %copy-done.2, ...), custom_call_target="tpu_custom_call" | custom-call | flops 1409286144 | bytes 1835008 | tf_op jit(solution)/shard_map/fit/pallas_call | solution.py:217
  59.8 0.4 collective-permute-start.4
  60.3 3.1 %fit.5 = (f32[128,1792]{1,0:T(8,128)S(1)}, bf16[128,1792]{1,0:T(8,128)(2,1)}, f32[512,256]{1,0:T(8,128)S(1)}) custom-call(bf16[512,256]{1,0:T(8,128)(2,1)S(1)} %copy.13.load_ref, bf16[256,512]{1,0:T(8,128)(2,1)S(1)} %convolution_convert_fusion.load_t_ref, bf16[512,7168]{1,0:T(8,128)(2,1)S(1)} %copy-done.2, ...), custom_call_target="tpu_custom_call" | custom-call | flops 1409286144 | bytes 1835008 | tf_op jit(solution)/shard_map/fit/pallas_call | solution.py:217
  63.5 2.5 %fit.6 = (f32[128,1792]{1,0:T(8,128)S(1)}, bf16[128,1792]{1,0:T(8,128)(2,1)S(1)}, f32[512,256]{1,0:T(8,128)S(1)}) custom-call(bf16[512,256]{1,0:T(8,128)(2,1)S(1)} %copy.13.load_ref, bf16[256,512]{1,0:T(8,128)(2,1)S(1)} %convolution_convert_fusion.load_t_ref, bf16[512,7168]{1,0:T(8,128)(2,1)S(1)} %copy-done.2, ...), custom_call_target="tpu_custom_call" | custom-call | flops 1409286144 | bytes 1835008 | tf_op jit(solution)/shard_map/fit/pallas_call | solution.py:217
  66.1 2.5 %fit.7 = (f32[128,1792]{1,0:T(8,128)S(1)}, bf16[128,1792]{1,0:T(8,128)(2,1)S(1)}, f32[512,256]{1,0:T(8,128)S(1)}) custom-call(bf16[512,256]{1,0:T(8,128)(2,1)S(1)} %copy.13.load_ref, bf16[256,512]{1,0:T(8,128)(2,1)S(1)} %convolution_convert_fusion.load_t_ref, bf16[512,7168]{1,0:T(8,128)(2,1)S(1)} %copy-done.2, ...), custom_call_target="tpu_custom_call" | custom-call | flops 1409286144 | bytes 1835008 | tf_op jit(solution)/shard_map/fit/pallas_call | solution.py:217
  68.6 0.4 collective-permute-start.39
  69.7 0.8 collective-permute-done.39.got_ref
  70.8 1.6 %collective-permute-start.40 = (bf16[64,1792]{1,0:T(8,128)(2,1)S(1)}, bf16[64,1792]{1,0:T(8,128)(2,1)S(1)}, u32[]{:S(2)}, u32[]{:S(2)}) collective-permute-start(bf16[64,1792]{1,0:T(8,128)(2,1)S(1)} %get-tuple-element.106), channel_id=1, source_target_pairs={{0,2},{1,3},{2,0},{3,1},{4,6},{5,7},{6,4},{7,5},{8,10},{9,11},{10,... | collective-permute-start | bytes 688136 | tf_op jit(solution)/shard_map/ppermute | solution.py:171
  72.7 1.0 collective-permute-start.35
  74.0 1.1 collective-permute-start.30
  75.4 1.0 collective-permute-start.25
  76.4 2.8 %collective-permute-done.40.got_ref = bf16[64,1792]{1,0:T(8,128)(2,1)S(1)} collective-permute-done((bf16[64,1792]{1,0:T(8,128)(2,1)S(1)}, bf16[64,1792]{1,0:T(8,128)(2,1)S(1)}, u32[]{:S(2)}, u32[]{:S(2)}) %collective-permute-start.40) | collective-permute-done | bytes 229408 | tf_op jit(solution)/shard_map/ppermute | solution.py:171
  79.5 1.0 collective-permute-start.41
  80.5 1.7 %collective-permute-start.42 = (bf16[16,1792]{1,0:T(8,128)(2,1)S(1)}, bf16[16,1792]{1,0:T(8,128)(2,1)S(1)}, u32[]{:S(2)}, u32[]{:S(2)}) collective-permute-start(bf16[16,1792]{1,0:T(8,128)(2,1)S(1)} %get-tuple-element.109), channel_id=1, source_target_pairs={{0,8},{1,9},{2,10},{3,11},{4,12},{5,13},{6,14},{7,15},{8,0},{9,1},... | collective-permute-start | bytes 172040 | tf_op jit(solution)/shard_map/ppermute | solution.py:171
  82.2 2.0 %collective-permute-done.35.got_ref = bf16[64,1792]{1,0:T(8,128)(2,1)S(1)} collective-permute-done((bf16[64,1792]{1,0:T(8,128)(2,1)S(1)}, bf16[64,1792]{1,0:T(8,128)(2,1)S(1)}, u32[]{:S(2)}, u32[]{:S(2)}) %collective-permute-start.35) | collective-permute-done | bytes 229408 | tf_op jit(solution)/shard_map/ppermute | solution.py:171
  84.2 2.1 %collective-permute-start.43 = (bf16[16,1792]{1,0:T(8,128)(2,1)S(1)}, bf16[16,1792]{1,0:T(8,128)(2,1)S(1)}, u32[]{:S(2)}, u32[]{:S(2)}) collective-permute-start(bf16[16,1792]{1,0:T(8,128)(2,1)S(1)} %get-tuple-element.110), channel_id=1, source_target_pairs={{0,12},{1,13},{2,14},{3,15},{4,8},{5,9},{6,10},{7,11},{8,4},{9,5},... | collective-permute-start | bytes 172040 | tf_op jit(solution)/shard_map/ppermute | solution.py:171
  86.3 1.2 convolution_multiply_fusion
  87.7 1.4 %collective-permute-done.30.got_ref = bf16[64,1792]{1,0:T(8,128)(2,1)S(1)} collective-permute-done((bf16[64,1792]{1,0:T(8,128)(2,1)S(1)}, bf16[64,1792]{1,0:T(8,128)(2,1)S(1)}, u32[]{:S(2)}, u32[]{:S(2)}) %collective-permute-start.30) | collective-permute-done | bytes 229408 | tf_op jit(solution)/shard_map/ppermute | solution.py:171
  89.1 0.9 collective-permute-start.36
  90.2 3.2 %collective-permute-done.25.got_ref = bf16[64,1792]{1,0:T(8,128)(2,1)S(1)} collective-permute-done((bf16[64,1792]{1,0:T(8,128)(2,1)S(1)}, bf16[64,1792]{1,0:T(8,128)(2,1)S(1)}, u32[]{:S(2)}, u32[]{:S(2)}) %collective-permute-start.25) | collective-permute-done | bytes 229408 | tf_op jit(solution)/shard_map/ppermute | solution.py:171
  94.1 2.9 %collective-permute-start.38 = (bf16[16,1792]{1,0:T(8,128)(2,1)S(1)}, bf16[16,1792]{1,0:T(8,128)(2,1)S(1)}, u32[]{:S(2)}, u32[]{:S(2)}) collective-permute-start(bf16[16,1792]{1,0:T(8,128)(2,1)S(1)} %get-tuple-element.102), channel_id=1, source_target_pairs={{0,12},{1,13},{2,14},{3,15},{4,8},{5,9},{6,10},{7,11},{8,4},{9,5},... | collective-permute-start | bytes 172040 | tf_op jit(solution)/shard_map/ppermute | solution.py:171
  97.2 1.3 collective-permute-start.32
  98.6 2.5 %inner.7 = f32[4,64]{1,0:T(4,128)S(1)} custom-call(s32[1]{0:T(128)} %bitcast.1.place_ref, bf16[1024,7168]{1,0:T(8,128)(2,1)S(1)} %bitcast.12, bf16[16,1792]{1,0:T(8,128)(2,1)S(1)} %get-tuple-element.107.refs_1_.refs_0_, bf16[16,1792]{1,0:T(8,128)(2,1)S(1)} %collective-permute-done.41.refs_2_.refs_1_, ...), custom_call_target="tpu_custom_call" | custom-call | flops 939524096 | bytes 3670016 | tf_op jit(solution)/shard_map/inner/pallas_call | solution.py:277
  101.1 2.9 %collective-permute-start.33 = (bf16[16,1792]{1,0:T(8,128)(2,1)S(1)}, bf16[16,1792]{1,0:T(8,128)(2,1)S(1)}, u32[]{:S(2)}, u32[]{:S(2)}) collective-permute-start(bf16[16,1792]{1,0:T(8,128)(2,1)S(1)} %get-tuple-element.94), channel_id=1, source_target_pairs={{0,12},{1,13},{2,14},{3,15},{4,8},{5,9},{6,10},{7,11},{8,4},{9,5},... | collective-permute-start | bytes 172040 | tf_op jit(solution)/shard_map/ppermute | solution.py:171
  104.0 1.5 %collective-permute-start.27 = (bf16[16,1792]{1,0:T(8,128)(2,1)S(1)}, bf16[16,1792]{1,0:T(8,128)(2,1)S(1)}, u32[]{:S(2)}, u32[]{:S(2)}) collective-permute-start(bf16[16,1792]{1,0:T(8,128)(2,1)S(1)} %get-tuple-element.85), channel_id=1, source_target_pairs={{0,8},{1,9},{2,10},{3,11},{4,12},{5,13},{6,14},{7,15},{8,0},{9,1},... | collective-permute-start | bytes 172040 | tf_op jit(solution)/shard_map/ppermute | solution.py:171
  105.6 2.3 %inner.6 = f32[4,64]{1,0:T(4,128)S(1)} custom-call(s32[1]{0:T(128)} %bitcast.1.place_ref, bf16[1024,7168]{1,0:T(8,128)(2,1)S(1)} %bitcast.13, bf16[16,1792]{1,0:T(8,128)(2,1)S(1)} %get-tuple-element.99.refs_1_.refs_0_, bf16[16,1792]{1,0:T(8,128)(2,1)S(1)} %collective-permute-done.36.refs_2_.refs_1_, ...), custom_call_target="tpu_custom_call" | custom-call | flops 939524096 | bytes 3670016 | tf_op jit(solution)/shard_map/inner/pallas_call | solution.py:277
  107.9 2.9 %collective-permute-start.28 = (bf16[16,1792]{1,0:T(8,128)(2,1)S(1)}, bf16[16,1792]{1,0:T(8,128)(2,1)S(1)}, u32[]{:S(2)}, u32[]{:S(2)}) collective-permute-start(bf16[16,1792]{1,0:T(8,128)(2,1)S(1)} %get-tuple-element.86), channel_id=1, source_target_pairs={{0,12},{1,13},{2,14},{3,15},{4,8},{5,9},{6,10},{7,11},{8,4},{9,5},... | collective-permute-start | bytes 172040 | tf_op jit(solution)/shard_map/ppermute | solution.py:171
  110.8 2.3 %inner.5 = f32[4,64]{1,0:T(4,128)S(1)} custom-call(s32[1]{0:T(128)} %bitcast.1.place_ref, bf16[1024,7168]{1,0:T(8,128)(2,1)S(1)} %bitcast.14, bf16[16,1792]{1,0:T(8,128)(2,1)S(1)} %get-tuple-element.91.refs_1_.refs_0_, bf16[16,1792]{1,0:T(8,128)(2,1)S(1)} %collective-permute-done.31.refs_2_.refs_1_, ...), custom_call_target="tpu_custom_call" | custom-call | flops 939524096 | bytes 3670016 | tf_op jit(solution)/shard_map/inner/pallas_call | solution.py:277
  113.1 0.8 collective-permute-done.28.refs_3_
  113.9 2.3 %inner.4 = f32[4,64]{1,0:T(4,128)S(1)} custom-call(s32[1]{0:T(128)} %bitcast.1.place_ref, bf16[1024,7168]{1,0:T(8,128)(2,1)S(1)} %bitcast.15, bf16[16,1792]{1,0:T(8,128)(2,1)S(1)} %get-tuple-element.83.refs_0_, bf16[16,1792]{1,0:T(8,128)(2,1)S(1)} %collective-permute-done.26.refs_1_, bf16[16,1792]{1,0:T(8,128)(2,1)S(1)} %collective-permute-done.27.refs_2_, ...), custom_call_target="tpu_custom_call" | custom-call | flops 939524096 | bytes 3670016 | tf_op jit(solution)/shard_map/inner/pallas_call | solution.py:277
  116.3 1.8 %collective-permute-start.45 = (f32[4,64]{1,0:T(4,128)S(1)}, f32[4,64]{1,0:T(4,128)S(1)}, u32[]{:S(2)}, u32[]{:S(2)}) collective-permute-start(f32[4,64]{1,0:T(4,128)S(1)} %add_add_fusion.1), channel_id=1, source_target_pairs={{0,2},{1,3},{2,0},{3,1},{4,6},{5,7},{6,4},{7,5},{8,10},{9,11},{10,... | collective-permute-start | bytes 3080 | tf_op jit(solution)/shard_map/ppermute | solution.py:171
  118.2 2.5 %basis.4.refs_0_ = bf16[1024,7168]{1,0:T(8,128)(2,1)} custom-call(bf16[1024,64]{1,0:T(8,128)(2,1)S(1)} %get-tuple-element.78.spread_t_ref, bf16[16,1792]{1,0:T(8,128)(2,1)S(1)} %get-tuple-element.83.refs_0_, bf16[16,1792]{1,0:T(8,128)(2,1)S(1)} %collective-permute-done.26.refs_1_, bf16[16,1792]{1,0:T(8,128)(2,1)S(1)} %collective-permute-done.27.refs_2_, ...), custom_call_target="tpu_custom_call" | custom-call | flops 939524096 | bytes 3670016 | tf_op jit(solution)/shard_map/basis/pallas_call | solution.py:297
  120.7 2.5 %basis.5.refs_0_ = bf16[1024,7168]{1,0:T(8,128)(2,1)} custom-call(bf16[1024,64]{1,0:T(8,128)(2,1)S(1)} %get-tuple-element.78.spread_t_ref, bf16[1024,7168]{1,0:T(8,128)(2,1)} %basis.4.refs_0_, bf16[16,1792]{1,0:T(8,128)(2,1)S(1)} %get-tuple-element.91.refs_1_.refs_0_, ...), custom_call_target="tpu_custom_call", output_to_operand_aliasing={{}: (1, {})} | custom-call | flops 939524096 | bytes 3670016 | tf_op jit(solution)/shard_map/basis/pallas_call | solution.py:297
  123.2 2.5 %basis.6.refs_0_ = bf16[1024,7168]{1,0:T(8,128)(2,1)} custom-call(bf16[1024,64]{1,0:T(8,128)(2,1)S(1)} %get-tuple-element.78.spread_t_ref, bf16[1024,7168]{1,0:T(8,128)(2,1)} %basis.5.refs_0_, bf16[16,1792]{1,0:T(8,128)(2,1)S(1)} %get-tuple-element.99.refs_1_.refs_0_, ...), custom_call_target="tpu_custom_call", output_to_operand_aliasing={{}: (1, {})} | custom-call | flops 939524096 | bytes 3670016 | tf_op jit(solution)/shard_map/basis/pallas_call | solution.py:297
  125.8 2.9 %collective-permute-start.49 = (f32[4,64]{1,0:T(4,128)S(1)}, f32[4,64]{1,0:T(4,128)S(1)}, u32[]{:S(2)}, u32[]{:S(2)}) collective-permute-start(f32[4,64]{1,0:T(4,128)S(1)} %add_add_fusion), channel_id=1, source_target_pairs={{0,12},{1,13},{2,14},{3,15},{4,8},{5,9},{6,10},{7,11},{8,4},{9,5},... | collective-permute-start | bytes 3080 | tf_op jit(solution)/shard_map/ppermute | solution.py:171
  128.7 1.5 %collective-permute-start.47 = (f32[4,64]{1,0:T(4,128)S(1)}, f32[4,64]{1,0:T(4,128)S(1)}, u32[]{:S(2)}, u32[]{:S(2)}) collective-permute-start(f32[4,64]{1,0:T(4,128)S(1)} %add_add_fusion), channel_id=1, source_target_pairs={{0,4},{1,5},{2,6},{3,7},{4,0},{5,1},{6,2},{7,3},{8,12},{9,13},{10,... | collective-permute-start | bytes 3080 | tf_op jit(solution)/shard_map/ppermute | solution.py:171
  130.2 2.5 %basis.7 = bf16[1024,7168]{1,0:T(8,128)(2,1)} custom-call(bf16[1024,64]{1,0:T(8,128)(2,1)S(1)} %get-tuple-element.78.spread_t_ref, bf16[1024,7168]{1,0:T(8,128)(2,1)} %basis.6.refs_0_, bf16[16,1792]{1,0:T(8,128)(2,1)S(1)} %get-tuple-element.107.refs_1_.refs_0_, ...), custom_call_target="tpu_custom_call", output_to_operand_aliasing={{}: (1, {})} | custom-call | flops 939524096 | bytes 3670016 | tf_op jit(solution)/shard_map/basis/pallas_call | solution.py:297
  133.2 0.6 multiply_multiply_fusion
  (103 shorter events, 5.7 us)
Async XLA Ops:
  0.6 51.0 %copy-start = (bf16[512,256]{1,0:T(8,128)(2,1)S(1)}, bf16[512,256]{1,0:T(8,128)(2,1)}, u32[]{:S(2)}) copy-start(bf16[512,256]{1,0:T(8,128)(2,1)} %param.5) | copy-start | bytes 786436
  0.7 0.7 copy-start.3
  1.7 5.2 %copy-start.1 = (bf16[64,16,7168]{2,1,0:T(8,128)(2,1)S(1)}, bf16[64,16,7168]{2,1,0:T(8,128)(2,1)}, u32[]{:S(2)}) copy-start(bf16[64,16,7168]{2,1,0:T(8,128)(2,1)} %param.6) | copy-start | bytes 44040196
  8.1 14.1 %collective-permute-start.18 = (bf16[16,1792]{1,0:T(8,128)(2,1)S(1)}, bf16[16,1792]{1,0:T(8,128)(2,1)S(1)}, u32[]{:S(2)}, u32[]{:S(2)}) collective-permute-start(bf16[16,1792]{1,0:T(8,128)(2,1)S(1)} %get-tuple-element.71), channel_id=1, source_target_pairs={{0,4},{1,5},{2,6},{3,7},{4,0},{5,1},{6,2},{7,3},{8,12},{9,13},{10,... | collective-permute-start | bytes 172040 | tf_op jit(solution)/shard_map/ppermute | solution.py:171
  11.2 11.1 %collective-permute-start.19 = (bf16[16,1792]{1,0:T(8,128)(2,1)S(1)}, bf16[16,1792]{1,0:T(8,128)(2,1)S(1)}, u32[]{:S(2)}, u32[]{:S(2)}) collective-permute-start(bf16[16,1792]{1,0:T(8,128)(2,1)S(1)} %get-tuple-element.72), channel_id=1, source_target_pairs={{0,8},{1,9},{2,10},{3,11},{4,12},{5,13},{6,14},{7,15},{8,0},{9,1},... | collective-permute-start | bytes 172040 | tf_op jit(solution)/shard_map/ppermute | solution.py:171
  13.8 9.1 %collective-permute-start.20 = (bf16[16,1792]{1,0:T(8,128)(2,1)S(1)}, bf16[16,1792]{1,0:T(8,128)(2,1)S(1)}, u32[]{:S(2)}, u32[]{:S(2)}) collective-permute-start(bf16[16,1792]{1,0:T(8,128)(2,1)S(1)} %get-tuple-element.73), channel_id=1, source_target_pairs={{0,12},{1,13},{2,14},{3,15},{4,8},{5,9},{6,10},{7,11},{8,4},{9,5},... | collective-permute-start | bytes 172040 | tf_op jit(solution)/shard_map/ppermute | solution.py:171
  15.1 11.7 %collective-permute-start.12 = (bf16[16,1792]{1,0:T(8,128)(2,1)S(1)}, bf16[16,1792]{1,0:T(8,128)(2,1)S(1)}, u32[]{:S(2)}, u32[]{:S(2)}) collective-permute-start(bf16[16,1792]{1,0:T(8,128)(2,1)S(1)} %get-tuple-element.67), channel_id=1, source_target_pairs={{0,4},{1,5},{2,6},{3,7},{4,0},{5,1},{6,2},{7,3},{8,12},{9,13},{10,... | collective-permute-start | bytes 172040 | tf_op jit(solution)/shard_map/ppermute | solution.py:171
  16.0 10.9 %collective-permute-start.13 = (bf16[16,1792]{1,0:T(8,128)(2,1)S(1)}, bf16[16,1792]{1,0:T(8,128)(2,1)S(1)}, u32[]{:S(2)}, u32[]{:S(2)}) collective-permute-start(bf16[16,1792]{1,0:T(8,128)(2,1)S(1)} %get-tuple-element.68), channel_id=1, source_target_pairs={{0,8},{1,9},{2,10},{3,11},{4,12},{5,13},{6,14},{7,15},{8,0},{9,1},... | collective-permute-start | bytes 172040 | tf_op jit(solution)/shard_map/ppermute | solution.py:171
  22.2 6.2 %collective-permute-start.14 = (bf16[16,1792]{1,0:T(8,128)(2,1)S(1)}, bf16[16,1792]{1,0:T(8,128)(2,1)S(1)}, u32[]{:S(2)}, u32[]{:S(2)}) collective-permute-start(bf16[16,1792]{1,0:T(8,128)(2,1)S(1)} %get-tuple-element.69), channel_id=1, source_target_pairs={{0,12},{1,13},{2,14},{3,15},{4,8},{5,9},{6,10},{7,11},{8,4},{9,5},... | collective-permute-start | bytes 172040 | tf_op jit(solution)/shard_map/ppermute | solution.py:171
  22.3 9.1 %collective-permute-start.6 = (bf16[16,1792]{1,0:T(8,128)(2,1)S(1)}, bf16[16,1792]{1,0:T(8,128)(2,1)S(1)}, u32[]{:S(2)}, u32[]{:S(2)}) collective-permute-start(bf16[16,1792]{1,0:T(8,128)(2,1)S(1)} %get-tuple-element.63), channel_id=1, source_target_pairs={{0,4},{1,5},{2,6},{3,7},{4,0},{5,1},{6,2},{7,3},{8,12},{9,13},{10,... | collective-permute-start | bytes 172040 | tf_op jit(solution)/shard_map/ppermute | solution.py:171
  22.9 9.1 %collective-permute-start.7 = (bf16[16,1792]{1,0:T(8,128)(2,1)S(1)}, bf16[16,1792]{1,0:T(8,128)(2,1)S(1)}, u32[]{:S(2)}, u32[]{:S(2)}) collective-permute-start(bf16[16,1792]{1,0:T(8,128)(2,1)S(1)} %get-tuple-element.64), channel_id=1, source_target_pairs={{0,8},{1,9},{2,10},{3,11},{4,12},{5,13},{6,14},{7,15},{8,0},{9,1},... | collective-permute-start | bytes 172040 | tf_op jit(solution)/shard_map/ppermute | solution.py:171
  26.8 6.4 %collective-permute-start.8 = (bf16[16,1792]{1,0:T(8,128)(2,1)S(1)}, bf16[16,1792]{1,0:T(8,128)(2,1)S(1)}, u32[]{:S(2)}, u32[]{:S(2)}) collective-permute-start(bf16[16,1792]{1,0:T(8,128)(2,1)S(1)} %get-tuple-element.65), channel_id=1, source_target_pairs={{0,12},{1,13},{2,14},{3,15},{4,8},{5,9},{6,10},{7,11},{8,4},{9,5},... | collective-permute-start | bytes 172040 | tf_op jit(solution)/shard_map/ppermute | solution.py:171
  26.9 7.9 %collective-permute-start = (bf16[16,1792]{1,0:T(8,128)(2,1)S(1)}, bf16[16,1792]{1,0:T(8,128)(2,1)S(1)}, u32[]{:S(2)}, u32[]{:S(2)}) collective-permute-start(bf16[16,1792]{1,0:T(8,128)(2,1)S(1)} %get-tuple-element.59), channel_id=1, source_target_pairs={{0,4},{1,5},{2,6},{3,7},{4,0},{5,1},{6,2},{7,3},{8,12},{9,13},{10,... | collective-permute-start | bytes 172040 | tf_op jit(solution)/shard_map/ppermute | solution.py:171
  28.4 7.1 %collective-permute-start.1 = (bf16[16,1792]{1,0:T(8,128)(2,1)S(1)}, bf16[16,1792]{1,0:T(8,128)(2,1)S(1)}, u32[]{:S(2)}, u32[]{:S(2)}) collective-permute-start(bf16[16,1792]{1,0:T(8,128)(2,1)S(1)} %get-tuple-element.60), channel_id=1, source_target_pairs={{0,8},{1,9},{2,10},{3,11},{4,12},{5,13},{6,14},{7,15},{8,0},{9,1},... | collective-permute-start | bytes 172040 | tf_op jit(solution)/shard_map/ppermute | solution.py:171
  31.5 6.0 %collective-permute-start.2 = (bf16[16,1792]{1,0:T(8,128)(2,1)S(1)}, bf16[16,1792]{1,0:T(8,128)(2,1)S(1)}, u32[]{:S(2)}, u32[]{:S(2)}) collective-permute-start(bf16[16,1792]{1,0:T(8,128)(2,1)S(1)} %get-tuple-element.61), channel_id=1, source_target_pairs={{0,12},{1,13},{2,14},{3,15},{4,8},{5,9},{6,10},{7,11},{8,4},{9,5},... | collective-permute-start | bytes 172040 | tf_op jit(solution)/shard_map/ppermute | solution.py:171
  32.0 28.2 %collective-permute-start.16 = (bf16[64,1792]{1,0:T(8,128)(2,1)S(1)}, bf16[64,1792]{1,0:T(8,128)(2,1)S(1)}, u32[]{:S(2)}, u32[]{:S(2)}) collective-permute-start(bf16[64,1792]{1,0:T(8,128)(2,1)S(1)} %constant_dynamic-update-slice_fusion.8.m0), channel_id=1, source_target_pairs={{0,1},{1,0},{2,3},{3,2},{4,5},{5,4},{6,7},{7,6},{8,9},{9,8},{10,11... | collective-permute-start | bytes 688136 | tf_op jit(solution)/shard_map/ppermute | solution.py:171
  33.3 15.0 %collective-permute-start.15 = (bf16[64,1792]{1,0:T(8,128)(2,1)S(1)}, bf16[64,1792]{1,0:T(8,128)(2,1)S(1)}, u32[]{:S(2)}, u32[]{:S(2)}) collective-permute-start(bf16[64,1792]{1,0:T(8,128)(2,1)S(1)} %constant_dynamic-update-slice_fusion.8.m0), channel_id=1, source_target_pairs={{0,2},{1,3},{2,0},{3,1},{4,6},{5,7},{6,4},{7,5},{8,10},{9,11},{10,... | collective-permute-start | bytes 688136 | tf_op jit(solution)/shard_map/ppermute | solution.py:171
  34.8 11.9 %collective-permute-start.9 = (bf16[64,1792]{1,0:T(8,128)(2,1)S(1)}, bf16[64,1792]{1,0:T(8,128)(2,1)S(1)}, u32[]{:S(2)}, u32[]{:S(2)}) collective-permute-start(bf16[64,1792]{1,0:T(8,128)(2,1)S(1)} %constant_dynamic-update-slice_fusion.4.m0), channel_id=1, source_target_pairs={{0,2},{1,3},{2,0},{3,1},{4,6},{5,7},{6,4},{7,5},{8,10},{9,11},{10,... | collective-permute-start | bytes 688136 | tf_op jit(solution)/shard_map/ppermute | solution.py:171
  35.6 16.1 %collective-permute-start.21 = (bf16[64,1792]{1,0:T(8,128)(2,1)S(1)}, bf16[64,1792]{1,0:T(8,128)(2,1)S(1)}, u32[]{:S(2)}, u32[]{:S(2)}) collective-permute-start(bf16[64,1792]{1,0:T(8,128)(2,1)S(1)} %constant_dynamic-update-slice_fusion.12.m0), channel_id=1, source_target_pairs={{0,2},{1,3},{2,0},{3,1},{4,6},{5,7},{6,4},{7,5},{8,10},{9,11},{10,... | collective-permute-start | bytes 688136 | tf_op jit(solution)/shard_map/ppermute | solution.py:171
  37.5 14.6 %collective-permute-start.22 = (bf16[64,1792]{1,0:T(8,128)(2,1)S(1)}, bf16[64,1792]{1,0:T(8,128)(2,1)}, u32[]{:S(2)}, u32[]{:S(2)}) collective-permute-start(bf16[64,1792]{1,0:T(8,128)(2,1)S(1)} %constant_dynamic-update-slice_fusion.12.m0), channel_id=1, source_target_pairs={{0,1},{1,0},{2,3},{3,2},{4,5},{5,4},{6,7},{7,6},{8,9},{9,8},{10,11... | collective-permute-start | bytes 688136 | tf_op jit(solution)/shard_map/ppermute | solution.py:171
  46.7 13.0 %collective-permute-start.3 = (bf16[64,1792]{1,0:T(8,128)(2,1)S(1)}, bf16[64,1792]{1,0:T(8,128)(2,1)S(1)}, u32[]{:S(2)}, u32[]{:S(2)}) collective-permute-start(bf16[64,1792]{1,0:T(8,128)(2,1)S(1)} %constant_dynamic-update-slice_fusion.m0), channel_id=1, source_target_pairs={{0,2},{1,3},{2,0},{3,1},{4,6},{5,7},{6,4},{7,5},{8,10},{9,11},{10,... | collective-permute-start | bytes 688136 | tf_op jit(solution)/shard_map/ppermute | solution.py:171
  48.3 12.1 %collective-permute-start.17 = (bf16[64,1792]{1,0:T(8,128)(2,1)S(1)}, bf16[64,1792]{1,0:T(8,128)(2,1)S(1)}, u32[]{:S(2)}, u32[]{:S(2)}) collective-permute-start(bf16[64,1792]{1,0:T(8,128)(2,1)S(1)} %collective-permute-done.15.m1), channel_id=1, source_target_pairs={{0,1},{1,0},{2,3},{3,2},{4,5},{5,4},{6,7},{7,6},{8,9},{9,8},{10,11... | collective-permute-start | bytes 688136 | tf_op jit(solution)/shard_map/ppermute | solution.py:171
  51.6 1.6 %collective-permute-start.23 = (bf16[64,1792]{1,0:T(8,128)(2,1)S(1)}, bf16[64,1792]{1,0:T(8,128)(2,1)}, u32[]{:S(2)}, u32[]{:S(2)}) collective-permute-start(bf16[64,1792]{1,0:T(8,128)(2,1)S(1)} %collective-permute-done.21.m1), channel_id=1, source_target_pairs={{0,1},{1,0},{2,3},{3,2},{4,5},{5,4},{6,7},{7,6},{8,9},{9,8},{10,11... | collective-permute-start | bytes 688136 | tf_op jit(solution)/shard_map/ppermute | solution.py:171
  52.1 11.4 %collective-permute-start.10 = (bf16[64,1792]{1,0:T(8,128)(2,1)S(1)}, bf16[64,1792]{1,0:T(8,128)(2,1)S(1)}, u32[]{:S(2)}, u32[]{:S(2)}) collective-permute-start(bf16[64,1792]{1,0:T(8,128)(2,1)S(1)} %constant_dynamic-update-slice_fusion.4.m0), channel_id=1, source_target_pairs={{0,1},{1,0},{2,3},{3,2},{4,5},{5,4},{6,7},{7,6},{8,9},{9,8},{10,11... | collective-permute-start | bytes 688136 | tf_op jit(solution)/shard_map/ppermute | solution.py:171
  53.3 10.2 %collective-permute-start.11 = (bf16[64,1792]{1,0:T(8,128)(2,1)S(1)}, bf16[64,1792]{1,0:T(8,128)(2,1)S(1)}, u32[]{:S(2)}, u32[]{:S(2)}) collective-permute-start(bf16[64,1792]{1,0:T(8,128)(2,1)S(1)} %collective-permute-done.9.m1), channel_id=1, source_target_pairs={{0,1},{1,0},{2,3},{3,2},{4,5},{5,4},{6,7},{7,6},{8,9},{9,8},{10,11... | collective-permute-start | bytes 688136 | tf_op jit(solution)/shard_map/ppermute | solution.py:171
  53.4 3.1 %copy-start.2 = (bf16[512,7168]{1,0:T(8,128)(2,1)S(1)}, bf16[512,7168]{1,0:T(8,128)(2,1)}, u32[]{:S(2)}) copy-start(bf16[512,7168]{1,0:T(8,128)(2,1)} %weights_ref.7) | copy-start | bytes 22020100
  59.8 6.3 %collective-permute-start.4 = (bf16[64,1792]{1,0:T(8,128)(2,1)S(1)}, bf16[64,1792]{1,0:T(8,128)(2,1)S(1)}, u32[]{:S(2)}, u32[]{:S(2)}) collective-permute-start(bf16[64,1792]{1,0:T(8,128)(2,1)S(1)} %constant_dynamic-update-slice_fusion.m0), channel_id=1, source_target_pairs={{0,1},{1,0},{2,3},{3,2},{4,5},{5,4},{6,7},{7,6},{8,9},{9,8},{10,11... | collective-permute-start | bytes 688136 | tf_op jit(solution)/shard_map/ppermute | solution.py:171
  60.2 5.8 %collective-permute-start.5 = (bf16[64,1792]{1,0:T(8,128)(2,1)S(1)}, bf16[64,1792]{1,0:T(8,128)(2,1)S(1)}, u32[]{:S(2)}, u32[]{:S(2)}) collective-permute-start(bf16[64,1792]{1,0:T(8,128)(2,1)S(1)} %collective-permute-done.3.m1), channel_id=1, source_target_pairs={{0,1},{1,0},{2,3},{3,2},{4,5},{5,4},{6,7},{7,6},{8,9},{9,8},{10,11... | collective-permute-start | bytes 688136 | tf_op jit(solution)/shard_map/ppermute | solution.py:171
  63.5 35.1 %slice-start = ((s8[14680064]{0:T(1024)(128)(4,1)}), s8[4194304]{0:T(1024)(128)(4,1)S(1)}, s32[]{:S(2)}) async-start(s8[14680064]{0:T(1024)(128)(4,1)} %bitcast.10), calls=%async_computation | async-start | bytes 8388608
  63.5 35.1 %slice-start.1 = ((s8[14680064]{0:T(1024)(128)(4,1)}), s8[4194304]{0:T(1024)(128)(4,1)S(1)}, s32[]{:S(2)}) async-start(s8[14680064]{0:T(1024)(128)(4,1)} %bitcast.10), calls=%async_computation.1 | async-start | bytes 8388608
  66.1 32.5 %slice-start.2 = ((s8[14680064]{0:T(1024)(128)(4,1)}), s8[4194304]{0:T(1024)(128)(4,1)S(1)}, s32[]{:S(2)}) async-start(s8[14680064]{0:T(1024)(128)(4,1)} %bitcast.10), calls=%async_computation.2 | async-start | bytes 8388608
  68.6 1.9 %collective-permute-start.39 = (bf16[128,1792]{1,0:T(8,128)(2,1)S(1)}, bf16[128,1792]{1,0:T(8,128)(2,1)S(1)}, u32[]{:S(2)}, u32[]{:S(2)}) collective-permute-start(bf16[128,1792]{1,0:T(8,128)(2,1)S(1)} %get-tuple-element.104), channel_id=1, source_target_pairs={{0,1},{1,0},{2,3},{3,2},{4,5},{5,4},{6,7},{7,6},{8,9},{9,8},{10,11... | collective-permute-start | bytes 1376264 | tf_op jit(solution)/shard_map/ppermute | solution.py:171
  69.0 3.3 %collective-permute-start.34 = (bf16[128,1792]{1,0:T(8,128)(2,1)S(1)}, bf16[128,1792]{1,0:T(8,128)(2,1)S(1)}, u32[]{:S(2)}, u32[]{:S(2)}) collective-permute-start(bf16[128,1792]{1,0:T(8,128)(2,1)S(1)} %get-tuple-element.96), channel_id=1, source_target_pairs={{0,1},{1,0},{2,3},{3,2},{4,5},{5,4},{6,7},{7,6},{8,9},{9,8},{10,11... | collective-permute-start | bytes 1376264 | tf_op jit(solution)/shard_map/ppermute | solution.py:171
  69.2 4.5 %collective-permute-start.29 = (bf16[128,1792]{1,0:T(8,128)(2,1)}, bf16[128,1792]{1,0:T(8,128)(2,1)S(1)}, u32[]{:S(2)}, u32[]{:S(2)}) collective-permute-start(bf16[128,1792]{1,0:T(8,128)(2,1)} %get-tuple-element.88), channel_id=1, source_target_pairs={{0,1},{1,0},{2,3},{3,2},{4,5},{5,4},{6,7},{7,6},{8,9},{9,8},{10,11... | collective-permute-start | bytes 1376264 | tf_op jit(solution)/shard_map/ppermute | solution.py:171
  69.5 5.6 %collective-permute-start.24 = (bf16[128,1792]{1,0:T(8,128)(2,1)S(1)}, bf16[128,1792]{1,0:T(8,128)(2,1)S(1)}, u32[]{:S(2)}, u32[]{:S(2)}) collective-permute-start(bf16[128,1792]{1,0:T(8,128)(2,1)S(1)} %get-tuple-element.80), channel_id=1, source_target_pairs={{0,1},{1,0},{2,3},{3,2},{4,5},{5,4},{6,7},{7,6},{8,9},{9,8},{10,11... | collective-permute-start | bytes 1376264 | tf_op jit(solution)/shard_map/ppermute | solution.py:171
  70.8 8.5 %collective-permute-start.40 = (bf16[64,1792]{1,0:T(8,128)(2,1)S(1)}, bf16[64,1792]{1,0:T(8,128)(2,1)S(1)}, u32[]{:S(2)}, u32[]{:S(2)}) collective-permute-start(bf16[64,1792]{1,0:T(8,128)(2,1)S(1)} %get-tuple-element.106), channel_id=1, source_target_pairs={{0,2},{1,3},{2,0},{3,1},{4,6},{5,7},{6,4},{7,5},{8,10},{9,11},{10,... | collective-permute-start | bytes 688136 | tf_op jit(solution)/shard_map/ppermute | solution.py:171
  72.4 26.2 %slice-start.3 = ((s8[14680064]{0:T(1024)(128)(4,1)}), s8[2097152]{0:T(1024)(128)(4,1)S(1)}, s32[]{:S(2)}) async-start(s8[14680064]{0:T(1024)(128)(4,1)} %bitcast.10), calls=%async_computation.3 | async-start | bytes 4194304
  72.7 11.5 %collective-permute-start.35 = (bf16[64,1792]{1,0:T(8,128)(2,1)S(1)}, bf16[64,1792]{1,0:T(8,128)(2,1)S(1)}, u32[]{:S(2)}, u32[]{:S(2)}) collective-permute-start(bf16[64,1792]{1,0:T(8,128)(2,1)S(1)} %get-tuple-element.98), channel_id=1, source_target_pairs={{0,2},{1,3},{2,0},{3,1},{4,6},{5,7},{6,4},{7,5},{8,10},{9,11},{10,... | collective-permute-start | bytes 688136 | tf_op jit(solution)/shard_map/ppermute | solution.py:171
  74.0 15.1 %collective-permute-start.30 = (bf16[64,1792]{1,0:T(8,128)(2,1)S(1)}, bf16[64,1792]{1,0:T(8,128)(2,1)S(1)}, u32[]{:S(2)}, u32[]{:S(2)}) collective-permute-start(bf16[64,1792]{1,0:T(8,128)(2,1)S(1)} %get-tuple-element.90), channel_id=1, source_target_pairs={{0,2},{1,3},{2,0},{3,1},{4,6},{5,7},{6,4},{7,5},{8,10},{9,11},{10,... | collective-permute-start | bytes 688136 | tf_op jit(solution)/shard_map/ppermute | solution.py:171
  75.4 18.0 %collective-permute-start.25 = (bf16[64,1792]{1,0:T(8,128)(2,1)S(1)}, bf16[64,1792]{1,0:T(8,128)(2,1)S(1)}, u32[]{:S(2)}, u32[]{:S(2)}) collective-permute-start(bf16[64,1792]{1,0:T(8,128)(2,1)S(1)} %get-tuple-element.82), channel_id=1, source_target_pairs={{0,2},{1,3},{2,0},{3,1},{4,6},{5,7},{6,4},{7,5},{8,10},{9,11},{10,... | collective-permute-start | bytes 688136 | tf_op jit(solution)/shard_map/ppermute | solution.py:171
  79.5 14.6 %collective-permute-start.41 = (bf16[16,1792]{1,0:T(8,128)(2,1)S(1)}, bf16[16,1792]{1,0:T(8,128)(2,1)S(1)}, u32[]{:S(2)}, u32[]{:S(2)}) collective-permute-start(bf16[16,1792]{1,0:T(8,128)(2,1)S(1)} %get-tuple-element.108), channel_id=1, source_target_pairs={{0,4},{1,5},{2,6},{3,7},{4,0},{5,1},{6,2},{7,3},{8,12},{9,13},{10,... | collective-permute-start | bytes 172040 | tf_op jit(solution)/shard_map/ppermute | solution.py:171
  80.5 16.6 %collective-permute-start.42 = (bf16[16,1792]{1,0:T(8,128)(2,1)S(1)}, bf16[16,1792]{1,0:T(8,128)(2,1)S(1)}, u32[]{:S(2)}, u32[]{:S(2)}) collective-permute-start(bf16[16,1792]{1,0:T(8,128)(2,1)S(1)} %get-tuple-element.109), channel_id=1, source_target_pairs={{0,8},{1,9},{2,10},{3,11},{4,12},{5,13},{6,14},{7,15},{8,0},{9,1},... | collective-permute-start | bytes 172040 | tf_op jit(solution)/shard_map/ppermute | solution.py:171
  84.2 13.0 %collective-permute-start.43 = (bf16[16,1792]{1,0:T(8,128)(2,1)S(1)}, bf16[16,1792]{1,0:T(8,128)(2,1)S(1)}, u32[]{:S(2)}, u32[]{:S(2)}) collective-permute-start(bf16[16,1792]{1,0:T(8,128)(2,1)S(1)} %get-tuple-element.110), channel_id=1, source_target_pairs={{0,12},{1,13},{2,14},{3,15},{4,8},{5,9},{6,10},{7,11},{8,4},{9,5},... | collective-permute-start | bytes 172040 | tf_op jit(solution)/shard_map/ppermute | solution.py:171
  89.1 12.0 %collective-permute-start.36 = (bf16[16,1792]{1,0:T(8,128)(2,1)S(1)}, bf16[16,1792]{1,0:T(8,128)(2,1)S(1)}, u32[]{:S(2)}, u32[]{:S(2)}) collective-permute-start(bf16[16,1792]{1,0:T(8,128)(2,1)S(1)} %get-tuple-element.100), channel_id=1, source_target_pairs={{0,4},{1,5},{2,6},{3,7},{4,0},{5,1},{6,2},{7,3},{8,12},{9,13},{10,... | collective-permute-start | bytes 172040 | tf_op jit(solution)/shard_map/ppermute | solution.py:171
  93.5 10.6 %collective-permute-start.37 = (bf16[16,1792]{1,0:T(8,128)(2,1)S(1)}, bf16[16,1792]{1,0:T(8,128)(2,1)S(1)}, u32[]{:S(2)}, u32[]{:S(2)}) collective-permute-start(bf16[16,1792]{1,0:T(8,128)(2,1)S(1)} %get-tuple-element.101), channel_id=1, source_target_pairs={{0,8},{1,9},{2,10},{3,11},{4,12},{5,13},{6,14},{7,15},{8,0},{9,1},... | collective-permute-start | bytes 172040 | tf_op jit(solution)/shard_map/ppermute | solution.py:171
  94.1 9.9 %collective-permute-start.38 = (bf16[16,1792]{1,0:T(8,128)(2,1)S(1)}, bf16[16,1792]{1,0:T(8,128)(2,1)S(1)}, u32[]{:S(2)}, u32[]{:S(2)}) collective-permute-start(bf16[16,1792]{1,0:T(8,128)(2,1)S(1)} %get-tuple-element.102), channel_id=1, source_target_pairs={{0,12},{1,13},{2,14},{3,15},{4,8},{5,9},{6,10},{7,11},{8,4},{9,5},... | collective-permute-start | bytes 172040 | tf_op jit(solution)/shard_map/ppermute | solution.py:171
  97.0 10.8 %collective-permute-start.31 = (bf16[16,1792]{1,0:T(8,128)(2,1)S(1)}, bf16[16,1792]{1,0:T(8,128)(2,1)S(1)}, u32[]{:S(2)}, u32[]{:S(2)}) collective-permute-start(bf16[16,1792]{1,0:T(8,128)(2,1)S(1)} %get-tuple-element.92), channel_id=1, source_target_pairs={{0,4},{1,5},{2,6},{3,7},{4,0},{5,1},{6,2},{7,3},{8,12},{9,13},{10,... | collective-permute-start | bytes 172040 | tf_op jit(solution)/shard_map/ppermute | solution.py:171
  97.2 13.6 %collective-permute-start.32 = (bf16[16,1792]{1,0:T(8,128)(2,1)S(1)}, bf16[16,1792]{1,0:T(8,128)(2,1)S(1)}, u32[]{:S(2)}, u32[]{:S(2)}) collective-permute-start(bf16[16,1792]{1,0:T(8,128)(2,1)S(1)} %get-tuple-element.93), channel_id=1, source_target_pairs={{0,8},{1,9},{2,10},{3,11},{4,12},{5,13},{6,14},{7,15},{8,0},{9,1},... | collective-permute-start | bytes 172040 | tf_op jit(solution)/shard_map/ppermute | solution.py:171
  101.1 9.7 %collective-permute-start.33 = (bf16[16,1792]{1,0:T(8,128)(2,1)S(1)}, bf16[16,1792]{1,0:T(8,128)(2,1)S(1)}, u32[]{:S(2)}, u32[]{:S(2)}) collective-permute-start(bf16[16,1792]{1,0:T(8,128)(2,1)S(1)} %get-tuple-element.94), channel_id=1, source_target_pairs={{0,12},{1,13},{2,14},{3,15},{4,8},{5,9},{6,10},{7,11},{8,4},{9,5},... | collective-permute-start | bytes 172040 | tf_op jit(solution)/shard_map/ppermute | solution.py:171
  104.0 9.1 %collective-permute-start.26 = (bf16[16,1792]{1,0:T(8,128)(2,1)S(1)}, bf16[16,1792]{1,0:T(8,128)(2,1)S(1)}, u32[]{:S(2)}, u32[]{:S(2)}) collective-permute-start(bf16[16,1792]{1,0:T(8,128)(2,1)S(1)} %get-tuple-element.84), channel_id=1, source_target_pairs={{0,4},{1,5},{2,6},{3,7},{4,0},{5,1},{6,2},{7,3},{8,12},{9,13},{10,... | collective-permute-start | bytes 172040 | tf_op jit(solution)/shard_map/ppermute | solution.py:171
  104.0 9.1 %collective-permute-start.27 = (bf16[16,1792]{1,0:T(8,128)(2,1)S(1)}, bf16[16,1792]{1,0:T(8,128)(2,1)S(1)}, u32[]{:S(2)}, u32[]{:S(2)}) collective-permute-start(bf16[16,1792]{1,0:T(8,128)(2,1)S(1)} %get-tuple-element.85), channel_id=1, source_target_pairs={{0,8},{1,9},{2,10},{3,11},{4,12},{5,13},{6,14},{7,15},{8,0},{9,1},... | collective-permute-start | bytes 172040 | tf_op jit(solution)/shard_map/ppermute | solution.py:171
  107.9 6.0 %collective-permute-start.28 = (bf16[16,1792]{1,0:T(8,128)(2,1)S(1)}, bf16[16,1792]{1,0:T(8,128)(2,1)S(1)}, u32[]{:S(2)}, u32[]{:S(2)}) collective-permute-start(bf16[16,1792]{1,0:T(8,128)(2,1)S(1)} %get-tuple-element.86), channel_id=1, source_target_pairs={{0,12},{1,13},{2,14},{3,15},{4,8},{5,9},{6,10},{7,11},{8,4},{9,5},... | collective-permute-start | bytes 172040 | tf_op jit(solution)/shard_map/ppermute | solution.py:171
  116.2 9.5 %collective-permute-start.46 = (f32[4,64]{1,0:T(4,128)S(1)}, f32[4,64]{1,0:T(4,128)S(1)}, u32[]{:S(2)}, u32[]{:S(2)}) collective-permute-start(f32[4,64]{1,0:T(4,128)S(1)} %add_add_fusion.1), channel_id=1, source_target_pairs={{0,3},{1,2},{2,1},{3,0},{4,7},{5,6},{6,5},{7,4},{8,11},{9,10},{10,... | collective-permute-start | bytes 3080 | tf_op jit(solution)/shard_map/ppermute | solution.py:171
  116.3 9.4 %collective-permute-start.45 = (f32[4,64]{1,0:T(4,128)S(1)}, f32[4,64]{1,0:T(4,128)S(1)}, u32[]{:S(2)}, u32[]{:S(2)}) collective-permute-start(f32[4,64]{1,0:T(4,128)S(1)} %add_add_fusion.1), channel_id=1, source_target_pairs={{0,2},{1,3},{2,0},{3,1},{4,6},{5,7},{6,4},{7,5},{8,10},{9,11},{10,... | collective-permute-start | bytes 3080 | tf_op jit(solution)/shard_map/ppermute | solution.py:171
  118.1 7.6 %collective-permute-start.44 = (f32[4,64]{1,0:T(4,128)S(1)}, f32[4,64]{1,0:T(4,128)S(1)}, u32[]{:S(2)}, u32[]{:S(2)}) collective-permute-start(f32[4,64]{1,0:T(4,128)S(1)} %add_add_fusion.1), channel_id=1, source_target_pairs={{0,1},{1,0},{2,3},{3,2},{4,5},{5,4},{6,7},{7,6},{8,9},{9,8},{10,11... | collective-permute-start | bytes 3080 | tf_op jit(solution)/shard_map/ppermute | solution.py:171
  125.8 7.4 %copy-start.4 = (f32[4,64]{1,0:T(4,128)S(1)}, f32[4,64]{1,0:T(4,128)}, u32[]{:S(2)}) copy-start(f32[4,64]{1,0:T(4,128)} %coeff_ref.1) | copy-start | bytes 3076
  125.8 7.0 %collective-permute-start.49 = (f32[4,64]{1,0:T(4,128)S(1)}, f32[4,64]{1,0:T(4,128)S(1)}, u32[]{:S(2)}, u32[]{:S(2)}) collective-permute-start(f32[4,64]{1,0:T(4,128)S(1)} %add_add_fusion), channel_id=1, source_target_pairs={{0,12},{1,13},{2,14},{3,15},{4,8},{5,9},{6,10},{7,11},{8,4},{9,5},... | collective-permute-start | bytes 3080 | tf_op jit(solution)/shard_map/ppermute | solution.py:171
  128.7 4.5 %collective-permute-start.48 = (f32[4,64]{1,0:T(4,128)S(1)}, f32[4,64]{1,0:T(4,128)S(1)}, u32[]{:S(2)}, u32[]{:S(2)}) collective-permute-start(f32[4,64]{1,0:T(4,128)S(1)} %add_add_fusion), channel_id=1, source_target_pairs={{0,8},{1,9},{2,10},{3,11},{4,12},{5,13},{6,14},{7,15},{8,0},{9,1},... | collective-permute-start | bytes 3080 | tf_op jit(solution)/shard_map/ppermute | solution.py:171
  128.7 4.5 %collective-permute-start.47 = (f32[4,64]{1,0:T(4,128)S(1)}, f32[4,64]{1,0:T(4,128)S(1)}, u32[]{:S(2)}, u32[]{:S(2)}) collective-permute-start(f32[4,64]{1,0:T(4,128)S(1)} %add_add_fusion), channel_id=1, source_target_pairs={{0,4},{1,5},{2,6},{3,7},{4,0},{5,1},{6,2},{7,3},{8,12},{9,13},{10,... | collective-permute-start | bytes 3080 | tf_op jit(solution)/shard_map/ppermute | solution.py:171

commit v2 on v1

v2 whole, which is shorter than its diff:
```python
import functools
import math

import jax
import jax.numpy as jnp
from jax import lax
from jax.experimental import pallas as pl
from jax.experimental.pallas import tpu as pltpu
from jax.sharding import PartitionSpec as P

F32, BF16 = jnp.float32, jnp.bfloat16
HIGHEST = lax.Precision.HIGHEST
SHARES = (1, 1)
LAG = 1
FAR = 2
FLOPS = 0
VMEM_LIMIT = 24 * 2**20


def iota(shape, dim):
    return lax.broadcasted_iota(jnp.int32, shape, dim)


def spread_kernel(rows, scale, place_ref, coeff_ref, spread_ref, spread_t_ref):
    experts, bases = coeff_ref.shape
    mix = jnp.tanh(coeff_ref[...]).astype(BF16).astype(F32)
    place = place_ref[0]
    tall = experts * rows
    wide = bases * rows
    owner = jnp.bitwise_xor(iota((tall, bases), 0) // rows, place)
    picked = jnp.zeros((tall, bases), F32)
    for e in range(experts):
        picked = jnp.where(owner == e, mix[e : e + 1, :], picked)
    widen = (iota((bases, wide), 1) // rows == iota((bases, wide), 0)).astype(BF16)
    spread = jnp.dot(picked.astype(BF16), widen, preferred_element_type=F32)
    same = iota((tall, wide), 0) % rows == iota((tall, wide), 1) % rows
    spread = jnp.where(same, spread, 0.0)
    spread_ref[...] = spread.astype(BF16)
    spread_t_ref[...] = (spread.T * scale).astype(BF16)


def streamed(start, source_ref, held_ref, sems):
    step = pl.program_id(0)
    block = held_ref.shape[2]

    def copy(at):
        column = start + at * block
        if not isinstance(column, int):
            column = pl.multiple_of(column, 128)
        return pltpu.make_async_copy(
            source_ref.at[:, pl.ds(column, block)], held_ref.at[at], sems.at[at]
        )

    @pl.when(step == 0)
    def _():
        for at in range(held_ref.shape[0]):
            copy(at).start()

    copy(step).wait()
    return held_ref[step]


def mix_kernel(start, spread_ref, bases_ref, *refs):
    *out_refs, held_ref, sems = refs
    held = streamed(start, bases_ref, held_ref, sems)
    mixed = jnp.dot(spread_ref[...], held, preferred_element_type=F32)
    rows = mixed.shape[0] // len(out_refs)
    for j, out_ref in enumerate(out_refs):
        out_ref[...] = mixed[j * rows : (j + 1) * rows].astype(BF16)


def join_kernel(*refs):
    *part_refs, out_ref = refs
    rows = part_refs[0].shape[0]
    for j, part_ref in enumerate(part_refs):
        out_ref[j * rows : (j + 1) * rows, :] = part_ref[...]


def fit_kernel(first, start, load_ref, load_t_ref, weights_ref, *refs):
    mixture_refs, refs = refs[:4], refs[4:]
    *refs, held_ref, sems = refs
    weights = streamed(start, weights_ref, held_ref, sems)
    if first:
        near_ref, *far_refs, grad_ref = refs
    else:
        before_ref, near_ref, *far_refs, grad_ref = refs
    mixture = jnp.concatenate([ref[...] for ref in mixture_refs], axis=0)
    product = jnp.dot(load_ref[...], mixture, preferred_element_type=F32)
    residual = (product - weights.astype(F32)).astype(BF16)
    grad = lax.dot_general(
        residual, mixture, (((1,), (1,)), ((), ())), preferred_element_type=F32
    )
    partial = jnp.dot(load_t_ref[...], residual, preferred_element_type=F32)
    half = partial.shape[0] // 2
    near_ref[...] = partial[:half]
    share = half // len(far_refs)
    for j, far_ref in enumerate(far_refs):
        far_ref[...] = partial[half + j * share : half + (j + 1) * share].astype(BF16)

    @pl.when(pl.program_id(0) == 0)
    def _():
        if first:
            grad_ref[...] = grad
        else:
            grad_ref[...] = before_ref[...] + grad

    @pl.when(pl.program_id(0) > 0)
    def _():
        grad_ref[...] += grad


def chip_sum_kernel(near_ref, *refs):
    *got_refs, keep_ref, send_ref = refs
    got = jnp.concatenate([ref[...] for ref in got_refs], axis=0)
    total = near_ref[...] + got.astype(F32)
    half = total.shape[0] // 2
    keep_ref[...] = total[:half]
    send_ref[...] = total[half:].astype(BF16)


def plane_sum_kernel(keep_ref, got_ref, *out_refs):
    total = keep_ref[...] + got_ref[...].astype(F32)
    rows = total.shape[0] // len(out_refs)
    for j, out_ref in enumerate(out_refs):
        out_ref[...] = total[j * rows : (j + 1) * rows].astype(BF16)


def inner_kernel(rows, experts, start, place_ref, bases_ref, *refs):
    *sum_refs, inner_ref, acc_ref, held_ref, sems = refs
    held = streamed(start, bases_ref, held_ref, sems)
    summed = jnp.concatenate([ref[...] for ref in sum_refs], axis=0)
    step = lax.dot_general(
        summed, held, (((1,), (1,)), ((), ())), preferred_element_type=F32
    )

    @pl.when(pl.program_id(0) == 0)
    def _():
        acc_ref[...] = step

    @pl.when(pl.program_id(0) > 0)
    def _():
        acc_ref[...] += step

    @pl.when(pl.program_id(0) == pl.num_programs(0) - 1)
    def _():
        tall, wide = acc_ref.shape
        bases = wide // rows
        same = iota((tall, wide), 0) % rows == iota((tall, wide), 1) % rows
        kept = jnp.where(same, acc_ref[...], 0.0)
        owner = jnp.bitwise_xor(iota((experts, tall), 1) // rows, place_ref[0])
        gather = (owner == iota((experts, tall), 0)).astype(F32)
        narrow = (iota((wide, bases), 0) // rows == iota((wide, bases), 1)).astype(F32)
        by_expert = jnp.dot(gather, kept, precision=HIGHEST, preferred_element_type=F32)
        inner_ref[...] = jnp.dot(
            by_expert, narrow, precision=HIGHEST, preferred_element_type=F32
        )


def basis_kernel(scale, skip, spread_t_ref, *refs):
    *sum_refs, out_ref, token_ref = refs[skip:]
    token_ref[...] = jnp.zeros_like(token_ref)
    summed = jnp.concatenate([ref[...] for ref in sum_refs], axis=0)
    grad = jnp.dot(spread_t_ref[...], summed, preferred_element_type=F32)
    if scale != 1.0:
        grad = grad * scale
    out_ref[...] = grad.astype(BF16)


def whole_spec(shape):
    return pl.BlockSpec(shape, lambda s: (0,) * len(shape))


def column_spec(rows, block, start=0):
    return pl.BlockSpec((rows, block), lambda s: (0, start + s))


def per_device(weights, loadings, bases, coeff):
    devices = lax.axis_size("expert")
    num_bases, rows, width = bases.shape
    experts = coeff.shape[0]
    group = devices // experts
    assert group == 4 and experts & (experts - 1) == 0
    ff = loadings.shape[0]
    rank = rows * devices
    tall, wide = experts * rows, num_bases * rows
    split = rows % 16 == 0
    widths = [width * share // sum(SHARES) for share in SHARES] if experts <= 8 else [width]
    chunks = len(widths)
    starts = [sum(widths[:j]) for j in range(chunks)]
    block = math.gcd(*widths)
    while block > 1024 and block % 256 == 0:
        block //= 2
    me = lax.axis_index("expert")
    place = (me // group).astype(jnp.int32).reshape(1)
    smem = pl.BlockSpec(memory_space=pltpu.SMEM)
    vmem = pl.BlockSpec(memory_space=pltpu.VMEM)
    anywhere = pl.BlockSpec(memory_space=pl.ANY)
    hbm = pl.BlockSpec(memory_space=pltpu.HBM)

    def send(x, flip):
        return lax.ppermute(x, "expert", [(i, i ^ flip) for i in range(devices)])

    def pieces_of(x):
        return [x[j * rows : (j + 1) * rows] for j in range(experts)]

    def pinned(array, spec):
        return pltpu.with_memory_space_constraint(array, pltpu.HBM) if spec is hbm else array

    def call(kernel, name, ins, outs, grid=None, after=(), flops=0, bytes_accessed=0, alias=None, **kw):
        count, late = len(ins), len(after)

        def body(*refs):
            kernel(*refs[:count], *refs[count + late :])

        return pl.pallas_call(
            body,
            out_shape=[shape for shape, _ in outs],
            in_specs=[spec for _, spec in ins] + [anywhere] * late,
            out_specs=[spec for _, spec in outs],
            compiler_params=pltpu.CompilerParams(vmem_limit_bytes=VMEM_LIMIT),
            cost_estimate=pl.CostEstimate(
                flops=FLOPS * flops, bytes_accessed=FLOPS * bytes_accessed, transcendentals=0
            ),
            input_output_aliases=alias or {},
            name=name,
            **({} if grid is None else {"grid": grid}),
            **kw,
        )(*[pinned(array, spec) for array, spec in ins], *after)

    def shape(*dims, dtype=BF16):
        return jax.ShapeDtypeStruct(dims, dtype)

    def col(rows_in, start=0):
        return column_spec(rows_in, block, start // block)

    def held(j, rows_in):
        steps = widths[j] // block
        return [pltpu.VMEM((steps, rows_in, block), BF16), pltpu.SemaphoreType.DMA((steps,))]

    flat = bases.reshape(wide, width)
    root = math.isqrt(experts)
    exact = root * root == experts and root & (root - 1) == 0
    spread, spread_t = call(
        functools.partial(spread_kernel, rows, 1.0 / root if exact else 1.0),
        "spread",
        [(place, smem), (coeff, vmem)],
        [(shape(tall, wide), vmem), (shape(wide, tall), vmem)],
    )
    late_scale = 1.0 if exact else 1.0 / math.sqrt(experts)

    local = jnp.arange(rank, dtype=jnp.int32)
    piece = local // rows
    flips = (piece % experts) * group + (piece // experts % 2) * 2 + piece // (2 * experts)
    absolute = (me ^ flips) * rows + local % rows
    order = (jnp.arange(rank, dtype=jnp.int32)[:, None] == absolute[None, :]).astype(BF16)
    load = jnp.dot(loadings, order, preferred_element_type=F32).astype(BF16)
    load_t = lax.dot_general(
        order, loadings, (((0,), (1,)), ((), ())), preferred_element_type=F32
    ).astype(BF16)

    def mix_chunk(j, after):
        count = experts if split else 1
        outs = call(
            functools.partial(mix_kernel, starts[j]),
            "mix",
            [(spread, whole_spec((tall, wide))), (flat, hbm)],
            [(shape(tall // count, widths[j]), col(tall // count))] * count,
            (widths[j] // block,),
            after,
            2 * tall * wide * widths[j] * 4,
            2 * wide * widths[j],
            scratch_shapes=held(j, wide),
        )
        return list(outs) if split else pieces_of(outs[0])

    def join(j, parts, after):
        if not split:
            return jnp.concatenate(parts, axis=0)
        return call(
            join_kernel,
            "join",
            [(part, vmem) for part in parts],
            [(shape(tall, widths[j]), vmem)],
            after=after,
        )[0]

    def fit_chunk(j, parts, before, after):
        first = before is None
        extra = [] if first else [(before, whole_spec((ff, rank)))]
        half = rank // 2
        return call(
            functools.partial(fit_kernel, first, starts[j]),
            "fit",
            [
                (load, whole_spec((ff, rank))),
                (load_t, whole_spec((rank, ff))),
                (weights, hbm),
                *[(part, col(half // 2)) for part in parts],
                *extra,
            ],
            [
                (shape(half, widths[j], dtype=F32), col(half)),
                *[(shape(half // FAR, widths[j]), col(half // FAR))] * FAR,
                (shape(ff, rank, dtype=F32), whole_spec((ff, rank))),
            ],
            (widths[j] // block,),
            after,
            6 * ff * rank * widths[j],
            2 * ff * widths[j],
            scratch_shapes=held(j, ff),
        )

    def chip_sum(j, near, got, after):
        half = rank // 4
        return call(
            chip_sum_kernel,
            "chip_sum",
            [(near, col(2 * half)), *[(part, col(2 * half // FAR)) for part in got]],
            [
                (shape(half, widths[j], dtype=F32), col(half)),
                (shape(half, widths[j]), col(half)),
            ],
            (widths[j] // block,),
            after,
            2 * half * widths[j],
            16 * half * widths[j],
        )

    def plane_sum(j, keep, got, after):
        count = experts if split else 1
        outs = call(
            plane_sum_kernel,
            "plane_sum",
            [(keep, col(tall)), (got, col(tall))],
            [(shape(tall // count, widths[j]), col(tall // count))] * count,
            (widths[j] // block,),
            after,
            tall * widths[j],
            8 * tall * widths[j],
        )
        return list(outs) if split else pieces_of(outs[0])

    def sums_of(sums):
        sums = sums if split else [jnp.concatenate(sums, axis=0)]
        return [(part, col(tall // len(sums))) for part in sums]

    def inner_chunk(j, sums, after):
        return call(
            functools.partial(inner_kernel, rows, experts, starts[j]),
            "inner",
            [(place, smem), (flat, hbm), *sums_of(sums)],
            [(shape(experts, num_bases, dtype=F32), whole_spec((experts, num_bases)))],
            (widths[j] // block,),
            after,
            2 * tall * wide * widths[j] * 4,
            2 * wide * widths[j],
            scratch_shapes=[pltpu.VMEM((tall, wide), F32), *held(j, wide)],
        )[0]

    def basis_chunk(j, sums, before, after, first=0, last=None):
        extra = [] if before is None else [(before, hbm)]
        last = widths[j] // block if last is None else last
        size = (last - first) * block
        return call(
            functools.partial(basis_kernel, late_scale, len(extra)),
            "basis",
            [
                (spread_t, whole_spec((wide, tall))),
                *extra,
                *[(part, col(part.shape[0], first * block)) for part, _ in sums_of(sums)],
            ],
            [
                (shape(wide, width), col(wide, starts[j] + first * block)),
                (shape(8, 128, dtype=F32), whole_spec((8, 128))),
            ],
            (last - first,),
            after,
            2 * tall * wide * size * 4,
            2 * wide * size,
            alias={1: 0} if extra else None,
        )

    mixes, gathered, returned, inners = [], [], [], []
    for j in range(chunks):
        mixes.append(mix_chunk(j, [mixes[-1][0]] if j else []))
    done = [mixes[-1][0]]
    for j in range(chunks):
        mixed = mixes[j]
        got = [mixed[0]] + [send(mixed[k], k * group) for k in range(1, experts)]
        own = join(j, got, done)
        done = [own]
        row = send(own, 2)
        gathered.append((own, row, send(own, 1), send(row, 1)))
    grad_local, kept = None, {}

    def return_plane(j, after):
        keep, away = kept.pop(j)
        sums = plane_sum(j, keep, away, after)
        returned.append([sums[0]] + [send(sums[k], k * group) for k in range(1, experts)])
        return [sums[0]]

    for j in range(chunks):
        near, *far, grad_local = fit_chunk(j, gathered[j], grad_local, done)
        done = [near]
        if j >= LAG:
            done = return_plane(j - LAG, done)
        keep, away = chip_sum(j, near, [send(part, 1) for part in far], done)
        kept[j] = keep, send(away, 2)
        done = [keep]
    grad_a = jnp.dot(
        grad_local, order.astype(F32).T, precision=HIGHEST, preferred_element_type=F32
    ) / math.sqrt(width)
    for j in sorted(kept):
        done = return_plane(j, done + [pinned(grad_a, hbm)])
    grad_flat = None
    for j in range(chunks):
        inners.append(inner_chunk(j, returned[j], done))
        done = [inners[-1]]
        if j < chunks - 1:
            grad_flat, token = basis_chunk(j, returned[j], grad_flat, done)
            done = [token]

    total = sum(inners[1:], inners[0])
    flip, at, blocks = 1, 0, widths[-1] // block
    while flip < devices:
        upto = -(-(at + blocks) // 2) if at == 0 else blocks
        before = total
        if flip * 2 < devices:
            a, b, c = (send(total, flip * k) for k in (1, 2, 3))
            total = (total + a) + (b + c)
            flip *= 4
        else:
            total = total + send(total, flip)
            flip *= 2
        if at < upto:
            grad_flat, _ = basis_chunk(-1, returned[-1], grad_flat, [before], at, upto)
            at = upto
    slope = 1.0 - jnp.tanh(coeff) ** 2
    grad_c = slope * total / math.sqrt(rank * width)
    return (grad_a, grad_flat.reshape(num_bases, rows, width), grad_c)


def solution(mesh):
    in_specs = (
        P(("layer", "expert"), None),
        P(("layer", "expert"), None),
        P("layer", "expert", None),
        P("layer", None),
    )
    out_specs = (P(("layer", "expert"), None), P("layer", "expert", None), P("layer", None))
    return jax.shard_map(
        per_device, mesh=mesh, in_specs=in_specs, out_specs=out_specs, check_vma=False
    )
```

time: 134 us -> 105 us (0.78)
  starting transfers between devices: 55.7 us -> 34.8 us
  local copies, waits for them, and re-layouts: 9.22 us -> 0.86 us
  Pallas kernels: 38.2 us -> 41.6 us
  waiting for transfers between devices: 27.4 us -> 25 us
    ppermute x50 -> x30, starting transfers between devices: 55.7 us -> 34.8 us  [send(): return lax.ppermute(x, 'expert', [(i, i ^ flip) for i in range(devices)])]
    unnamed x30 -> x6, local copies, waits for them, and re-layouts: 9.07 us -> 0.73 us
    pallas_call x25 -> x16, Pallas kernels: 38.2 us -> 41.6 us  [call(): pl.pallas_call(body, out_shape=[shape for shape, _ in outs], in_specs=[sp...]
    ppermute x50 -> x30, waiting for transfers between devices: 27.4 us -> 25 us  [send(): return lax.ppermute(x, 'expert', [(i, i ^ flip) for i in range(devices)])]
  transfers between devices with their start and end apart: 50 -> 30, of which waited for: 14 -> 9; matrix products, arithmetic and copies ran while one was open for 1% -> 2% of each run, Pallas kernels for 24% -> 30%
where the time goes in v2:
time: 105 us
  Pallas kernels  41.6 us (40%)
  starting transfers between devices  34.8 us (33%)
  waiting for transfers between devices  25 us (24%)
  matrix products  1.48 us (1%)
    pallas_call x16, Pallas kernels, call(): pl.pallas_call(body, out_shape=[shape for shape, _ in outs], in_specs=[sp...  41.6 us
    ppermute x30, starting transfers between devices, send(): return lax.ppermute(x, 'expert', [(i, i ^ flip) for i in range(devices)])  34.8 us
    ppermute x30, waiting for transfers between devices, send(): return lax.ppermute(x, 'expert', [(i, i ^ flip) for i in range(devices)])  25 us
  transfers between devices with their start and end apart: 30, of which 9 were waited for; matrix products, arithmetic and copies ran while one was open for 2% of the time, Pallas kernels for 30%

profile of v2, /device:TPU:0, one launch (start us, length us, event | category | flops | bytes accessed | tf_op | source)
XLA Modules:
  0.0 105.2 jit_solution(6537222816260043142)
XLA Ops:
  0.6 0.0 copy-start
  0.7 0.0 copy-start.1
  0.7 0.7 copy-done.1
  1.4 0.3 spread.1
  1.7 3.7 %mix.2 = (bf16[16,3584]{1,0:T(8,128)(2,1)S(1)}, bf16[16,3584]{1,0:T(8,128)(2,1)S(1)}, bf16[16,3584]{1,0:T(8,128)(2,1)S(1)}, bf16[16,3584]{1,0:T(8,128)(2,1)S(1)}) custom-call(bf16[64,1024]{1,0:T(8,128)(2,1)S(1)} %get-tuple-element.37.refs_0_, bf16[1024,7168]{1,0:T(8,128)(2,1)} %bitcast.7), custom_call_target="tpu_custom_call" | custom-call | tf_op jit(solution)/shard_map/mix/pallas_call | solution.py:215
  5.4 3.1 %collective-permute-start.3 = (bf16[16,3584]{1,0:T(8,128)(2,1)S(1)}, bf16[16,3584]{1,0:T(8,128)(2,1)S(1)}, u32[]{:S(2)}, u32[]{:S(2)}) collective-permute-start(bf16[16,3584]{1,0:T(8,128)(2,1)S(1)} %get-tuple-element.43), channel_id=1, source_target_pairs={{0,4},{1,5},{2,6},{3,7},{4,0},{5,1},{6,2},{7,3},{8,12},{9,13},{10,... | collective-permute-start | bytes 344072 | tf_op jit(solution)/shard_map/ppermute | solution.py:201
  8.5 2.6 %collective-permute-start.4 = (bf16[16,3584]{1,0:T(8,128)(2,1)S(1)}, bf16[16,3584]{1,0:T(8,128)(2,1)S(1)}, u32[]{:S(2)}, u32[]{:S(2)}) collective-permute-start(bf16[16,3584]{1,0:T(8,128)(2,1)S(1)} %get-tuple-element.44), channel_id=1, source_target_pairs={{0,8},{1,9},{2,10},{3,11},{4,12},{5,13},{6,14},{7,15},{8,0},{9,1},... | collective-permute-start | bytes 344072 | tf_op jit(solution)/shard_map/ppermute | solution.py:201
  11.1 0.0 collective-permute-start.5
  11.1 3.7 %mix.3 = (bf16[16,3584]{1,0:T(8,128)(2,1)S(1)}, bf16[16,3584]{1,0:T(8,128)(2,1)S(1)}, bf16[16,3584]{1,0:T(8,128)(2,1)S(1)}, bf16[16,3584]{1,0:T(8,128)(2,1)S(1)}) custom-call(bf16[64,1024]{1,0:T(8,128)(2,1)S(1)} %get-tuple-element.37.refs_0_, bf16[1024,7168]{1,0:T(8,128)(2,1)} %bitcast.8, bf16[16,3584]{1,0:T(8,128)(2,1)S(1)} %get-tuple-element.38.refs_2_.refs_0_), custom_call_target="tpu_custom_call" | custom-call | tf_op jit(solution)/shard_map/mix/pallas_call | solution.py:215
  14.8 5.4 %collective-permute-done.4.refs_2_ = bf16[16,3584]{1,0:T(8,128)(2,1)S(1)} collective-permute-done((bf16[16,3584]{1,0:T(8,128)(2,1)S(1)}, bf16[16,3584]{1,0:T(8,128)(2,1)S(1)}, u32[]{:S(2)}, u32[]{:S(2)}) %collective-permute-start.4) | collective-permute-done | bytes 114720 | tf_op jit(solution)/shard_map/ppermute | solution.py:201
  20.2 1.6 %collective-permute-start.9 = (bf16[64,3584]{1,0:T(8,128)(2,1)S(1)}, bf16[64,3584]{1,0:T(8,128)(2,1)S(1)}, u32[]{:S(2)}, u32[]{:S(2)}) collective-permute-start(bf16[64,3584]{1,0:T(8,128)(2,1)S(1)} %join.2.refs_4_.refs_3_), channel_id=1, source_target_pairs={{0,2},{1,3},{2,0},{3,1},{4,6},{5,7},{6,4},{7,5},{8,10},{9,11},{10,... | collective-permute-start | bytes 1376264 | tf_op jit(solution)/shard_map/ppermute | solution.py:201
  21.8 1.8 %collective-permute-start = (bf16[16,3584]{1,0:T(8,128)(2,1)S(1)}, bf16[16,3584]{1,0:T(8,128)(2,1)S(1)}, u32[]{:S(2)}, u32[]{:S(2)}) collective-permute-start(bf16[16,3584]{1,0:T(8,128)(2,1)S(1)} %get-tuple-element.40), channel_id=1, source_target_pairs={{0,4},{1,5},{2,6},{3,7},{4,0},{5,1},{6,2},{7,3},{8,12},{9,13},{10,... | collective-permute-start | bytes 344072 | tf_op jit(solution)/shard_map/ppermute | solution.py:201
  23.6 1.2 %collective-permute-start.1 = (bf16[16,3584]{1,0:T(8,128)(2,1)S(1)}, bf16[16,3584]{1,0:T(8,128)(2,1)S(1)}, u32[]{:S(2)}, u32[]{:S(2)}) collective-permute-start(bf16[16,3584]{1,0:T(8,128)(2,1)S(1)} %get-tuple-element.41), channel_id=1, source_target_pairs={{0,8},{1,9},{2,10},{3,11},{4,12},{5,13},{6,14},{7,15},{8,0},{9,1},... | collective-permute-start | bytes 344072 | tf_op jit(solution)/shard_map/ppermute | solution.py:201
  24.9 1.4 %collective-permute-start.2 = (bf16[16,3584]{1,0:T(8,128)(2,1)S(1)}, bf16[16,3584]{1,0:T(8,128)(2,1)S(1)}, u32[]{:S(2)}, u32[]{:S(2)}) collective-permute-start(bf16[16,3584]{1,0:T(8,128)(2,1)S(1)} %get-tuple-element.42), channel_id=1, source_target_pairs={{0,12},{1,13},{2,14},{3,15},{4,8},{5,9},{6,10},{7,11},{8,4},{9,5},... | collective-permute-start | bytes 344072 | tf_op jit(solution)/shard_map/ppermute | solution.py:201
  26.2 4.1 %collective-permute-done.9.refs_4_ = bf16[64,3584]{1,0:T(8,128)(2,1)S(1)} collective-permute-done((bf16[64,3584]{1,0:T(8,128)(2,1)S(1)}, bf16[64,3584]{1,0:T(8,128)(2,1)S(1)}, u32[]{:S(2)}, u32[]{:S(2)}) %collective-permute-start.9) | collective-permute-done | bytes 458784 | tf_op jit(solution)/shard_map/ppermute | solution.py:201
  30.3 0.0 collective-permute-done.refs_1_
  30.3 3.4 %collective-permute-done.1.refs_2_ = bf16[16,3584]{1,0:T(8,128)(2,1)S(1)} collective-permute-done((bf16[16,3584]{1,0:T(8,128)(2,1)S(1)}, bf16[16,3584]{1,0:T(8,128)(2,1)S(1)}, u32[]{:S(2)}, u32[]{:S(2)}) %collective-permute-start.1) | collective-permute-done | bytes 114720 | tf_op jit(solution)/shard_map/ppermute | solution.py:201
  33.7 0.6 collective-permute-start.6
  34.3 0.3 convolution_convert_fusion.refs_1_
  34.6 0.1 copy.10.refs_0_
  34.7 0.0 collective-permute-done.10.refs_5_
  34.8 6.7 %fit.2 = (f32[128,3584]{1,0:T(8,128)S(1)}, bf16[64,3584]{1,0:T(8,128)(2,1)S(1)}, bf16[64,3584]{1,0:T(8,128)(2,1)S(1)}, f32[512,256]{1,0:T(8,128)S(1)}) custom-call(bf16[512,256]{1,0:T(8,128)(2,1)S(1)} %copy.10.refs_0_, bf16[256,512]{1,0:T(8,128)(2,1)S(1)} %convolution_convert_fusion.refs_1_, bf16[512,7168]{1,0:T(8,128)(2,1)} %refs_2_.3, ...), custom_call_target="tpu_custom_call" | custom-call | tf_op jit(solution)/shard_map/fit/pallas_call | solution.py:215
  41.5 0.1 collective-permute-start.12
  41.6 0.5 collective-permute-start.13
  42.1 0.1 collective-permute-start.7
  42.1 1.2 %collective-permute-done.6.refs_4_ = bf16[64,3584]{1,0:T(8,128)(2,1)S(1)} collective-permute-done((bf16[64,3584]{1,0:T(8,128)(2,1)S(1)}, bf16[64,3584]{1,0:T(8,128)(2,1)S(1)}, u32[]{:S(2)}, u32[]{:S(2)}) %collective-permute-start.6) | collective-permute-done | bytes 458784 | tf_op jit(solution)/shard_map/ppermute | solution.py:201
  43.4 0.0 collective-permute-start.8
  43.4 0.0 collective-permute-done.12.refs_1_
  43.4 0.7 collective-permute-done.13.refs_2_
  44.0 0.6 chip_sum.2
  44.6 1.6 %collective-permute-start.14 = (bf16[64,3584]{1,0:T(8,128)(2,1)S(1)}, bf16[64,3584]{1,0:T(8,128)(2,1)S(1)}, u32[]{:S(2)}, u32[]{:S(2)}) collective-permute-start(bf16[64,3584]{1,0:T(8,128)(2,1)S(1)} %get-tuple-element.53), channel_id=1, source_target_pairs={{0,2},{1,3},{2,0},{3,1},{4,6},{5,7},{6,4},{7,5},{8,10},{9,11},{10,... | collective-permute-start | bytes 1376264 | tf_op jit(solution)/shard_map/ppermute | solution.py:201
  46.2 0.0 collective-permute-done.7.refs_5_
  46.2 0.0 collective-permute-done.8.refs_6_
  46.2 5.9 %fit.3 = (f32[128,3584]{1,0:T(8,128)S(1)}, bf16[64,3584]{1,0:T(8,128)(2,1)S(1)}, bf16[64,3584]{1,0:T(8,128)(2,1)S(1)}, f32[512,256]{1,0:T(8,128)S(1)}) custom-call(bf16[512,256]{1,0:T(8,128)(2,1)S(1)} %copy.10.refs_0_, bf16[256,512]{1,0:T(8,128)(2,1)S(1)} %convolution_convert_fusion.refs_1_, bf16[512,7168]{1,0:T(8,128)(2,1)} %refs_2_.3, ...), custom_call_target="tpu_custom_call" | custom-call | tf_op jit(solution)/shard_map/fit/pallas_call | solution.py:215
  52.1 0.1 collective-permute-start.18
  52.1 0.5 collective-permute-start.19
  52.6 4.6 %collective-permute-done.14.refs_1_ = bf16[64,3584]{1,0:T(8,128)(2,1)S(1)} collective-permute-done((bf16[64,3584]{1,0:T(8,128)(2,1)S(1)}, bf16[64,3584]{1,0:T(8,128)(2,1)S(1)}, u32[]{:S(2)}, u32[]{:S(2)}) %collective-permute-start.14) | collective-permute-done | bytes 458784 | tf_op jit(solution)/shard_map/ppermute | solution.py:201
  57.2 0.3 plane_sum.2
  57.6 0.0 collective-permute-done.18.refs_1_
  57.6 0.6 chip_sum.3
  58.2 1.6 %collective-permute-start.20 = (bf16[64,3584]{1,0:T(8,128)(2,1)S(1)}, bf16[64,3584]{1,0:T(8,128)(2,1)S(1)}, u32[]{:S(2)}, u32[]{:S(2)}) collective-permute-start(bf16[64,3584]{1,0:T(8,128)(2,1)S(1)} %get-tuple-element.62), channel_id=1, source_target_pairs={{0,2},{1,3},{2,0},{3,1},{4,6},{5,7},{6,4},{7,5},{8,10},{9,11},{10,... | collective-permute-start | bytes 1376264 | tf_op jit(solution)/shard_map/ppermute | solution.py:201
  59.8 2.5 %collective-permute-start.15 = (bf16[16,3584]{1,0:T(8,128)(2,1)S(1)}, bf16[16,3584]{1,0:T(8,128)(2,1)S(1)}, u32[]{:S(2)}, u32[]{:S(2)}) collective-permute-start(bf16[16,3584]{1,0:T(8,128)(2,1)S(1)} %get-tuple-element.56), channel_id=1, source_target_pairs={{0,4},{1,5},{2,6},{3,7},{4,0},{5,1},{6,2},{7,3},{8,12},{9,13},{10,... | collective-permute-start | bytes 344072 | tf_op jit(solution)/shard_map/ppermute | solution.py:201
  62.2 1.2 %convolution_multiply_fusion.refs_3_ = f32[512,256]{1,0:T(8,128)} fusion(f32[512,256]{1,0:T(8,128)S(1)} %get-tuple-element.51, s32[256]{0:T(256)S(1)} %fusion.6), kind=kOutput, calls=%fused_computation | convolution fusion | flops 402849792 | bytes 1049600 | tf_op jit(solution)/shard_map/dot_general | solution.py:410
  63.4 1.2 %collective-permute-start.16 = (bf16[16,3584]{1,0:T(8,128)(2,1)S(1)}, bf16[16,3584]{1,0:T(8,128)(2,1)S(1)}, u32[]{:S(2)}, u32[]{:S(2)}) collective-permute-start(bf16[16,3584]{1,0:T(8,128)(2,1)S(1)} %get-tuple-element.57), channel_id=1, source_target_pairs={{0,8},{1,9},{2,10},{3,11},{4,12},{5,13},{6,14},{7,15},{8,0},{9,1},... | collective-permute-start | bytes 344072 | tf_op jit(solution)/shard_map/ppermute | solution.py:201
  64.6 1.5 %collective-permute-start.17 = (bf16[16,3584]{1,0:T(8,128)(2,1)S(1)}, bf16[16,3584]{1,0:T(8,128)(2,1)S(1)}, u32[]{:S(2)}, u32[]{:S(2)}) collective-permute-start(bf16[16,3584]{1,0:T(8,128)(2,1)S(1)} %get-tuple-element.58), channel_id=1, source_target_pairs={{0,12},{1,13},{2,14},{3,15},{4,8},{5,9},{6,10},{7,11},{8,4},{9,5},... | collective-permute-start | bytes 344072 | tf_op jit(solution)/shard_map/ppermute | solution.py:201
  66.1 3.9 %collective-permute-done.20.refs_1_ = bf16[64,3584]{1,0:T(8,128)(2,1)S(1)} collective-permute-done((bf16[64,3584]{1,0:T(8,128)(2,1)S(1)}, bf16[64,3584]{1,0:T(8,128)(2,1)S(1)}, u32[]{:S(2)}, u32[]{:S(2)}) %collective-permute-start.20) | collective-permute-done | bytes 458784 | tf_op jit(solution)/shard_map/ppermute | solution.py:201
  70.0 0.3 plane_sum.3
  70.3 3.3 %collective-permute-start.21 = (bf16[16,3584]{1,0:T(8,128)(2,1)S(1)}, bf16[16,3584]{1,0:T(8,128)(2,1)S(1)}, u32[]{:S(2)}, u32[]{:S(2)}) collective-permute-start(bf16[16,3584]{1,0:T(8,128)(2,1)S(1)} %get-tuple-element.65), channel_id=1, source_target_pairs={{0,4},{1,5},{2,6},{3,7},{4,0},{5,1},{6,2},{7,3},{8,12},{9,13},{10,... | collective-permute-start | bytes 344072 | tf_op jit(solution)/shard_map/ppermute | solution.py:201
  73.6 2.0 %collective-permute-start.22 = (bf16[16,3584]{1,0:T(8,128)(2,1)S(1)}, bf16[16,3584]{1,0:T(8,128)(2,1)S(1)}, u32[]{:S(2)}, u32[]{:S(2)}) collective-permute-start(bf16[16,3584]{1,0:T(8,128)(2,1)S(1)} %get-tuple-element.66), channel_id=1, source_target_pairs={{0,8},{1,9},{2,10},{3,11},{4,12},{5,13},{6,14},{7,15},{8,0},{9,1},... | collective-permute-start | bytes 344072 | tf_op jit(solution)/shard_map/ppermute | solution.py:201
  75.6 1.4 %collective-permute-start.23 = (bf16[16,3584]{1,0:T(8,128)(2,1)S(1)}, bf16[16,3584]{1,0:T(8,128)(2,1)S(1)}, u32[]{:S(2)}, u32[]{:S(2)}) collective-permute-start(bf16[16,3584]{1,0:T(8,128)(2,1)S(1)} %get-tuple-element.67), channel_id=1, source_target_pairs={{0,12},{1,13},{2,14},{3,15},{4,8},{5,9},{6,10},{7,11},{8,4},{9,5},... | collective-permute-start | bytes 344072 | tf_op jit(solution)/shard_map/ppermute | solution.py:201
  77.0 5.0 %inner.2.refs_5_ = f32[4,64]{1,0:T(4,128)S(1)} custom-call(s32[1]{0:T(128)} %bitcast.1.refs_0_, bf16[1024,7168]{1,0:T(8,128)(2,1)} %bitcast.9, bf16[16,3584]{1,0:T(8,128)(2,1)S(1)} %get-tuple-element.55.refs_3_.refs_2_.refs_1_, bf16[16,3584]{1,0:T(8,128)(2,1)S(1)} %collective-permute-done.15.refs_3_.refs_2_, ...), custom_call_target="tpu_custom_call" | custom-call | tf_op jit(solution)/shard_map/inner/pallas_call | solution.py:215
  81.9 4.4 %basis.3 = (bf16[1024,7168]{1,0:T(8,128)(2,1)}, f32[8,128]{1,0:T(8,128)S(1)}) custom-call(bf16[1024,64]{1,0:T(8,128)(2,1)S(1)} %get-tuple-element.52.refs_0_, bf16[16,3584]{1,0:T(8,128)(2,1)S(1)} %get-tuple-element.55.refs_3_.refs_2_.refs_1_, bf16[16,3584]{1,0:T(8,128)(2,1)S(1)} %collective-permute-done.15.refs_3_.refs_2_, ...), custom_call_target="tpu_custom_call" | custom-call | tf_op jit(solution)/shard_map/basis/pallas_call | solution.py:215
  86.3 5.0 %inner.3 = f32[4,64]{1,0:T(4,128)S(1)} custom-call(s32[1]{0:T(128)} %bitcast.1.refs_0_, bf16[1024,7168]{1,0:T(8,128)(2,1)} %bitcast.10, bf16[16,3584]{1,0:T(8,128)(2,1)S(1)} %get-tuple-element.63.refs_6_.refs_2_, bf16[16,3584]{1,0:T(8,128)(2,1)S(1)} %collective-permute-done.21.refs_3_, bf16[16,3584]{1,0:T(8,128)(2,1)S(1)} %collective-permute-done.22.refs_4_, ...), custom_call_target="tpu_custom_call" | custom-call | tf_op jit(solution)/shard_map/inner/pallas_call | solution.py:215
  91.3 0.1 collective-permute-start.26
  91.4 0.6 collective-permute-start.25
  92.0 1.3 %collective-permute-start.24 = (f32[4,64]{1,0:T(4,128)S(1)}, f32[4,64]{1,0:T(4,128)S(1)}, u32[]{:S(2)}, u32[]{:S(2)}) collective-permute-start(f32[4,64]{1,0:T(4,128)S(1)} %add.90.refs_6_), channel_id=1, source_target_pairs={{0,1},{1,0},{2,3},{3,2},{4,5},{5,4},{6,7},{7,6},{8,9},{9,8},{10,11... | collective-permute-start | bytes 3080 | tf_op jit(solution)/shard_map/ppermute | solution.py:201
  93.3 1.1 %collective-permute-done.26 = f32[4,64]{1,0:T(4,128)S(1)} collective-permute-done((f32[4,64]{1,0:T(4,128)S(1)}, f32[4,64]{1,0:T(4,128)S(1)}, u32[]{:S(2)}, u32[]{:S(2)}) %collective-permute-start.26) | collective-permute-done | bytes 1056 | tf_op jit(solution)/shard_map/ppermute | solution.py:201
  94.4 0.7 collective-permute-done.25
  95.1 2.5 %collective-permute-start.29 = (f32[4,64]{1,0:T(4,128)S(1)}, f32[4,64]{1,0:T(4,128)S(1)}, u32[]{:S(2)}, u32[]{:S(2)}) collective-permute-start(f32[4,64]{1,0:T(4,128)S(1)} %add_add_fusion.refs_6_), channel_id=1, source_target_pairs={{0,12},{1,13},{2,14},{3,15},{4,8},{5,9},{6,10},{7,11},{8,4},{9,5},... | collective-permute-start | bytes 3080 | tf_op jit(solution)/shard_map/ppermute | solution.py:201
  97.6 0.5 collective-permute-start.28
  98.1 1.5 %collective-permute-start.27 = (f32[4,64]{1,0:T(4,128)S(1)}, f32[4,64]{1,0:T(4,128)S(1)}, u32[]{:S(2)}, u32[]{:S(2)}) collective-permute-start(f32[4,64]{1,0:T(4,128)S(1)} %add_add_fusion.refs_6_), channel_id=1, source_target_pairs={{0,4},{1,5},{2,6},{3,7},{4,0},{5,1},{6,2},{7,3},{8,12},{9,13},{10,... | collective-permute-start | bytes 3080 | tf_op jit(solution)/shard_map/ppermute | solution.py:201
  99.5 2.5 %basis.4 = (bf16[1024,7168]{1,0:T(8,128)(2,1)}, f32[8,128]{1,0:T(8,128)}) custom-call(bf16[1024,64]{1,0:T(8,128)(2,1)S(1)} %get-tuple-element.52.refs_0_, bf16[1024,7168]{1,0:T(8,128)(2,1)} %get-tuple-element.64.refs_1_, bf16[16,3584]{1,0:T(8,128)(2,1)S(1)} %get-tuple-element.63.refs_6_.refs_2_, ...), custom_call_target="tpu_custom_call", output_to_operand_aliasing={{0}: (1, {})} | custom-call | tf_op jit(solution)/shard_map/basis/pallas_call | solution.py:215
  102.1 2.5 %basis.5 = (bf16[1024,7168]{1,0:T(8,128)(2,1)}, f32[8,128]{1,0:T(8,128)}) custom-call(bf16[1024,64]{1,0:T(8,128)(2,1)S(1)} %get-tuple-element.52.refs_0_, bf16[1024,7168]{1,0:T(8,128)(2,1)} %get-tuple-element.69.refs_1_, bf16[16,3584]{1,0:T(8,128)(2,1)S(1)} %get-tuple-element.63.refs_6_.refs_2_, ...), custom_call_target="tpu_custom_call", output_to_operand_aliasing={{0}: (1, {})} | custom-call | tf_op jit(solution)/shard_map/basis/pallas_call | solution.py:215
  104.6 0.6 multiply_multiply_fusion
  (25 shorter events, 0.1 us)
Async XLA Ops:
  0.6 33.7 %copy-start = (bf16[512,256]{1,0:T(8,128)(2,1)S(1)}, bf16[512,256]{1,0:T(8,128)(2,1)}, u32[]{:S(2)}) copy-start(bf16[512,256]{1,0:T(8,128)(2,1)} %param.5) | copy-start | bytes 786436
  0.7 0.7 copy-start.1
  5.4 9.4 %collective-permute-start.3 = (bf16[16,3584]{1,0:T(8,128)(2,1)S(1)}, bf16[16,3584]{1,0:T(8,128)(2,1)S(1)}, u32[]{:S(2)}, u32[]{:S(2)}) collective-permute-start(bf16[16,3584]{1,0:T(8,128)(2,1)S(1)} %get-tuple-element.43), channel_id=1, source_target_pairs={{0,4},{1,5},{2,6},{3,7},{4,0},{5,1},{6,2},{7,3},{8,12},{9,13},{10,... | collective-permute-start | bytes 344072 | tf_op jit(solution)/shard_map/ppermute | solution.py:201
  8.5 11.7 %collective-permute-start.4 = (bf16[16,3584]{1,0:T(8,128)(2,1)S(1)}, bf16[16,3584]{1,0:T(8,128)(2,1)S(1)}, u32[]{:S(2)}, u32[]{:S(2)}) collective-permute-start(bf16[16,3584]{1,0:T(8,128)(2,1)S(1)} %get-tuple-element.44), channel_id=1, source_target_pairs={{0,8},{1,9},{2,10},{3,11},{4,12},{5,13},{6,14},{7,15},{8,0},{9,1},... | collective-permute-start | bytes 344072 | tf_op jit(solution)/shard_map/ppermute | solution.py:201
  11.1 9.1 %collective-permute-start.5 = (bf16[16,3584]{1,0:T(8,128)(2,1)S(1)}, bf16[16,3584]{1,0:T(8,128)(2,1)S(1)}, u32[]{:S(2)}, u32[]{:S(2)}) collective-permute-start(bf16[16,3584]{1,0:T(8,128)(2,1)S(1)} %get-tuple-element.45), channel_id=1, source_target_pairs={{0,12},{1,13},{2,14},{3,15},{4,8},{5,9},{6,10},{7,11},{8,4},{9,5},... | collective-permute-start | bytes 344072 | tf_op jit(solution)/shard_map/ppermute | solution.py:201
  20.2 10.1 %collective-permute-start.9 = (bf16[64,3584]{1,0:T(8,128)(2,1)S(1)}, bf16[64,3584]{1,0:T(8,128)(2,1)S(1)}, u32[]{:S(2)}, u32[]{:S(2)}) collective-permute-start(bf16[64,3584]{1,0:T(8,128)(2,1)S(1)} %join.2.refs_4_.refs_3_), channel_id=1, source_target_pairs={{0,2},{1,3},{2,0},{3,1},{4,6},{5,7},{6,4},{7,5},{8,10},{9,11},{10,... | collective-permute-start | bytes 1376264 | tf_op jit(solution)/shard_map/ppermute | solution.py:201
  21.8 8.5 %collective-permute-start = (bf16[16,3584]{1,0:T(8,128)(2,1)S(1)}, bf16[16,3584]{1,0:T(8,128)(2,1)S(1)}, u32[]{:S(2)}, u32[]{:S(2)}) collective-permute-start(bf16[16,3584]{1,0:T(8,128)(2,1)S(1)} %get-tuple-element.40), channel_id=1, source_target_pairs={{0,4},{1,5},{2,6},{3,7},{4,0},{5,1},{6,2},{7,3},{8,12},{9,13},{10,... | collective-permute-start | bytes 344072 | tf_op jit(solution)/shard_map/ppermute | solution.py:201
  23.6 10.1 %collective-permute-start.1 = (bf16[16,3584]{1,0:T(8,128)(2,1)S(1)}, bf16[16,3584]{1,0:T(8,128)(2,1)S(1)}, u32[]{:S(2)}, u32[]{:S(2)}) collective-permute-start(bf16[16,3584]{1,0:T(8,128)(2,1)S(1)} %get-tuple-element.41), channel_id=1, source_target_pairs={{0,8},{1,9},{2,10},{3,11},{4,12},{5,13},{6,14},{7,15},{8,0},{9,1},... | collective-permute-start | bytes 344072 | tf_op jit(solution)/shard_map/ppermute | solution.py:201
  24.9 8.8 %collective-permute-start.2 = (bf16[16,3584]{1,0:T(8,128)(2,1)S(1)}, bf16[16,3584]{1,0:T(8,128)(2,1)S(1)}, u32[]{:S(2)}, u32[]{:S(2)}) collective-permute-start(bf16[16,3584]{1,0:T(8,128)(2,1)S(1)} %get-tuple-element.42), channel_id=1, source_target_pairs={{0,12},{1,13},{2,14},{3,15},{4,8},{5,9},{6,10},{7,11},{8,4},{9,5},... | collective-permute-start | bytes 344072 | tf_op jit(solution)/shard_map/ppermute | solution.py:201
  26.2 8.5 %collective-permute-start.10 = (bf16[64,3584]{1,0:T(8,128)(2,1)S(1)}, bf16[64,3584]{1,0:T(8,128)(2,1)S(1)}, u32[]{:S(2)}, u32[]{:S(2)}) collective-permute-start(bf16[64,3584]{1,0:T(8,128)(2,1)S(1)} %join.2.refs_4_.refs_3_), channel_id=1, source_target_pairs={{0,1},{1,0},{2,3},{3,2},{4,5},{5,4},{6,7},{7,6},{8,9},{9,8},{10,11... | collective-permute-start | bytes 1376264 | tf_op jit(solution)/shard_map/ppermute | solution.py:201
  30.3 4.4 %collective-permute-start.11 = (bf16[64,3584]{1,0:T(8,128)(2,1)S(1)}, bf16[64,3584]{1,0:T(8,128)(2,1)}, u32[]{:S(2)}, u32[]{:S(2)}) collective-permute-start(bf16[64,3584]{1,0:T(8,128)(2,1)S(1)} %collective-permute-done.9.refs_4_), channel_id=1, source_target_pairs={{0,1},{1,0},{2,3},{3,2},{4,5},{5,4},{6,7},{7,6},{8,9},{9,8},{10,11... | collective-permute-start | bytes 1376264 | tf_op jit(solution)/shard_map/ppermute | solution.py:201
  33.7 9.6 %collective-permute-start.6 = (bf16[64,3584]{1,0:T(8,128)(2,1)S(1)}, bf16[64,3584]{1,0:T(8,128)(2,1)S(1)}, u32[]{:S(2)}, u32[]{:S(2)}) collective-permute-start(bf16[64,3584]{1,0:T(8,128)(2,1)S(1)} %join.3.refs_7_.refs_3_), channel_id=1, source_target_pairs={{0,2},{1,3},{2,0},{3,1},{4,6},{5,7},{6,4},{7,5},{8,10},{9,11},{10,... | collective-permute-start | bytes 1376264 | tf_op jit(solution)/shard_map/ppermute | solution.py:201
  41.5 1.9 %collective-permute-start.12 = (bf16[64,3584]{1,0:T(8,128)(2,1)S(1)}, bf16[64,3584]{1,0:T(8,128)(2,1)S(1)}, u32[]{:S(2)}, u32[]{:S(2)}) collective-permute-start(bf16[64,3584]{1,0:T(8,128)(2,1)S(1)} %get-tuple-element.48), channel_id=1, source_target_pairs={{0,1},{1,0},{2,3},{3,2},{4,5},{5,4},{6,7},{7,6},{8,9},{9,8},{10,11... | collective-permute-start | bytes 1376264 | tf_op jit(solution)/shard_map/ppermute | solution.py:201
  41.6 2.5 %collective-permute-start.13 = (bf16[64,3584]{1,0:T(8,128)(2,1)S(1)}, bf16[64,3584]{1,0:T(8,128)(2,1)S(1)}, u32[]{:S(2)}, u32[]{:S(2)}) collective-permute-start(bf16[64,3584]{1,0:T(8,128)(2,1)S(1)} %get-tuple-element.49), channel_id=1, source_target_pairs={{0,1},{1,0},{2,3},{3,2},{4,5},{5,4},{6,7},{7,6},{8,9},{9,8},{10,11... | collective-permute-start | bytes 1376264 | tf_op jit(solution)/shard_map/ppermute | solution.py:201
  42.1 4.1 %collective-permute-start.7 = (bf16[64,3584]{1,0:T(8,128)(2,1)S(1)}, bf16[64,3584]{1,0:T(8,128)(2,1)S(1)}, u32[]{:S(2)}, u32[]{:S(2)}) collective-permute-start(bf16[64,3584]{1,0:T(8,128)(2,1)S(1)} %join.3.refs_7_.refs_3_), channel_id=1, source_target_pairs={{0,1},{1,0},{2,3},{3,2},{4,5},{5,4},{6,7},{7,6},{8,9},{9,8},{10,11... | collective-permute-start | bytes 1376264 | tf_op jit(solution)/shard_map/ppermute | solution.py:201
  43.4 2.8 %collective-permute-start.8 = (bf16[64,3584]{1,0:T(8,128)(2,1)S(1)}, bf16[64,3584]{1,0:T(8,128)(2,1)S(1)}, u32[]{:S(2)}, u32[]{:S(2)}) collective-permute-start(bf16[64,3584]{1,0:T(8,128)(2,1)S(1)} %collective-permute-done.6.refs_4_), channel_id=1, source_target_pairs={{0,1},{1,0},{2,3},{3,2},{4,5},{5,4},{6,7},{7,6},{8,9},{9,8},{10,11... | collective-permute-start | bytes 1376264 | tf_op jit(solution)/shard_map/ppermute | solution.py:201
  44.6 12.6 %collective-permute-start.14 = (bf16[64,3584]{1,0:T(8,128)(2,1)S(1)}, bf16[64,3584]{1,0:T(8,128)(2,1)S(1)}, u32[]{:S(2)}, u32[]{:S(2)}) collective-permute-start(bf16[64,3584]{1,0:T(8,128)(2,1)S(1)} %get-tuple-element.53), channel_id=1, source_target_pairs={{0,2},{1,3},{2,0},{3,1},{4,6},{5,7},{6,4},{7,5},{8,10},{9,11},{10,... | collective-permute-start | bytes 1376264 | tf_op jit(solution)/shard_map/ppermute | solution.py:201
  52.1 5.5 %collective-permute-start.18 = (bf16[64,3584]{1,0:T(8,128)(2,1)S(1)}, bf16[64,3584]{1,0:T(8,128)(2,1)S(1)}, u32[]{:S(2)}, u32[]{:S(2)}) collective-permute-start(bf16[64,3584]{1,0:T(8,128)(2,1)S(1)} %get-tuple-element.59), channel_id=1, source_target_pairs={{0,1},{1,0},{2,3},{3,2},{4,5},{5,4},{6,7},{7,6},{8,9},{9,8},{10,11... | collective-permute-start | bytes 1376264 | tf_op jit(solution)/shard_map/ppermute | solution.py:201
  52.1 5.4 %collective-permute-start.19 = (bf16[64,3584]{1,0:T(8,128)(2,1)S(1)}, bf16[64,3584]{1,0:T(8,128)(2,1)S(1)}, u32[]{:S(2)}, u32[]{:S(2)}) collective-permute-start(bf16[64,3584]{1,0:T(8,128)(2,1)S(1)} %get-tuple-element.60), channel_id=1, source_target_pairs={{0,1},{1,0},{2,3},{3,2},{4,5},{5,4},{6,7},{7,6},{8,9},{9,8},{10,11... | collective-permute-start | bytes 1376264 | tf_op jit(solution)/shard_map/ppermute | solution.py:201
  58.2 11.8 %collective-permute-start.20 = (bf16[64,3584]{1,0:T(8,128)(2,1)S(1)}, bf16[64,3584]{1,0:T(8,128)(2,1)S(1)}, u32[]{:S(2)}, u32[]{:S(2)}) collective-permute-start(bf16[64,3584]{1,0:T(8,128)(2,1)S(1)} %get-tuple-element.62), channel_id=1, source_target_pairs={{0,2},{1,3},{2,0},{3,1},{4,6},{5,7},{6,4},{7,5},{8,10},{9,11},{10,... | collective-permute-start | bytes 1376264 | tf_op jit(solution)/shard_map/ppermute | solution.py:201
  59.8 15.8 %collective-permute-start.15 = (bf16[16,3584]{1,0:T(8,128)(2,1)S(1)}, bf16[16,3584]{1,0:T(8,128)(2,1)S(1)}, u32[]{:S(2)}, u32[]{:S(2)}) collective-permute-start(bf16[16,3584]{1,0:T(8,128)(2,1)S(1)} %get-tuple-element.56), channel_id=1, source_target_pairs={{0,4},{1,5},{2,6},{3,7},{4,0},{5,1},{6,2},{7,3},{8,12},{9,13},{10,... | collective-permute-start | bytes 344072 | tf_op jit(solution)/shard_map/ppermute | solution.py:201
  63.4 13.5 %collective-permute-start.16 = (bf16[16,3584]{1,0:T(8,128)(2,1)S(1)}, bf16[16,3584]{1,0:T(8,128)(2,1)S(1)}, u32[]{:S(2)}, u32[]{:S(2)}) collective-permute-start(bf16[16,3584]{1,0:T(8,128)(2,1)S(1)} %get-tuple-element.57), channel_id=1, source_target_pairs={{0,8},{1,9},{2,10},{3,11},{4,12},{5,13},{6,14},{7,15},{8,0},{9,1},... | collective-permute-start | bytes 344072 | tf_op jit(solution)/shard_map/ppermute | solution.py:201
  64.6 12.3 %collective-permute-start.17 = (bf16[16,3584]{1,0:T(8,128)(2,1)S(1)}, bf16[16,3584]{1,0:T(8,128)(2,1)S(1)}, u32[]{:S(2)}, u32[]{:S(2)}) collective-permute-start(bf16[16,3584]{1,0:T(8,128)(2,1)S(1)} %get-tuple-element.58), channel_id=1, source_target_pairs={{0,12},{1,13},{2,14},{3,15},{4,8},{5,9},{6,10},{7,11},{8,4},{9,5},... | collective-permute-start | bytes 344072 | tf_op jit(solution)/shard_map/ppermute | solution.py:201
  70.3 16.0 %collective-permute-start.21 = (bf16[16,3584]{1,0:T(8,128)(2,1)S(1)}, bf16[16,3584]{1,0:T(8,128)(2,1)S(1)}, u32[]{:S(2)}, u32[]{:S(2)}) collective-permute-start(bf16[16,3584]{1,0:T(8,128)(2,1)S(1)} %get-tuple-element.65), channel_id=1, source_target_pairs={{0,4},{1,5},{2,6},{3,7},{4,0},{5,1},{6,2},{7,3},{8,12},{9,13},{10,... | collective-permute-start | bytes 344072 | tf_op jit(solution)/shard_map/ppermute | solution.py:201
  73.6 12.8 %collective-permute-start.22 = (bf16[16,3584]{1,0:T(8,128)(2,1)S(1)}, bf16[16,3584]{1,0:T(8,128)(2,1)S(1)}, u32[]{:S(2)}, u32[]{:S(2)}) collective-permute-start(bf16[16,3584]{1,0:T(8,128)(2,1)S(1)} %get-tuple-element.66), channel_id=1, source_target_pairs={{0,8},{1,9},{2,10},{3,11},{4,12},{5,13},{6,14},{7,15},{8,0},{9,1},... | collective-permute-start | bytes 344072 | tf_op jit(solution)/shard_map/ppermute | solution.py:201
  75.6 10.8 %collective-permute-start.23 = (bf16[16,3584]{1,0:T(8,128)(2,1)S(1)}, bf16[16,3584]{1,0:T(8,128)(2,1)S(1)}, u32[]{:S(2)}, u32[]{:S(2)}) collective-permute-start(bf16[16,3584]{1,0:T(8,128)(2,1)S(1)} %get-tuple-element.67), channel_id=1, source_target_pairs={{0,12},{1,13},{2,14},{3,15},{4,8},{5,9},{6,10},{7,11},{8,4},{9,5},... | collective-permute-start | bytes 344072 | tf_op jit(solution)/shard_map/ppermute | solution.py:201
  91.3 3.1 %collective-permute-start.26 = (f32[4,64]{1,0:T(4,128)S(1)}, f32[4,64]{1,0:T(4,128)S(1)}, u32[]{:S(2)}, u32[]{:S(2)}) collective-permute-start(f32[4,64]{1,0:T(4,128)S(1)} %add.90.refs_6_), channel_id=1, source_target_pairs={{0,3},{1,2},{2,1},{3,0},{4,7},{5,6},{6,5},{7,4},{8,11},{9,10},{10,... | collective-permute-start | bytes 3080 | tf_op jit(solution)/shard_map/ppermute | solution.py:201
  91.4 3.7 %collective-permute-start.25 = (f32[4,64]{1,0:T(4,128)S(1)}, f32[4,64]{1,0:T(4,128)S(1)}, u32[]{:S(2)}, u32[]{:S(2)}) collective-permute-start(f32[4,64]{1,0:T(4,128)S(1)} %add.90.refs_6_), channel_id=1, source_target_pairs={{0,2},{1,3},{2,0},{3,1},{4,6},{5,7},{6,4},{7,5},{8,10},{9,11},{10,... | collective-permute-start | bytes 3080 | tf_op jit(solution)/shard_map/ppermute | solution.py:201
  92.0 3.1 %collective-permute-start.24 = (f32[4,64]{1,0:T(4,128)S(1)}, f32[4,64]{1,0:T(4,128)S(1)}, u32[]{:S(2)}, u32[]{:S(2)}) collective-permute-start(f32[4,64]{1,0:T(4,128)S(1)} %add.90.refs_6_), channel_id=1, source_target_pairs={{0,1},{1,0},{2,3},{3,2},{4,5},{5,4},{6,7},{7,6},{8,9},{9,8},{10,11... | collective-permute-start | bytes 3080 | tf_op jit(solution)/shard_map/ppermute | solution.py:201
  95.1 9.5 %collective-permute-start.29 = (f32[4,64]{1,0:T(4,128)S(1)}, f32[4,64]{1,0:T(4,128)S(1)}, u32[]{:S(2)}, u32[]{:S(2)}) collective-permute-start(f32[4,64]{1,0:T(4,128)S(1)} %add_add_fusion.refs_6_), channel_id=1, source_target_pairs={{0,12},{1,13},{2,14},{3,15},{4,8},{5,9},{6,10},{7,11},{8,4},{9,5},... | collective-permute-start | bytes 3080 | tf_op jit(solution)/shard_map/ppermute | solution.py:201
  97.6 7.0 %collective-permute-start.28 = (f32[4,64]{1,0:T(4,128)S(1)}, f32[4,64]{1,0:T(4,128)S(1)}, u32[]{:S(2)}, u32[]{:S(2)}) collective-permute-start(f32[4,64]{1,0:T(4,128)S(1)} %add_add_fusion.refs_6_), channel_id=1, source_target_pairs={{0,8},{1,9},{2,10},{3,11},{4,12},{5,13},{6,14},{7,15},{8,0},{9,1},... | collective-permute-start | bytes 3080 | tf_op jit(solution)/shard_map/ppermute | solution.py:201
  98.1 6.6 %collective-permute-start.27 = (f32[4,64]{1,0:T(4,128)S(1)}, f32[4,64]{1,0:T(4,128)S(1)}, u32[]{:S(2)}, u32[]{:S(2)}) collective-permute-start(f32[4,64]{1,0:T(4,128)S(1)} %add_add_fusion.refs_6_), channel_id=1, source_target_pairs={{0,4},{1,5},{2,6},{3,7},{4,0},{5,1},{6,2},{7,3},{8,12},{9,13},{10,... | collective-permute-start | bytes 3080 | tf_op jit(solution)/shard_map/ppermute | solution.py:201
  99.5 5.1 %copy-start.2 = (f32[4,64]{1,0:T(4,128)S(1)}, f32[4,64]{1,0:T(4,128)}, u32[]{:S(2)}) copy-start(f32[4,64]{1,0:T(4,128)} %refs_1_.1) | copy-start | bytes 3076

commit v3 on v2

--- a/solution.py
+++ b/solution.py
@@ -12,18 +12,35 @@
 HIGHEST = lax.Precision.HIGHEST
 SHARES = (1, 1)
 LAG = 1
-FAR = 2
+FAR = (2, 4)
+FB = (0, 1)
+Z_ORDER = (3, 2, 1)
+P_ORDER = (1, 2, 3)
+FETCH_COST = 1
 FLOPS = 0
-VMEM_LIMIT = 24 * 2**20
+VMEM_LIMIT = 14 * 2**20
 
 
 def iota(shape, dim):
     return lax.broadcasted_iota(jnp.int32, shape, dim)
 
 
-def spread_kernel(rows, scale, place_ref, coeff_ref, spread_ref, spread_t_ref):
+def far_first(count):
+    order = [k + j for k in range(0, count, 4) for j in (*Z_ORDER, 0)]
+    return [k for k in order if k < count]
+
+
+def by_place(refs):
+    order = far_first(len(refs))
+    return [refs[order.index(k)] for k in range(len(refs))]
+
+
+def spread_kernel(rows, scale, inner_scale, place_ref, coeff_ref, *refs):
+    spread_ref, spread_t_ref, slope_ref = refs
     experts, bases = coeff_ref.shape
-    mix = jnp.tanh(coeff_ref[...]).astype(BF16).astype(F32)
+    mix = jnp.tanh(coeff_ref[...])
+    slope_ref[...] = (1.0 - mix * mix) * inner_scale
+    mix = mix.astype(BF16).astype(F32)
     place = place_ref[0]
     tall = experts * rows
     wide = bases * rows
@@ -60,6 +77,23 @@
     return held_ref[step]
 
 
+def fetch_kernel(start, source_ref, held_ref, token_ref, sems):
+    block = held_ref.shape[2]
+    copies = [
+        pltpu.make_async_copy(
+            source_ref.at[:, start + at * block : start + (at + 1) * block],
+            held_ref.at[at],
+            sems.at[at],
+        )
+        for at in range(held_ref.shape[0])
+    ]
+    for copy in copies:
+        copy.start()
+    token_ref[...] = jnp.zeros_like(token_ref)
+    for copy in copies:
+        copy.wait()
+
+
 def mix_kernel(start, spread_ref, bases_ref, *refs):
     *out_refs, held_ref, sems = refs
     held = streamed(start, bases_ref, held_ref, sems)
@@ -72,7 +106,7 @@
 def join_kernel(*refs):
     *part_refs, out_ref = refs
     rows = part_refs[0].shape[0]
-    for j, part_ref in enumerate(part_refs):
+    for j, part_ref in enumerate(by_place(part_refs)):
         out_ref[j * rows : (j + 1) * rows, :] = part_ref[...]
 
 
@@ -126,9 +160,13 @@
 
 
 def inner_kernel(rows, experts, start, place_ref, bases_ref, *refs):
-    *sum_refs, inner_ref, acc_ref, held_ref, sems = refs
-    held = streamed(start, bases_ref, held_ref, sems)
-    summed = jnp.concatenate([ref[...] for ref in sum_refs], axis=0)
+    if start is None:
+        *sum_refs, inner_ref, acc_ref = refs
+        held = bases_ref[0]
+    else:
+        *sum_refs, inner_ref, acc_ref, held_ref, sems = refs
+        held = streamed(start, bases_ref, held_ref, sems)
+    summed = jnp.concatenate([ref[...] for ref in by_place(sum_refs)], axis=0)
     step = lax.dot_general(
         summed, held, (((1,), (1,)), ((), ())), preferred_element_type=F32
     )
@@ -159,11 +197,22 @@
 def basis_kernel(scale, skip, spread_t_ref, *refs):
     *sum_refs, out_ref, token_ref = refs[skip:]
     token_ref[...] = jnp.zeros_like(token_ref)
-    summed = jnp.concatenate([ref[...] for ref in sum_refs], axis=0)
+    summed = jnp.concatenate([ref[...] for ref in by_place(sum_refs)], axis=0)
     grad = jnp.dot(spread_t_ref[...], summed, preferred_element_type=F32)
     if scale != 1.0:
         grad = grad * scale
     out_ref[...] = grad.astype(BF16)
+
+
+def add_kernel(turns, scaled, *refs):
+    *part_refs, out_ref = refs
+    if scaled:
+        *part_refs, slope_ref = part_refs
+    part = {turn: ref[...] for turn, ref in zip((*turns, 0), part_refs)}
+    total = part[0] + part[1]
+    if len(turns) == 3:
+        total = total + (part[2] + part[3])
+    out_ref[...] = total * slope_ref[...] if scaled else total
 
 
 def whole_spec(shape):
@@ -200,6 +249,10 @@
     def send(x, flip):
         return lax.ppermute(x, "expert", [(i, i ^ flip) for i in range(devices)])
 
+    def send_places(parts):
+        sent = {k: send(parts[k], k * group) for k in far_first(experts) if k}
+        return [parts[0]] + [sent[k] for k in range(1, experts)]
+
     def pieces_of(x):
         return [x[j * rows : (j + 1) * rows] for j in range(experts)]
 
@@ -219,7 +272,7 @@
             out_specs=[spec for _, spec in outs],
             compiler_params=pltpu.CompilerParams(vmem_limit_bytes=VMEM_LIMIT),
             cost_estimate=pl.CostEstimate(
-                flops=FLOPS * flops, bytes_accessed=FLOPS * bytes_accessed, transcendentals=0
+                flops=flops, bytes_accessed=bytes_accessed, transcendentals=0
             ),
             input_output_aliases=alias or {},
             name=name,
@@ -240,11 +293,17 @@
     flat = bases.reshape(wide, width)
     root = math.isqrt(experts)
     exact = root * root == experts and root & (root - 1) == 0
-    spread, spread_t = call(
-        functools.partial(spread_kernel, rows, 1.0 / root if exact else 1.0),
+    spread, spread_t, slope = call(
+        functools.partial(
+            spread_kernel, rows, 1.0 / root if exact else 1.0, 1.0 / math.sqrt(rank * width)
+        ),
         "spread",
         [(place, smem), (coeff, vmem)],
-        [(shape(tall, wide), vmem), (shape(wide, tall), vmem)],
+        [
+            (shape(tall, wide), vmem),
+            (shape(wide, tall), vmem),
+            (shape(experts, num_bases, dtype=F32), vmem),
+        ],
     )
     late_scale = 1.0 if exact else 1.0 / math.sqrt(experts)
 
@@ -267,8 +326,8 @@
             [(shape(tall // count, widths[j]), col(tall // count))] * count,
             (widths[j] // block,),
             after,
-            2 * tall * wide * widths[j] * 4,
-            2 * wide * widths[j],
+            FLOPS * 2 * tall * wide * widths[j],
+            FLOPS * 2 * wide * widths[j],
             scratch_shapes=held(j, wide),
         )
         return list(outs) if split else pieces_of(outs[0])
@@ -279,10 +338,25 @@
         return call(
             join_kernel,
             "join",
-            [(part, vmem) for part in parts],
+            [(parts[k], vmem) for k in far_first(experts)],
             [(shape(tall, widths[j]), vmem)],
             after=after,
         )[0]
+
+    def far_parts(j):
+        return FAR[min(j, len(FAR) - 1)]
+
+    def fetch(j, source, after):
+        steps, rows_in = widths[j] // block, source.shape[0]
+        return call(
+            functools.partial(fetch_kernel, starts[j]),
+            "fetch",
+            [(source, hbm)],
+            [(shape(steps, rows_in, block), vmem), (shape(8, 128, dtype=F32), vmem)],
+            after=after,
+            bytes_accessed=FETCH_COST * 4 * rows_in * widths[j],
+            scratch_shapes=[pltpu.SemaphoreType.DMA((steps,))],
+        )
 
     def fit_chunk(j, parts, before, after):
         first = before is None
@@ -300,13 +374,13 @@
             ],
             [
                 (shape(half, widths[j], dtype=F32), col(half)),
-                *[(shape(half // FAR, widths[j]), col(half // FAR))] * FAR,
+                *[(shape(half // far_parts(j), widths[j]), col(half // far_parts(j)))] * far_parts(j),
                 (shape(ff, rank, dtype=F32), whole_spec((ff, rank))),
             ],
             (widths[j] // block,),
             after,
-            6 * ff * rank * widths[j],
-            2 * ff * widths[j],
+            FLOPS * 6 * ff * rank * widths[j],
+            FLOPS * 2 * ff * widths[j],
             scratch_shapes=held(j, ff),
         )
 
@@ -315,15 +389,15 @@
         return call(
             chip_sum_kernel,
             "chip_sum",
-            [(near, col(2 * half)), *[(part, col(2 * half // FAR)) for part in got]],
+            [(near, col(2 * half)), *[(part, col(2 * half // len(got))) for part in got]],
             [
                 (shape(half, widths[j], dtype=F32), col(half)),
                 (shape(half, widths[j]), col(half)),
             ],
             (widths[j] // block,),
             after,
-            2 * half * widths[j],
-            16 * half * widths[j],
+            FLOPS * 2 * half * widths[j],
+            FLOPS * 16 * half * widths[j],
         )
 
     def plane_sum(j, keep, got, after):
@@ -335,26 +409,33 @@
             [(shape(tall // count, widths[j]), col(tall // count))] * count,
             (widths[j] // block,),
             after,
-            tall * widths[j],
-            8 * tall * widths[j],
+            FLOPS * tall * widths[j],
+            FLOPS * 8 * tall * widths[j],
         )
         return list(outs) if split else pieces_of(outs[0])
 
     def sums_of(sums):
         sums = sums if split else [jnp.concatenate(sums, axis=0)]
-        return [(part, col(tall // len(sums))) for part in sums]
-
-    def inner_chunk(j, sums, after):
+        return [(sums[k], col(tall // len(sums))) for k in far_first(len(sums))]
+
+    def inner_chunk(j, sums, after, fetched=None):
+        there = fetched is not None
         return call(
-            functools.partial(inner_kernel, rows, experts, starts[j]),
+            functools.partial(inner_kernel, rows, experts, None if there else starts[j]),
             "inner",
-            [(place, smem), (flat, hbm), *sums_of(sums)],
+            [
+                (place, smem),
+                (fetched, pl.BlockSpec((1, wide, block), lambda s: (s, 0, 0)))
+                if there
+                else (flat, hbm),
+                *sums_of(sums),
+            ],
             [(shape(experts, num_bases, dtype=F32), whole_spec((experts, num_bases)))],
             (widths[j] // block,),
             after,
-            2 * tall * wide * widths[j] * 4,
-            2 * wide * widths[j],
-            scratch_shapes=[pltpu.VMEM((tall, wide), F32), *held(j, wide)],
+            FLOPS * 2 * tall * wide * widths[j],
+            FLOPS * 2 * wide * widths[j],
+            scratch_shapes=[pltpu.VMEM((tall, wide), F32), *([] if there else held(j, wide))],
         )[0]
 
     def basis_chunk(j, sums, before, after, first=0, last=None):
@@ -375,8 +456,8 @@
             ],
             (last - first,),
             after,
-            2 * tall * wide * size * 4,
-            2 * wide * size,
+            FLOPS * 2 * tall * wide * size,
+            FLOPS * 2 * wide * size,
             alias={1: 0} if extra else None,
         )
 
@@ -386,27 +467,30 @@
     done = [mixes[-1][0]]
     for j in range(chunks):
         mixed = mixes[j]
-        got = [mixed[0]] + [send(mixed[k], k * group) for k in range(1, experts)]
+        got = send_places(mixed)
         own = join(j, got, done)
         done = [own]
         row = send(own, 2)
         gathered.append((own, row, send(own, 1), send(row, 1)))
-    grad_local, kept = None, {}
+    grad_local, kept, at_hand = None, {}, {}
 
     def return_plane(j, after):
+        if split and j in FB:
+            at_hand[j], token = fetch(j, flat, after)
+            after = [token]
         keep, away = kept.pop(j)
         sums = plane_sum(j, keep, away, after)
-        returned.append([sums[0]] + [send(sums[k], k * group) for k in range(1, experts)])
+        returned.append(send_places(sums))
         return [sums[0]]
 
     for j in range(chunks):
         near, *far, grad_local = fit_chunk(j, gathered[j], grad_local, done)
         done = [near]
-        if j >= LAG:
-            done = return_plane(j - LAG, done)
         keep, away = chip_sum(j, near, [send(part, 1) for part in far], done)
         kept[j] = keep, send(away, 2)
         done = [keep]
+        if j >= LAG:
+            done = return_plane(j - LAG, done)
     grad_a = jnp.dot(
         grad_local, order.astype(F32).T, precision=HIGHEST, preferred_element_type=F32
     ) / math.sqrt(width)
@@ -414,7 +498,7 @@
         done = return_plane(j, done + [pinned(grad_a, hbm)])
     grad_flat = None
     for j in range(chunks):
-        inners.append(inner_chunk(j, returned[j], done))
+        inners.append(inner_chunk(j, returned[j], done, at_hand.get(j)))
         done = [inners[-1]]
         if j < chunks - 1:
             grad_flat, token = basis_chunk(j, returned[j], grad_flat, done)
@@ -423,21 +507,22 @@
     total = sum(inners[1:], inners[0])
     flip, at, blocks = 1, 0, widths[-1] // block
     while flip < devices:
-        upto = -(-(at + blocks) // 2) if at == 0 else blocks
-        before = total
-        if flip * 2 < devices:
-            a, b, c = (send(total, flip * k) for k in (1, 2, 3))
-            total = (total + a) + (b + c)
-            flip *= 4
-        else:
-            total = total + send(total, flip)
-            flip *= 2
+        upto = -(-blocks // 2) if at == 0 else blocks
+        turns = P_ORDER if flip * 2 < devices else (1,)
+        got = {turn: send(total, turn * flip) for turn in turns}
+        flip *= len(turns) + 1
         if at < upto:
-            grad_flat, _ = basis_chunk(-1, returned[-1], grad_flat, [before], at, upto)
+            grad_flat, token = basis_chunk(-1, returned[-1], grad_flat, [total], at, upto)
             at = upto
-    slope = 1.0 - jnp.tanh(coeff) ** 2
-    grad_c = slope * total / math.sqrt(rank * width)
-    return (grad_a, grad_flat.reshape(num_bases, rows, width), grad_c)
+        last = flip >= devices
+        total = call(
+            functools.partial(add_kernel, turns, last),
+            "add",
+            [(got[turn], vmem) for turn in turns] + [(total, vmem)] + [(slope, vmem)] * last,
+            [(shape(experts, num_bases, dtype=F32), vmem)],
+            after=[token],
+        )[0]
+    return (grad_a, grad_flat.reshape(num_bases, rows, width), total)
 
 
 def solution(mesh):

time: 105 us -> 98.3 us (0.936)
  waiting for transfers between devices: 25 us -> 18.4 us
  Pallas kernels: 41.6 us -> 44.7 us
  starting transfers between devices: 34.8 us -> 31.9 us
    ppermute x30 -> x32, waiting for transfers between devices: 25 us -> 18.4 us  [send(): return lax.ppermute(x, 'expert', [(i, i ^ flip) for i in range(devices)])]
    pallas_call x16 -> x20, Pallas kernels: 41.6 us -> 44.7 us  [call(): pl.pallas_call(body, out_shape=[shape for shape, _ in outs], in_specs=[sp...]
    ppermute x30 -> x32, starting transfers between devices: 34.8 us -> 31.9 us  [send(): return lax.ppermute(x, 'expert', [(i, i ^ flip) for i in range(devices)])]
  transfers between devices with their start and end apart: 30 -> 32, of which waited for: 9 -> 9; matrix products, arithmetic and copies ran while one was open for 2% -> 2% of each run, Pallas kernels for 30% -> 37%
where the time goes in v3:
time: 98.3 us; the launch traced here: 98.1 us
  Pallas kernels  44.7 us (45%)
  starting transfers between devices  31.9 us (32%)
  waiting for transfers between devices  18.4 us (19%)
  matrix products  1.48 us (2%)
    pallas_call x20, Pallas kernels, call(): pl.pallas_call(body, out_shape=[shape for shape, _ in outs], in_specs=[sp...  44.7 us
    ppermute x32, starting transfers between devices, send(): return lax.ppermute(x, 'expert', [(i, i ^ flip) for i in range(devices)])  31.9 us
    ppermute x32, waiting for transfers between devices, send(): return lax.ppermute(x, 'expert', [(i, i ^ flip) for i in range(devices)])  18.4 us
  transfers between devices with their start and end apart: 32, of which 9 were waited for; matrix products, arithmetic and copies ran while one was open for 2% of the time, Pallas kernels for 37%

profile of v3, /device:TPU:0, one launch (start us, length us, event | category | flops | bytes accessed | tf_op | source)
XLA Modules:
  0.0 98.1 jit_solution(13954032503357295356)
XLA Ops:
  0.6 0.0 copy-start
  0.7 0.7 copy-done.2
  1.4 0.3 spread.1
  1.7 3.7 %mix.2 = (bf16[16,3584]{1,0:T(8,128)(2,1)S(1)}, bf16[16,3584]{1,0:T(8,128)(2,1)S(1)}, bf16[16,3584]{1,0:T(8,128)(2,1)S(1)}, bf16[16,3584]{1,0:T(8,128)(2,1)S(1)}) custom-call(bf16[64,1024]{1,0:T(8,128)(2,1)S(1)} %get-tuple-element.46.refs_0_, bf16[1024,7168]{1,0:T(8,128)(2,1)} %bitcast.7), custom_call_target="tpu_custom_call" | custom-call | tf_op jit(solution)/shard_map/mix/pallas_call | solution.py:268
  5.4 5.1 %collective-permute-start.3 = (bf16[16,3584]{1,0:T(8,128)(2,1)S(1)}, bf16[16,3584]{1,0:T(8,128)(2,1)S(1)}, u32[]{:S(2)}, u32[]{:S(2)}) collective-permute-start(bf16[16,3584]{1,0:T(8,128)(2,1)S(1)} %get-tuple-element.52), channel_id=1, source_target_pairs={{0,12},{1,13},{2,14},{3,15},{4,8},{5,9},{6,10},{7,11},{8,4},{9,5},... | collective-permute-start | bytes 344072 | tf_op jit(solution)/shard_map/ppermute | solution.py:250
  10.5 0.0 collective-permute-start.4
  10.5 0.6 collective-permute-start.5
  11.2 3.7 %mix.3 = (bf16[16,3584]{1,0:T(8,128)(2,1)S(1)}, bf16[16,3584]{1,0:T(8,128)(2,1)S(1)}, bf16[16,3584]{1,0:T(8,128)(2,1)S(1)}, bf16[16,3584]{1,0:T(8,128)(2,1)S(1)}) custom-call(bf16[64,1024]{1,0:T(8,128)(2,1)S(1)} %get-tuple-element.46.refs_0_, bf16[1024,7168]{1,0:T(8,128)(2,1)} %bitcast.8, bf16[16,3584]{1,0:T(8,128)(2,1)S(1)} %get-tuple-element.47.refs_2_.refs_3_), custom_call_target="tpu_custom_call" | custom-call | tf_op jit(solution)/shard_map/mix/pallas_call | solution.py:268
  14.9 0.0 collective-permute-done.3.refs_0_
  14.9 5.3 %collective-permute-done.4.refs_1_ = bf16[16,3584]{1,0:T(8,128)(2,1)S(1)} collective-permute-done((bf16[16,3584]{1,0:T(8,128)(2,1)S(1)}, bf16[16,3584]{1,0:T(8,128)(2,1)S(1)}, u32[]{:S(2)}, u32[]{:S(2)}) %collective-permute-start.4) | collective-permute-done | bytes 114720 | tf_op jit(solution)/shard_map/ppermute | solution.py:250
  20.2 0.0 collective-permute-done.5.refs_2_
  20.2 1.6 %collective-permute-start.9 = (bf16[64,3584]{1,0:T(8,128)(2,1)S(1)}, bf16[64,3584]{1,0:T(8,128)(2,1)S(1)}, u32[]{:S(2)}, u32[]{:S(2)}) collective-permute-start(bf16[64,3584]{1,0:T(8,128)(2,1)S(1)} %join.2.refs_4_.refs_3_), channel_id=1, source_target_pairs={{0,2},{1,3},{2,0},{3,1},{4,6},{5,7},{6,4},{7,5},{8,10},{9,11},{10,... | collective-permute-start | bytes 1376264 | tf_op jit(solution)/shard_map/ppermute | solution.py:250
  21.8 2.5 %collective-permute-start = (bf16[16,3584]{1,0:T(8,128)(2,1)S(1)}, bf16[16,3584]{1,0:T(8,128)(2,1)S(1)}, u32[]{:S(2)}, u32[]{:S(2)}) collective-permute-start(bf16[16,3584]{1,0:T(8,128)(2,1)S(1)} %get-tuple-element.48), channel_id=1, source_target_pairs={{0,12},{1,13},{2,14},{3,15},{4,8},{5,9},{6,10},{7,11},{8,4},{9,5},... | collective-permute-start | bytes 344072 | tf_op jit(solution)/shard_map/ppermute | solution.py:250
  24.3 1.9 %collective-permute-start.2 = (bf16[16,3584]{1,0:T(8,128)(2,1)S(1)}, bf16[16,3584]{1,0:T(8,128)(2,1)S(1)}, u32[]{:S(2)}, u32[]{:S(2)}) collective-permute-start(bf16[16,3584]{1,0:T(8,128)(2,1)S(1)} %get-tuple-element.50), channel_id=1, source_target_pairs={{0,4},{1,5},{2,6},{3,7},{4,0},{5,1},{6,2},{7,3},{8,12},{9,13},{10,... | collective-permute-start | bytes 344072 | tf_op jit(solution)/shard_map/ppermute | solution.py:250
  26.2 0.0 collective-permute-start.10
  26.2 5.7 %collective-permute-done.9.refs_4_ = bf16[64,3584]{1,0:T(8,128)(2,1)S(1)} collective-permute-done((bf16[64,3584]{1,0:T(8,128)(2,1)S(1)}, bf16[64,3584]{1,0:T(8,128)(2,1)S(1)}, u32[]{:S(2)}, u32[]{:S(2)}) %collective-permute-start.9) | collective-permute-done | bytes 458784 | tf_op jit(solution)/shard_map/ppermute | solution.py:250
  31.9 0.0 collective-permute-start.11
  31.9 0.0 collective-permute-done.refs_0_
  31.9 1.7 %collective-permute-done.1.refs_1_ = bf16[16,3584]{1,0:T(8,128)(2,1)S(1)} collective-permute-done((bf16[16,3584]{1,0:T(8,128)(2,1)S(1)}, bf16[16,3584]{1,0:T(8,128)(2,1)S(1)}, u32[]{:S(2)}, u32[]{:S(2)}) %collective-permute-start.1) | collective-permute-done | bytes 114720 | tf_op jit(solution)/shard_map/ppermute | solution.py:250
  33.6 0.0 collective-permute-done.2.refs_2_
  33.6 0.6 collective-permute-start.6
  34.2 0.3 convolution_convert_fusion.refs_1_
  34.5 0.1 copy.10.refs_0_
  34.7 5.9 %fit.2 = (f32[128,3584]{1,0:T(8,128)S(1)}, bf16[64,3584]{1,0:T(8,128)(2,1)S(1)}, bf16[64,3584]{1,0:T(8,128)(2,1)S(1)}, f32[512,256]{1,0:T(8,128)S(1)}) custom-call(bf16[512,256]{1,0:T(8,128)(2,1)S(1)} %copy.10.refs_0_, bf16[256,512]{1,0:T(8,128)(2,1)S(1)} %convolution_convert_fusion.refs_1_, bf16[512,7168]{1,0:T(8,128)(2,1)} %refs_2_.3, ...), custom_call_target="tpu_custom_call" | custom-call | tf_op jit(solution)/shard_map/fit/pallas_call | solution.py:268
  40.6 0.1 collective-permute-start.12
  40.6 0.5 collective-permute-start.13
  41.1 0.1 collective-permute-start.7
  41.2 4.0 %collective-permute-done.6.refs_4_ = bf16[64,3584]{1,0:T(8,128)(2,1)S(1)} collective-permute-done((bf16[64,3584]{1,0:T(8,128)(2,1)S(1)}, bf16[64,3584]{1,0:T(8,128)(2,1)S(1)}, u32[]{:S(2)}, u32[]{:S(2)}) %collective-permute-start.6) | collective-permute-done | bytes 458784 | tf_op jit(solution)/shard_map/ppermute | solution.py:250
  45.2 0.0 collective-permute-start.8
  45.2 0.0 collective-permute-done.12.refs_1_
  45.2 0.6 chip_sum.2
  45.8 1.3 %collective-permute-start.14 = (bf16[64,3584]{1,0:T(8,128)(2,1)S(1)}, bf16[64,3584]{1,0:T(8,128)(2,1)S(1)}, u32[]{:S(2)}, u32[]{:S(2)}) collective-permute-start(bf16[64,3584]{1,0:T(8,128)(2,1)S(1)} %get-tuple-element.62), channel_id=1, source_target_pairs={{0,2},{1,3},{2,0},{3,1},{4,6},{5,7},{6,4},{7,5},{8,10},{9,11},{10,... | collective-permute-start | bytes 1376264 | tf_op jit(solution)/shard_map/ppermute | solution.py:250
  47.1 5.9 %fit.3 = (f32[128,3584]{1,0:T(8,128)S(1)}, bf16[32,3584]{1,0:T(8,128)(2,1)S(1)}, bf16[32,3584]{1,0:T(8,128)(2,1)S(1)}, bf16[32,3584]{1,0:T(8,128)(2,1)S(1)}, bf1...) custom-call(bf16[512,256]{1,0:T(8,128)(2,1)S(1)} %copy.10.refs_0_, ...), custom_call_target="tpu_custom_call" | custom-call | tf_op jit(solution)/shard_map/fit/pallas_call | solution.py:268
  53.0 0.3 collective-permute-start.15
  53.3 0.3 collective-permute-start.16
  53.6 0.2 collective-permute-start.17
  53.8 0.3 collective-permute-start.18
  54.1 0.5 collective-permute-done.15.refs_1_
  54.6 0.3 collective-permute-done.16.refs_2_
  54.9 0.3 collective-permute-done.17.refs_3_
  55.3 0.3 collective-permute-done.18.refs_4_
  55.6 0.6 chip_sum.3
  56.2 1.2 %collective-permute-start.22 = (bf16[64,3584]{1,0:T(8,128)(2,1)S(1)}, bf16[64,3584]{1,0:T(8,128)(2,1)S(1)}, u32[]{:S(2)}, u32[]{:S(2)}) collective-permute-start(bf16[64,3584]{1,0:T(8,128)(2,1)S(1)} %get-tuple-element.75), channel_id=1, source_target_pairs={{0,2},{1,3},{2,0},{3,1},{4,6},{5,7},{6,4},{7,5},{8,10},{9,11},{10,... | collective-permute-start | bytes 1376264 | tf_op jit(solution)/shard_map/ppermute | solution.py:250
  57.4 3.2 %fetch.2 = (bf16[4,1024,896]{2,1,0:T(8,128)(2,1)S(1)}, f32[8,128]{1,0:T(8,128)S(1)}) custom-call(bf16[1024,7168]{1,0:T(8,128)(2,1)} %bitcast.9, f32[64,3584]{1,0:T(8,128)S(1)} %get-tuple-element.68.refs_1_.refs_0_), custom_call_target="tpu_custom_call" | custom-call | bytes 14680064 | tf_op jit(solution)/shard_map/fetch/pallas_call | solution.py:268
  60.6 0.4 plane_sum.2
  61.0 2.4 %collective-permute-start.19 = (bf16[16,3584]{1,0:T(8,128)(2,1)S(1)}, bf16[16,3584]{1,0:T(8,128)(2,1)S(1)}, u32[]{:S(2)}, u32[]{:S(2)}) collective-permute-start(bf16[16,3584]{1,0:T(8,128)(2,1)S(1)} %get-tuple-element.70), channel_id=1, source_target_pairs={{0,12},{1,13},{2,14},{3,15},{4,8},{5,9},{6,10},{7,11},{8,4},{9,5},... | collective-permute-start | bytes 344072 | tf_op jit(solution)/shard_map/ppermute | solution.py:250
  63.3 1.2 %convolution_multiply_fusion.refs_2_ = f32[512,256]{1,0:T(8,128)} fusion(f32[512,256]{1,0:T(8,128)S(1)} %get-tuple-element.60, s32[256]{0:T(256)S(1)} %fusion.6), kind=kOutput, calls=%fused_computation | convolution fusion | flops 402849792 | bytes 1049600 | tf_op jit(solution)/shard_map/dot_general | solution.py:494
  64.6 2.1 %collective-permute-start.21 = (bf16[16,3584]{1,0:T(8,128)(2,1)S(1)}, bf16[16,3584]{1,0:T(8,128)(2,1)S(1)}, u32[]{:S(2)}, u32[]{:S(2)}) collective-permute-start(bf16[16,3584]{1,0:T(8,128)(2,1)S(1)} %get-tuple-element.72), channel_id=1, source_target_pairs={{0,4},{1,5},{2,6},{3,7},{4,0},{5,1},{6,2},{7,3},{8,12},{9,13},{10,... | collective-permute-start | bytes 344072 | tf_op jit(solution)/shard_map/ppermute | solution.py:250
  66.6 3.2 %fetch.3 = (bf16[4,1024,896]{2,1,0:T(8,128)(2,1)S(1)}, f32[8,128]{1,0:T(8,128)S(1)}) custom-call(bf16[1024,7168]{1,0:T(8,128)(2,1)} %bitcast.10, bf16[16,3584]{1,0:T(8,128)(2,1)S(1)} %get-tuple-element.73.refs_1_.refs_5_.refs_4_, f32[512,256]{1,0:T(8,128)} %convolution_multiply_fusion.refs_2_), custom_call_target="tpu_custom_call" | custom-call | bytes 14680064 | tf_op jit(solution)/shard_map/fetch/pallas_call | solution.py:268
  69.9 0.4 plane_sum.3
  70.2 2.4 %collective-permute-start.23 = (bf16[16,3584]{1,0:T(8,128)(2,1)S(1)}, bf16[16,3584]{1,0:T(8,128)(2,1)S(1)}, u32[]{:S(2)}, u32[]{:S(2)}) collective-permute-start(bf16[16,3584]{1,0:T(8,128)(2,1)S(1)} %get-tuple-element.79), channel_id=1, source_target_pairs={{0,12},{1,13},{2,14},{3,15},{4,8},{5,9},{6,10},{7,11},{8,4},{9,5},... | collective-permute-start | bytes 344072 | tf_op jit(solution)/shard_map/ppermute | solution.py:250
  72.6 2.1 %collective-permute-start.25 = (bf16[16,3584]{1,0:T(8,128)(2,1)S(1)}, bf16[16,3584]{1,0:T(8,128)(2,1)S(1)}, u32[]{:S(2)}, u32[]{:S(2)}) collective-permute-start(bf16[16,3584]{1,0:T(8,128)(2,1)S(1)} %get-tuple-element.81), channel_id=1, source_target_pairs={{0,4},{1,5},{2,6},{3,7},{4,0},{5,1},{6,2},{7,3},{8,12},{9,13},{10,... | collective-permute-start | bytes 344072 | tf_op jit(solution)/shard_map/ppermute | solution.py:250
  74.7 3.4 %inner.2.refs_5_ = f32[4,64]{1,0:T(4,128)S(1)} custom-call(s32[1]{0:T(128)} %bitcast.1.refs_0_, bf16[4,1024,896]{2,1,0:T(8,128)(2,1)S(1)} %get-tuple-element.74.refs_1_, bf16[16,3584]{1,0:T(8,128)(2,1)S(1)} %collective-permute-done.19.refs_2_.refs_1_, bf16[16,3584]{1,0:T(8,128)(2,1)S(1)} %collective-permute-done.20.refs_3_.refs_2_, ...), custom_call_target="tpu_custom_call" | custom-call | tf_op jit(solution)/shard_map/inner/pallas_call | solution.py:268
  78.1 4.4 %basis.3 = (bf16[1024,7168]{1,0:T(8,128)(2,1)}, f32[8,128]{1,0:T(8,128)S(1)}) custom-call(bf16[1024,64]{1,0:T(8,128)(2,1)S(1)} %get-tuple-element.61.refs_0_, bf16[16,3584]{1,0:T(8,128)(2,1)S(1)} %collective-permute-done.19.refs_2_.refs_1_, bf16[16,3584]{1,0:T(8,128)(2,1)S(1)} %collective-permute-done.20.refs_3_.refs_2_, ...), custom_call_target="tpu_custom_call" | custom-call | tf_op jit(solution)/shard_map/basis/pallas_call | solution.py:268
  82.5 0.1 collective-permute-done.24.refs_3_
  82.7 3.4 %inner.3 = f32[4,64]{1,0:T(4,128)S(1)} custom-call(s32[1]{0:T(128)} %bitcast.1.refs_0_, bf16[4,1024,896]{2,1,0:T(8,128)(2,1)S(1)} %get-tuple-element.82.refs_1_, bf16[16,3584]{1,0:T(8,128)(2,1)S(1)} %collective-permute-done.23.refs_2_, bf16[16,3584]{1,0:T(8,128)(2,1)S(1)} %collective-permute-done.24.refs_3_, ...), custom_call_target="tpu_custom_call" | custom-call | tf_op jit(solution)/shard_map/inner/pallas_call | solution.py:268
  86.1 0.2 collective-permute-start.28
  86.3 1.1 %collective-permute-start.27 = (f32[4,64]{1,0:T(4,128)S(1)}, f32[4,64]{1,0:T(4,128)S(1)}, u32[]{:S(2)}, u32[]{:S(2)}) collective-permute-start(f32[4,64]{1,0:T(4,128)S(1)} %add.74.refs_6_.refs_3_), channel_id=1, source_target_pairs={{0,2},{1,3},{2,0},{3,1},{4,6},{5,7},{6,4},{7,5},{8,10},{9,11},{10,... | collective-permute-start | bytes 3080 | tf_op jit(solution)/shard_map/ppermute | solution.py:250
  87.4 0.6 collective-permute-start.26
  88.0 2.5 %basis.4 = (bf16[1024,7168]{1,0:T(8,128)(2,1)}, f32[8,128]{1,0:T(8,128)S(1)}) custom-call(bf16[1024,64]{1,0:T(8,128)(2,1)S(1)} %get-tuple-element.61.refs_0_, bf16[1024,7168]{1,0:T(8,128)(2,1)} %get-tuple-element.78.refs_1_, bf16[16,3584]{1,0:T(8,128)(2,1)S(1)} %collective-permute-done.23.refs_2_, ...), custom_call_target="tpu_custom_call", output_to_operand_aliasing={{0}: (1, {})} | custom-call | tf_op jit(solution)/shard_map/basis/pallas_call | solution.py:268
  90.6 2.2 %collective-permute-start.31 = (f32[4,64]{1,0:T(4,128)S(1)}, f32[4,64]{1,0:T(4,128)S(1)}, u32[]{:S(2)}, u32[]{:S(2)}) collective-permute-start(f32[4,64]{1,0:T(4,128)S(1)} %add.103.refs_6_.refs_3_), channel_id=1, source_target_pairs={{0,12},{1,13},{2,14},{3,15},{4,8},{5,9},{6,10},{7,11},{8,4},{9,5},... | collective-permute-start | bytes 3080 | tf_op jit(solution)/shard_map/ppermute | solution.py:250
  92.8 2.2 %collective-permute-start.29 = (f32[4,64]{1,0:T(4,128)S(1)}, f32[4,64]{1,0:T(4,128)S(1)}, u32[]{:S(2)}, u32[]{:S(2)}) collective-permute-start(f32[4,64]{1,0:T(4,128)S(1)} %add.103.refs_6_.refs_3_), channel_id=1, source_target_pairs={{0,4},{1,5},{2,6},{3,7},{4,0},{5,1},{6,2},{7,3},{8,12},{9,13},{10,... | collective-permute-start | bytes 3080 | tf_op jit(solution)/shard_map/ppermute | solution.py:250
  95.0 2.5 %basis.5 = (bf16[1024,7168]{1,0:T(8,128)(2,1)}, f32[8,128]{1,0:T(8,128)S(1)}) custom-call(bf16[1024,64]{1,0:T(8,128)(2,1)S(1)} %get-tuple-element.61.refs_0_, bf16[1024,7168]{1,0:T(8,128)(2,1)} %get-tuple-element.84.refs_1_, bf16[16,3584]{1,0:T(8,128)(2,1)S(1)} %collective-permute-done.23.refs_2_, ...), custom_call_target="tpu_custom_call", output_to_operand_aliasing={{0}: (1, {})} | custom-call | tf_op jit(solution)/shard_map/basis/pallas_call | solution.py:268
  97.6 0.6 add.104
  (31 shorter events, 0.2 us)
Async XLA Ops:
  0.6 33.6 %copy-start = (bf16[512,256]{1,0:T(8,128)(2,1)S(1)}, bf16[512,256]{1,0:T(8,128)(2,1)}, u32[]{:S(2)}) copy-start(bf16[512,256]{1,0:T(8,128)(2,1)} %param.5) | copy-start | bytes 786436
  0.7 0.7 copy-start.2
  5.4 9.4 %collective-permute-start.3 = (bf16[16,3584]{1,0:T(8,128)(2,1)S(1)}, bf16[16,3584]{1,0:T(8,128)(2,1)S(1)}, u32[]{:S(2)}, u32[]{:S(2)}) collective-permute-start(bf16[16,3584]{1,0:T(8,128)(2,1)S(1)} %get-tuple-element.52), channel_id=1, source_target_pairs={{0,12},{1,13},{2,14},{3,15},{4,8},{5,9},{6,10},{7,11},{8,4},{9,5},... | collective-permute-start | bytes 344072 | tf_op jit(solution)/shard_map/ppermute | solution.py:250
  10.5 9.7 %collective-permute-start.4 = (bf16[16,3584]{1,0:T(8,128)(2,1)S(1)}, bf16[16,3584]{1,0:T(8,128)(2,1)S(1)}, u32[]{:S(2)}, u32[]{:S(2)}) collective-permute-start(bf16[16,3584]{1,0:T(8,128)(2,1)S(1)} %get-tuple-element.53), channel_id=1, source_target_pairs={{0,8},{1,9},{2,10},{3,11},{4,12},{5,13},{6,14},{7,15},{8,0},{9,1},... | collective-permute-start | bytes 344072 | tf_op jit(solution)/shard_map/ppermute | solution.py:250
  10.5 9.7 %collective-permute-start.5 = (bf16[16,3584]{1,0:T(8,128)(2,1)S(1)}, bf16[16,3584]{1,0:T(8,128)(2,1)S(1)}, u32[]{:S(2)}, u32[]{:S(2)}) collective-permute-start(bf16[16,3584]{1,0:T(8,128)(2,1)S(1)} %get-tuple-element.54), channel_id=1, source_target_pairs={{0,4},{1,5},{2,6},{3,7},{4,0},{5,1},{6,2},{7,3},{8,12},{9,13},{10,... | collective-permute-start | bytes 344072 | tf_op jit(solution)/shard_map/ppermute | solution.py:250
  20.2 11.6 %collective-permute-start.9 = (bf16[64,3584]{1,0:T(8,128)(2,1)S(1)}, bf16[64,3584]{1,0:T(8,128)(2,1)S(1)}, u32[]{:S(2)}, u32[]{:S(2)}) collective-permute-start(bf16[64,3584]{1,0:T(8,128)(2,1)S(1)} %join.2.refs_4_.refs_3_), channel_id=1, source_target_pairs={{0,2},{1,3},{2,0},{3,1},{4,6},{5,7},{6,4},{7,5},{8,10},{9,11},{10,... | collective-permute-start | bytes 1376264 | tf_op jit(solution)/shard_map/ppermute | solution.py:250
  21.8 10.1 %collective-permute-start = (bf16[16,3584]{1,0:T(8,128)(2,1)S(1)}, bf16[16,3584]{1,0:T(8,128)(2,1)S(1)}, u32[]{:S(2)}, u32[]{:S(2)}) collective-permute-start(bf16[16,3584]{1,0:T(8,128)(2,1)S(1)} %get-tuple-element.48), channel_id=1, source_target_pairs={{0,12},{1,13},{2,14},{3,15},{4,8},{5,9},{6,10},{7,11},{8,4},{9,5},... | collective-permute-start | bytes 344072 | tf_op jit(solution)/shard_map/ppermute | solution.py:250
  24.3 9.3 %collective-permute-start.1 = (bf16[16,3584]{1,0:T(8,128)(2,1)S(1)}, bf16[16,3584]{1,0:T(8,128)(2,1)S(1)}, u32[]{:S(2)}, u32[]{:S(2)}) collective-permute-start(bf16[16,3584]{1,0:T(8,128)(2,1)S(1)} %get-tuple-element.49), channel_id=1, source_target_pairs={{0,8},{1,9},{2,10},{3,11},{4,12},{5,13},{6,14},{7,15},{8,0},{9,1},... | collective-permute-start | bytes 344072 | tf_op jit(solution)/shard_map/ppermute | solution.py:250
  24.3 9.3 %collective-permute-start.2 = (bf16[16,3584]{1,0:T(8,128)(2,1)S(1)}, bf16[16,3584]{1,0:T(8,128)(2,1)S(1)}, u32[]{:S(2)}, u32[]{:S(2)}) collective-permute-start(bf16[16,3584]{1,0:T(8,128)(2,1)S(1)} %get-tuple-element.50), channel_id=1, source_target_pairs={{0,4},{1,5},{2,6},{3,7},{4,0},{5,1},{6,2},{7,3},{8,12},{9,13},{10,... | collective-permute-start | bytes 344072 | tf_op jit(solution)/shard_map/ppermute | solution.py:250
  26.2 8.4 %collective-permute-start.10 = (bf16[64,3584]{1,0:T(8,128)(2,1)S(1)}, bf16[64,3584]{1,0:T(8,128)(2,1)S(1)}, u32[]{:S(2)}, u32[]{:S(2)}) collective-permute-start(bf16[64,3584]{1,0:T(8,128)(2,1)S(1)} %join.2.refs_4_.refs_3_), channel_id=1, source_target_pairs={{0,1},{1,0},{2,3},{3,2},{4,5},{5,4},{6,7},{7,6},{8,9},{9,8},{10,11... | collective-permute-start | bytes 1376264 | tf_op jit(solution)/shard_map/ppermute | solution.py:250
  31.9 2.8 %collective-permute-start.11 = (bf16[64,3584]{1,0:T(8,128)(2,1)S(1)}, bf16[64,3584]{1,0:T(8,128)(2,1)S(1)}, u32[]{:S(2)}, u32[]{:S(2)}) collective-permute-start(bf16[64,3584]{1,0:T(8,128)(2,1)S(1)} %collective-permute-done.9.refs_4_), channel_id=1, source_target_pairs={{0,1},{1,0},{2,3},{3,2},{4,5},{5,4},{6,7},{7,6},{8,9},{9,8},{10,11... | collective-permute-start | bytes 1376264 | tf_op jit(solution)/shard_map/ppermute | solution.py:250
  33.6 11.6 %collective-permute-start.6 = (bf16[64,3584]{1,0:T(8,128)(2,1)S(1)}, bf16[64,3584]{1,0:T(8,128)(2,1)S(1)}, u32[]{:S(2)}, u32[]{:S(2)}) collective-permute-start(bf16[64,3584]{1,0:T(8,128)(2,1)S(1)} %join.3.refs_7_.refs_3_), channel_id=1, source_target_pairs={{0,2},{1,3},{2,0},{3,1},{4,6},{5,7},{6,4},{7,5},{8,10},{9,11},{10,... | collective-permute-start | bytes 1376264 | tf_op jit(solution)/shard_map/ppermute | solution.py:250
  40.6 4.7 %collective-permute-start.12 = (bf16[64,3584]{1,0:T(8,128)(2,1)S(1)}, bf16[64,3584]{1,0:T(8,128)(2,1)S(1)}, u32[]{:S(2)}, u32[]{:S(2)}) collective-permute-start(bf16[64,3584]{1,0:T(8,128)(2,1)S(1)} %get-tuple-element.57), channel_id=1, source_target_pairs={{0,1},{1,0},{2,3},{3,2},{4,5},{5,4},{6,7},{7,6},{8,9},{9,8},{10,11... | collective-permute-start | bytes 1376264 | tf_op jit(solution)/shard_map/ppermute | solution.py:250
  40.6 4.6 %collective-permute-start.13 = (bf16[64,3584]{1,0:T(8,128)(2,1)S(1)}, bf16[64,3584]{1,0:T(8,128)(2,1)S(1)}, u32[]{:S(2)}, u32[]{:S(2)}) collective-permute-start(bf16[64,3584]{1,0:T(8,128)(2,1)S(1)} %get-tuple-element.58), channel_id=1, source_target_pairs={{0,1},{1,0},{2,3},{3,2},{4,5},{5,4},{6,7},{7,6},{8,9},{9,8},{10,11... | collective-permute-start | bytes 1376264 | tf_op jit(solution)/shard_map/ppermute | solution.py:250
  41.1 6.0 %collective-permute-start.7 = (bf16[64,3584]{1,0:T(8,128)(2,1)S(1)}, bf16[64,3584]{1,0:T(8,128)(2,1)S(1)}, u32[]{:S(2)}, u32[]{:S(2)}) collective-permute-start(bf16[64,3584]{1,0:T(8,128)(2,1)S(1)} %join.3.refs_7_.refs_3_), channel_id=1, source_target_pairs={{0,1},{1,0},{2,3},{3,2},{4,5},{5,4},{6,7},{7,6},{8,9},{9,8},{10,11... | collective-permute-start | bytes 1376264 | tf_op jit(solution)/shard_map/ppermute | solution.py:250
  45.2 1.9 %collective-permute-start.8 = (bf16[64,3584]{1,0:T(8,128)(2,1)S(1)}, bf16[64,3584]{1,0:T(8,128)(2,1)S(1)}, u32[]{:S(2)}, u32[]{:S(2)}) collective-permute-start(bf16[64,3584]{1,0:T(8,128)(2,1)S(1)} %collective-permute-done.6.refs_4_), channel_id=1, source_target_pairs={{0,1},{1,0},{2,3},{3,2},{4,5},{5,4},{6,7},{7,6},{8,9},{9,8},{10,11... | collective-permute-start | bytes 1376264 | tf_op jit(solution)/shard_map/ppermute | solution.py:250
  45.8 14.8 %collective-permute-start.14 = (bf16[64,3584]{1,0:T(8,128)(2,1)S(1)}, bf16[64,3584]{1,0:T(8,128)(2,1)S(1)}, u32[]{:S(2)}, u32[]{:S(2)}) collective-permute-start(bf16[64,3584]{1,0:T(8,128)(2,1)S(1)} %get-tuple-element.62), channel_id=1, source_target_pairs={{0,2},{1,3},{2,0},{3,1},{4,6},{5,7},{6,4},{7,5},{8,10},{9,11},{10,... | collective-permute-start | bytes 1376264 | tf_op jit(solution)/shard_map/ppermute | solution.py:250
  53.0 1.6 %collective-permute-start.15 = (bf16[32,3584]{1,0:T(8,128)(2,1)S(1)}, bf16[32,3584]{1,0:T(8,128)(2,1)S(1)}, u32[]{:S(2)}, u32[]{:S(2)}) collective-permute-start(bf16[32,3584]{1,0:T(8,128)(2,1)S(1)} %get-tuple-element.64), channel_id=1, source_target_pairs={{0,1},{1,0},{2,3},{3,2},{4,5},{5,4},{6,7},{7,6},{8,9},{9,8},{10,11... | collective-permute-start | bytes 688136 | tf_op jit(solution)/shard_map/ppermute | solution.py:250
  53.3 1.6 %collective-permute-start.16 = (bf16[32,3584]{1,0:T(8,128)(2,1)S(1)}, bf16[32,3584]{1,0:T(8,128)(2,1)S(1)}, u32[]{:S(2)}, u32[]{:S(2)}) collective-permute-start(bf16[32,3584]{1,0:T(8,128)(2,1)S(1)} %get-tuple-element.65), channel_id=1, source_target_pairs={{0,1},{1,0},{2,3},{3,2},{4,5},{5,4},{6,7},{7,6},{8,9},{9,8},{10,11... | collective-permute-start | bytes 688136 | tf_op jit(solution)/shard_map/ppermute | solution.py:250
  53.6 1.6 %collective-permute-start.17 = (bf16[32,3584]{1,0:T(8,128)(2,1)S(1)}, bf16[32,3584]{1,0:T(8,128)(2,1)S(1)}, u32[]{:S(2)}, u32[]{:S(2)}) collective-permute-start(bf16[32,3584]{1,0:T(8,128)(2,1)S(1)} %get-tuple-element.66), channel_id=1, source_target_pairs={{0,1},{1,0},{2,3},{3,2},{4,5},{5,4},{6,7},{7,6},{8,9},{9,8},{10,11... | collective-permute-start | bytes 688136 | tf_op jit(solution)/shard_map/ppermute | solution.py:250
  53.8 1.8 %collective-permute-start.18 = (bf16[32,3584]{1,0:T(8,128)(2,1)S(1)}, bf16[32,3584]{1,0:T(8,128)(2,1)S(1)}, u32[]{:S(2)}, u32[]{:S(2)}) collective-permute-start(bf16[32,3584]{1,0:T(8,128)(2,1)S(1)} %get-tuple-element.67), channel_id=1, source_target_pairs={{0,1},{1,0},{2,3},{3,2},{4,5},{5,4},{6,7},{7,6},{8,9},{9,8},{10,11... | collective-permute-start | bytes 688136 | tf_op jit(solution)/shard_map/ppermute | solution.py:250
  56.2 13.7 %collective-permute-start.22 = (bf16[64,3584]{1,0:T(8,128)(2,1)S(1)}, bf16[64,3584]{1,0:T(8,128)(2,1)S(1)}, u32[]{:S(2)}, u32[]{:S(2)}) collective-permute-start(bf16[64,3584]{1,0:T(8,128)(2,1)S(1)} %get-tuple-element.75), channel_id=1, source_target_pairs={{0,2},{1,3},{2,0},{3,1},{4,6},{5,7},{6,4},{7,5},{8,10},{9,11},{10,... | collective-permute-start | bytes 1376264 | tf_op jit(solution)/shard_map/ppermute | solution.py:250
  61.0 11.6 %collective-permute-start.19 = (bf16[16,3584]{1,0:T(8,128)(2,1)S(1)}, bf16[16,3584]{1,0:T(8,128)(2,1)S(1)}, u32[]{:S(2)}, u32[]{:S(2)}) collective-permute-start(bf16[16,3584]{1,0:T(8,128)(2,1)S(1)} %get-tuple-element.70), channel_id=1, source_target_pairs={{0,12},{1,13},{2,14},{3,15},{4,8},{5,9},{6,10},{7,11},{8,4},{9,5},... | collective-permute-start | bytes 344072 | tf_op jit(solution)/shard_map/ppermute | solution.py:250
  64.5 10.1 %collective-permute-start.20 = (bf16[16,3584]{1,0:T(8,128)(2,1)S(1)}, bf16[16,3584]{1,0:T(8,128)(2,1)S(1)}, u32[]{:S(2)}, u32[]{:S(2)}) collective-permute-start(bf16[16,3584]{1,0:T(8,128)(2,1)S(1)} %get-tuple-element.71), channel_id=1, source_target_pairs={{0,8},{1,9},{2,10},{3,11},{4,12},{5,13},{6,14},{7,15},{8,0},{9,1},... | collective-permute-start | bytes 344072 | tf_op jit(solution)/shard_map/ppermute | solution.py:250
  64.6 10.1 %collective-permute-start.21 = (bf16[16,3584]{1,0:T(8,128)(2,1)S(1)}, bf16[16,3584]{1,0:T(8,128)(2,1)S(1)}, u32[]{:S(2)}, u32[]{:S(2)}) collective-permute-start(bf16[16,3584]{1,0:T(8,128)(2,1)S(1)} %get-tuple-element.72), channel_id=1, source_target_pairs={{0,4},{1,5},{2,6},{3,7},{4,0},{5,1},{6,2},{7,3},{8,12},{9,13},{10,... | collective-permute-start | bytes 344072 | tf_op jit(solution)/shard_map/ppermute | solution.py:250
  70.2 12.3 %collective-permute-start.23 = (bf16[16,3584]{1,0:T(8,128)(2,1)S(1)}, bf16[16,3584]{1,0:T(8,128)(2,1)S(1)}, u32[]{:S(2)}, u32[]{:S(2)}) collective-permute-start(bf16[16,3584]{1,0:T(8,128)(2,1)S(1)} %get-tuple-element.79), channel_id=1, source_target_pairs={{0,12},{1,13},{2,14},{3,15},{4,8},{5,9},{6,10},{7,11},{8,4},{9,5},... | collective-permute-start | bytes 344072 | tf_op jit(solution)/shard_map/ppermute | solution.py:250
  72.6 10.1 %collective-permute-start.24 = (bf16[16,3584]{1,0:T(8,128)(2,1)S(1)}, bf16[16,3584]{1,0:T(8,128)(2,1)S(1)}, u32[]{:S(2)}, u32[]{:S(2)}) collective-permute-start(bf16[16,3584]{1,0:T(8,128)(2,1)S(1)} %get-tuple-element.80), channel_id=1, source_target_pairs={{0,8},{1,9},{2,10},{3,11},{4,12},{5,13},{6,14},{7,15},{8,0},{9,1},... | collective-permute-start | bytes 344072 | tf_op jit(solution)/shard_map/ppermute | solution.py:250
  72.6 10.1 %collective-permute-start.25 = (bf16[16,3584]{1,0:T(8,128)(2,1)S(1)}, bf16[16,3584]{1,0:T(8,128)(2,1)S(1)}, u32[]{:S(2)}, u32[]{:S(2)}) collective-permute-start(bf16[16,3584]{1,0:T(8,128)(2,1)S(1)} %get-tuple-element.81), channel_id=1, source_target_pairs={{0,4},{1,5},{2,6},{3,7},{4,0},{5,1},{6,2},{7,3},{8,12},{9,13},{10,... | collective-permute-start | bytes 344072 | tf_op jit(solution)/shard_map/ppermute | solution.py:250
  86.1 4.4 %collective-permute-start.28 = (f32[4,64]{1,0:T(4,128)S(1)}, f32[4,64]{1,0:T(4,128)S(1)}, u32[]{:S(2)}, u32[]{:S(2)}) collective-permute-start(f32[4,64]{1,0:T(4,128)S(1)} %add.74.refs_6_.refs_3_), channel_id=1, source_target_pairs={{0,3},{1,2},{2,1},{3,0},{4,7},{5,6},{6,5},{7,4},{8,11},{9,10},{10,... | collective-permute-start | bytes 3080 | tf_op jit(solution)/shard_map/ppermute | solution.py:250
  86.3 4.3 %collective-permute-start.27 = (f32[4,64]{1,0:T(4,128)S(1)}, f32[4,64]{1,0:T(4,128)S(1)}, u32[]{:S(2)}, u32[]{:S(2)}) collective-permute-start(f32[4,64]{1,0:T(4,128)S(1)} %add.74.refs_6_.refs_3_), channel_id=1, source_target_pairs={{0,2},{1,3},{2,0},{3,1},{4,6},{5,7},{6,4},{7,5},{8,10},{9,11},{10,... | collective-permute-start | bytes 3080 | tf_op jit(solution)/shard_map/ppermute | solution.py:250
  87.4 3.2 %collective-permute-start.26 = (f32[4,64]{1,0:T(4,128)S(1)}, f32[4,64]{1,0:T(4,128)S(1)}, u32[]{:S(2)}, u32[]{:S(2)}) collective-permute-start(f32[4,64]{1,0:T(4,128)S(1)} %add.74.refs_6_.refs_3_), channel_id=1, source_target_pairs={{0,1},{1,0},{2,3},{3,2},{4,5},{5,4},{6,7},{7,6},{8,9},{9,8},{10,11... | collective-permute-start | bytes 3080 | tf_op jit(solution)/shard_map/ppermute | solution.py:250
  90.6 7.0 %collective-permute-start.31 = (f32[4,64]{1,0:T(4,128)S(1)}, f32[4,64]{1,0:T(4,128)S(1)}, u32[]{:S(2)}, u32[]{:S(2)}) collective-permute-start(f32[4,64]{1,0:T(4,128)S(1)} %add.103.refs_6_.refs_3_), channel_id=1, source_target_pairs={{0,12},{1,13},{2,14},{3,15},{4,8},{5,9},{6,10},{7,11},{8,4},{9,5},... | collective-permute-start | bytes 3080 | tf_op jit(solution)/shard_map/ppermute | solution.py:250
  92.8 4.8 %collective-permute-start.30 = (f32[4,64]{1,0:T(4,128)S(1)}, f32[4,64]{1,0:T(4,128)S(1)}, u32[]{:S(2)}, u32[]{:S(2)}) collective-permute-start(f32[4,64]{1,0:T(4,128)S(1)} %add.103.refs_6_.refs_3_), channel_id=1, source_target_pairs={{0,8},{1,9},{2,10},{3,11},{4,12},{5,13},{6,14},{7,15},{8,0},{9,1},... | collective-permute-start | bytes 3080 | tf_op jit(solution)/shard_map/ppermute | solution.py:250
  92.8 4.8 %collective-permute-start.29 = (f32[4,64]{1,0:T(4,128)S(1)}, f32[4,64]{1,0:T(4,128)S(1)}, u32[]{:S(2)}, u32[]{:S(2)}) collective-permute-start(f32[4,64]{1,0:T(4,128)S(1)} %add.103.refs_6_.refs_3_), channel_id=1, source_target_pairs={{0,4},{1,5},{2,6},{3,7},{4,0},{5,1},{6,2},{7,3},{8,12},{9,13},{10,... | collective-permute-start | bytes 3080 | tf_op jit(solution)/shard_map/ppermute | solution.py:250
  95.0 3.1 %copy-start.1 = (bf16[512,256]{1,0:T(8,128)(2,1)S(1)}, bf16[512,256]{1,0:T(8,128)(2,1)}, u32[]{:S(2)}) copy-start(bf16[512,256]{1,0:T(8,128)(2,1)} %param.5) | copy-start | bytes 786436

commit v4 on v3

--- a/solution.py
+++ b/solution.py
@@ -12,13 +12,14 @@
 HIGHEST = lax.Precision.HIGHEST
 SHARES = (1, 1)
 LAG = 1
+LARGE = 2048
 FAR = (2, 4)
 FB = (0, 1)
 Z_ORDER = (3, 2, 1)
 P_ORDER = (1, 2, 3)
 FETCH_COST = 1
 FLOPS = 0
-VMEM_LIMIT = 14 * 2**20
+VMEM_LIMIT = 26 * 2**20
 
 
 def iota(shape, dim):
@@ -237,8 +238,9 @@
     chunks = len(widths)
     starts = [sum(widths[:j]) for j in range(chunks)]
     block = math.gcd(*widths)
-    while block > 1024 and block % 256 == 0:
+    while block > LARGE and block % 256 == 0:
         block //= 2
+    small = block // 2 if block % 256 == 0 else block
     me = lax.axis_index("expert")
     place = (me // group).astype(jnp.int32).reshape(1)
     smem = pl.BlockSpec(memory_space=pltpu.SMEM)
@@ -283,12 +285,13 @@
     def shape(*dims, dtype=BF16):
         return jax.ShapeDtypeStruct(dims, dtype)
 
-    def col(rows_in, start=0):
-        return column_spec(rows_in, block, start // block)
-
-    def held(j, rows_in):
-        steps = widths[j] // block
-        return [pltpu.VMEM((steps, rows_in, block), BF16), pltpu.SemaphoreType.DMA((steps,))]
+    def col(rows_in, start=0, size=None):
+        size = size or block
+        return column_spec(rows_in, size, start // size)
+
+    def held(j, rows_in, size):
+        steps = widths[j] // size
+        return [pltpu.VMEM((steps, rows_in, size), BF16), pltpu.SemaphoreType.DMA((steps,))]
 
     flat = bases.reshape(wide, width)
     root = math.isqrt(experts)
@@ -323,12 +326,12 @@
             functools.partial(mix_kernel, starts[j]),
             "mix",
             [(spread, whole_spec((tall, wide))), (flat, hbm)],
-            [(shape(tall // count, widths[j]), col(tall // count))] * count,
-            (widths[j] // block,),
+            [(shape(tall // count, widths[j]), col(tall // count, 0, small))] * count,
+            (widths[j] // small,),
             after,
             FLOPS * 2 * tall * wide * widths[j],
             FLOPS * 2 * wide * widths[j],
-            scratch_shapes=held(j, wide),
+            scratch_shapes=held(j, wide, small),
         )
         return list(outs) if split else pieces_of(outs[0])
 
@@ -381,7 +384,7 @@
             after,
             FLOPS * 6 * ff * rank * widths[j],
             FLOPS * 2 * ff * widths[j],
-            scratch_shapes=held(j, ff),
+            scratch_shapes=held(j, ff, block),
         )
 
     def chip_sum(j, near, got, after):
@@ -435,23 +438,24 @@
             after,
             FLOPS * 2 * tall * wide * widths[j],
             FLOPS * 2 * wide * widths[j],
-            scratch_shapes=[pltpu.VMEM((tall, wide), F32), *([] if there else held(j, wide))],
+            scratch_shapes=[pltpu.VMEM((tall, wide), F32), *([] if there else held(j, wide, block))],
         )[0]
 
     def basis_chunk(j, sums, before, after, first=0, last=None):
         extra = [] if before is None else [(before, hbm)]
+        unit = block if last is None else small
         last = widths[j] // block if last is None else last
-        size = (last - first) * block
+        size = (last - first) * unit
         return call(
             functools.partial(basis_kernel, late_scale, len(extra)),
             "basis",
             [
                 (spread_t, whole_spec((wide, tall))),
                 *extra,
-                *[(part, col(part.shape[0], first * block)) for part, _ in sums_of(sums)],
+                *[(part, col(part.shape[0], first * unit, unit)) for part, _ in sums_of(sums)],
             ],
             [
-                (shape(wide, width), col(wide, starts[j] + first * block)),
+                (shape(wide, width), col(wide, starts[j] + first * unit, unit)),
                 (shape(8, 128, dtype=F32), whole_spec((8, 128))),
             ],
             (last - first,),
@@ -505,7 +509,7 @@
             done = [token]
 
     total = sum(inners[1:], inners[0])
-    flip, at, blocks = 1, 0, widths[-1] // block
+    flip, at, blocks = 1, 0, widths[-1] // small
     while flip < devices:
         upto = -(-blocks // 2) if at == 0 else blocks
         turns = P_ORDER if flip * 2 < devices else (1,)

time: 98.3 us -> 97.1 us (0.988)
  Pallas kernels: 44.7 us -> 42 us
  waiting for transfers between devices: 18.4 us -> 19.7 us
    pallas_call x20, Pallas kernels: 44.7 us -> 42 us  [call(): pl.pallas_call(body, out_shape=[shape for shape, _ in outs], in_specs=[sp...]
    ppermute x32, waiting for transfers between devices: 18.4 us -> 19.7 us  [send(): return lax.ppermute(x, 'expert', [(i, i ^ flip) for i in range(devices)])]
  transfers between devices with their start and end apart: 32 -> 32, of which waited for: 9 -> 9; matrix products, arithmetic and copies ran while one was open for 2% -> 2% of each run, Pallas kernels for 37% -> 35%
where the time goes in v4:
time: 97.1 us; the launch traced here: 96.9 us
  Pallas kernels  42 us (43%)
  starting transfers between devices  31.9 us (33%)
  waiting for transfers between devices  19.7 us (20%)
  matrix products  1.48 us (2%)
    pallas_call x20, Pallas kernels, call(): pl.pallas_call(body, out_shape=[shape for shape, _ in outs], in_specs=[sp...  42 us
    ppermute x32, starting transfers between devices, send(): return lax.ppermute(x, 'expert', [(i, i ^ flip) for i in range(devices)])  31.9 us
    ppermute x32, waiting for transfers between devices, send(): return lax.ppermute(x, 'expert', [(i, i ^ flip) for i in range(devices)])  19.7 us
  transfers between devices with their start and end apart: 32, of which 9 were waited for; matrix products, arithmetic and copies ran while one was open for 2% of the time, Pallas kernels for 35%

profile of v4, /device:TPU:0, one launch (start us, length us, event | category | flops | bytes accessed | tf_op | source)
XLA Modules:
  0.0 96.9 jit_solution(1384401641329985613)
XLA Ops:
  0.6 0.0 copy-start
  0.7 0.7 copy-done.2
  1.4 0.3 spread.1
  1.7 3.7 %mix.2 = (bf16[16,3584]{1,0:T(8,128)(2,1)S(1)}, bf16[16,3584]{1,0:T(8,128)(2,1)S(1)}, bf16[16,3584]{1,0:T(8,128)(2,1)S(1)}, bf16[16,3584]{1,0:T(8,128)(2,1)S(1)}) custom-call(bf16[64,1024]{1,0:T(8,128)(2,1)S(1)} %get-tuple-element.46.refs_0_, bf16[1024,7168]{1,0:T(8,128)(2,1)} %bitcast.7), custom_call_target="tpu_custom_call" | custom-call | tf_op jit(solution)/shard_map/mix/pallas_call | solution.py:270
  5.4 5.1 %collective-permute-start.3 = (bf16[16,3584]{1,0:T(8,128)(2,1)S(1)}, bf16[16,3584]{1,0:T(8,128)(2,1)S(1)}, u32[]{:S(2)}, u32[]{:S(2)}) collective-permute-start(bf16[16,3584]{1,0:T(8,128)(2,1)S(1)} %get-tuple-element.52), channel_id=1, source_target_pairs={{0,12},{1,13},{2,14},{3,15},{4,8},{5,9},{6,10},{7,11},{8,4},{9,5},... | collective-permute-start | bytes 344072 | tf_op jit(solution)/shard_map/ppermute | solution.py:252
  10.5 0.6 collective-permute-start.5
  11.2 3.7 %mix.3 = (bf16[16,3584]{1,0:T(8,128)(2,1)S(1)}, bf16[16,3584]{1,0:T(8,128)(2,1)S(1)}, bf16[16,3584]{1,0:T(8,128)(2,1)S(1)}, bf16[16,3584]{1,0:T(8,128)(2,1)S(1)}) custom-call(bf16[64,1024]{1,0:T(8,128)(2,1)S(1)} %get-tuple-element.46.refs_0_, bf16[1024,7168]{1,0:T(8,128)(2,1)} %bitcast.8, bf16[16,3584]{1,0:T(8,128)(2,1)S(1)} %get-tuple-element.47.refs_2_.refs_3_), custom_call_target="tpu_custom_call" | custom-call | tf_op jit(solution)/shard_map/mix/pallas_call | solution.py:270
  14.9 0.0 collective-permute-done.3.refs_0_
  14.9 5.3 %collective-permute-done.4.refs_1_ = bf16[16,3584]{1,0:T(8,128)(2,1)S(1)} collective-permute-done((bf16[16,3584]{1,0:T(8,128)(2,1)S(1)}, bf16[16,3584]{1,0:T(8,128)(2,1)S(1)}, u32[]{:S(2)}, u32[]{:S(2)}) %collective-permute-start.4) | collective-permute-done | bytes 114720 | tf_op jit(solution)/shard_map/ppermute | solution.py:252
  20.2 0.0 collective-permute-done.5.refs_2_
  20.2 1.6 %collective-permute-start.9 = (bf16[64,3584]{1,0:T(8,128)(2,1)S(1)}, bf16[64,3584]{1,0:T(8,128)(2,1)S(1)}, u32[]{:S(2)}, u32[]{:S(2)}) collective-permute-start(bf16[64,3584]{1,0:T(8,128)(2,1)S(1)} %join.2.refs_4_.refs_3_), channel_id=1, source_target_pairs={{0,2},{1,3},{2,0},{3,1},{4,6},{5,7},{6,4},{7,5},{8,10},{9,11},{10,... | collective-permute-start | bytes 1376264 | tf_op jit(solution)/shard_map/ppermute | solution.py:252
  21.8 2.5 %collective-permute-start = (bf16[16,3584]{1,0:T(8,128)(2,1)S(1)}, bf16[16,3584]{1,0:T(8,128)(2,1)S(1)}, u32[]{:S(2)}, u32[]{:S(2)}) collective-permute-start(bf16[16,3584]{1,0:T(8,128)(2,1)S(1)} %get-tuple-element.48), channel_id=1, source_target_pairs={{0,12},{1,13},{2,14},{3,15},{4,8},{5,9},{6,10},{7,11},{8,4},{9,5},... | collective-permute-start | bytes 344072 | tf_op jit(solution)/shard_map/ppermute | solution.py:252
  24.3 1.9 %collective-permute-start.2 = (bf16[16,3584]{1,0:T(8,128)(2,1)S(1)}, bf16[16,3584]{1,0:T(8,128)(2,1)S(1)}, u32[]{:S(2)}, u32[]{:S(2)}) collective-permute-start(bf16[16,3584]{1,0:T(8,128)(2,1)S(1)} %get-tuple-element.50), channel_id=1, source_target_pairs={{0,4},{1,5},{2,6},{3,7},{4,0},{5,1},{6,2},{7,3},{8,12},{9,13},{10,... | collective-permute-start | bytes 344072 | tf_op jit(solution)/shard_map/ppermute | solution.py:252
  26.2 0.0 collective-permute-start.10
  26.2 5.7 %collective-permute-done.9.refs_4_ = bf16[64,3584]{1,0:T(8,128)(2,1)S(1)} collective-permute-done((bf16[64,3584]{1,0:T(8,128)(2,1)S(1)}, bf16[64,3584]{1,0:T(8,128)(2,1)S(1)}, u32[]{:S(2)}, u32[]{:S(2)}) %collective-permute-start.9) | collective-permute-done | bytes 458784 | tf_op jit(solution)/shard_map/ppermute | solution.py:252
  31.9 0.0 collective-permute-start.11
  31.9 0.0 collective-permute-done.refs_0_
  31.9 1.7 %collective-permute-done.1.refs_1_ = bf16[16,3584]{1,0:T(8,128)(2,1)S(1)} collective-permute-done((bf16[16,3584]{1,0:T(8,128)(2,1)S(1)}, bf16[16,3584]{1,0:T(8,128)(2,1)S(1)}, u32[]{:S(2)}, u32[]{:S(2)}) %collective-permute-start.1) | collective-permute-done | bytes 114720 | tf_op jit(solution)/shard_map/ppermute | solution.py:252
  33.6 0.6 collective-permute-start.6
  34.2 0.3 convolution_convert_fusion.refs_1_
  34.5 0.1 copy.10.refs_0_
  34.7 0.0 collective-permute-done.11.refs_6_
  34.7 5.2 %fit.2 = (f32[128,3584]{1,0:T(8,128)S(1)}, bf16[64,3584]{1,0:T(8,128)(2,1)S(1)}, bf16[64,3584]{1,0:T(8,128)(2,1)S(1)}, f32[512,256]{1,0:T(8,128)S(1)}) custom-call(bf16[512,256]{1,0:T(8,128)(2,1)S(1)} %copy.10.refs_0_, bf16[256,512]{1,0:T(8,128)(2,1)S(1)} %convolution_convert_fusion.refs_1_, bf16[512,7168]{1,0:T(8,128)(2,1)} %refs_2_.3, ...), custom_call_target="tpu_custom_call" | custom-call | tf_op jit(solution)/shard_map/fit/pallas_call | solution.py:270
  39.9 0.1 collective-permute-start.12
  40.0 0.5 collective-permute-start.13
  40.5 0.1 collective-permute-start.7
  40.5 4.7 %collective-permute-done.6.refs_4_ = bf16[64,3584]{1,0:T(8,128)(2,1)S(1)} collective-permute-done((bf16[64,3584]{1,0:T(8,128)(2,1)S(1)}, bf16[64,3584]{1,0:T(8,128)(2,1)S(1)}, u32[]{:S(2)}, u32[]{:S(2)}) %collective-permute-start.6) | collective-permute-done | bytes 458784 | tf_op jit(solution)/shard_map/ppermute | solution.py:252
  45.2 0.0 collective-permute-done.12.refs_1_
  45.2 0.0 collective-permute-done.13.refs_2_
  45.2 0.5 chip_sum.2
  45.7 1.3 %collective-permute-start.14 = (bf16[64,3584]{1,0:T(8,128)(2,1)S(1)}, bf16[64,3584]{1,0:T(8,128)(2,1)S(1)}, u32[]{:S(2)}, u32[]{:S(2)}) collective-permute-start(bf16[64,3584]{1,0:T(8,128)(2,1)S(1)} %get-tuple-element.62), channel_id=1, source_target_pairs={{0,2},{1,3},{2,0},{3,1},{4,6},{5,7},{6,4},{7,5},{8,10},{9,11},{10,... | collective-permute-start | bytes 1376264 | tf_op jit(solution)/shard_map/ppermute | solution.py:252
  47.1 5.2 %fit.3 = (f32[128,3584]{1,0:T(8,128)S(1)}, bf16[32,3584]{1,0:T(8,128)(2,1)S(1)}, bf16[32,3584]{1,0:T(8,128)(2,1)S(1)}, bf16[32,3584]{1,0:T(8,128)(2,1)S(1)}, bf1...) custom-call(bf16[512,256]{1,0:T(8,128)(2,1)S(1)} %copy.10.refs_0_, ...), custom_call_target="tpu_custom_call" | custom-call | tf_op jit(solution)/shard_map/fit/pallas_call | solution.py:270
  52.3 0.3 collective-permute-start.15
  52.6 0.3 collective-permute-start.16
  52.9 0.2 collective-permute-start.17
  53.1 0.3 collective-permute-start.18
  53.4 0.5 collective-permute-done.15.refs_1_
  53.9 0.3 collective-permute-done.16.refs_2_
  54.2 0.3 collective-permute-done.17.refs_3_
  54.5 0.3 collective-permute-done.18.refs_4_
  54.8 0.5 chip_sum.3
  55.3 1.3 %collective-permute-start.22 = (bf16[64,3584]{1,0:T(8,128)(2,1)S(1)}, bf16[64,3584]{1,0:T(8,128)(2,1)S(1)}, u32[]{:S(2)}, u32[]{:S(2)}) collective-permute-start(bf16[64,3584]{1,0:T(8,128)(2,1)S(1)} %get-tuple-element.75), channel_id=1, source_target_pairs={{0,2},{1,3},{2,0},{3,1},{4,6},{5,7},{6,4},{7,5},{8,10},{9,11},{10,... | collective-permute-start | bytes 1376264 | tf_op jit(solution)/shard_map/ppermute | solution.py:252
  56.6 3.2 %fetch.2 = (bf16[2,1024,1792]{2,1,0:T(8,128)(2,1)S(1)}, f32[8,128]{1,0:T(8,128)S(1)}) custom-call(bf16[1024,7168]{1,0:T(8,128)(2,1)} %bitcast.9, f32[64,3584]{1,0:T(8,128)S(1)} %get-tuple-element.68.refs_1_.refs_0_), custom_call_target="tpu_custom_call" | custom-call | bytes 14680064 | tf_op jit(solution)/shard_map/fetch/pallas_call | solution.py:270
  59.8 0.0 collective-permute-done.14.refs_1_
  59.8 0.3 plane_sum.2
  60.1 2.4 %collective-permute-start.19 = (bf16[16,3584]{1,0:T(8,128)(2,1)S(1)}, bf16[16,3584]{1,0:T(8,128)(2,1)S(1)}, u32[]{:S(2)}, u32[]{:S(2)}) collective-permute-start(bf16[16,3584]{1,0:T(8,128)(2,1)S(1)} %get-tuple-element.70), channel_id=1, source_target_pairs={{0,12},{1,13},{2,14},{3,15},{4,8},{5,9},{6,10},{7,11},{8,4},{9,5},... | collective-permute-start | bytes 344072 | tf_op jit(solution)/shard_map/ppermute | solution.py:252
  62.5 1.2 %convolution_multiply_fusion.refs_2_ = f32[512,256]{1,0:T(8,128)} fusion(f32[512,256]{1,0:T(8,128)S(1)} %get-tuple-element.60, s32[256]{0:T(256)S(1)} %fusion.6), kind=kOutput, calls=%fused_computation | convolution fusion | flops 402849792 | bytes 1049600 | tf_op jit(solution)/shard_map/dot_general | solution.py:498
  63.7 2.1 %collective-permute-start.21 = (bf16[16,3584]{1,0:T(8,128)(2,1)S(1)}, bf16[16,3584]{1,0:T(8,128)(2,1)S(1)}, u32[]{:S(2)}, u32[]{:S(2)}) collective-permute-start(bf16[16,3584]{1,0:T(8,128)(2,1)S(1)} %get-tuple-element.72), channel_id=1, source_target_pairs={{0,4},{1,5},{2,6},{3,7},{4,0},{5,1},{6,2},{7,3},{8,12},{9,13},{10,... | collective-permute-start | bytes 344072 | tf_op jit(solution)/shard_map/ppermute | solution.py:252
  65.8 3.2 %fetch.3 = (bf16[2,1024,1792]{2,1,0:T(8,128)(2,1)S(1)}, f32[8,128]{1,0:T(8,128)S(1)}) custom-call(bf16[1024,7168]{1,0:T(8,128)(2,1)} %bitcast.10, bf16[16,3584]{1,0:T(8,128)(2,1)S(1)} %get-tuple-element.73.refs_1_.refs_5_.refs_4_, f32[512,256]{1,0:T(8,128)} %convolution_multiply_fusion.refs_2_), custom_call_target="tpu_custom_call" | custom-call | bytes 14680064 | tf_op jit(solution)/shard_map/fetch/pallas_call | solution.py:270
  69.0 0.3 plane_sum.3
  69.3 2.4 %collective-permute-start.23 = (bf16[16,3584]{1,0:T(8,128)(2,1)S(1)}, bf16[16,3584]{1,0:T(8,128)(2,1)S(1)}, u32[]{:S(2)}, u32[]{:S(2)}) collective-permute-start(bf16[16,3584]{1,0:T(8,128)(2,1)S(1)} %get-tuple-element.79), channel_id=1, source_target_pairs={{0,12},{1,13},{2,14},{3,15},{4,8},{5,9},{6,10},{7,11},{8,4},{9,5},... | collective-permute-start | bytes 344072 | tf_op jit(solution)/shard_map/ppermute | solution.py:252
  71.6 2.1 %collective-permute-start.25 = (bf16[16,3584]{1,0:T(8,128)(2,1)S(1)}, bf16[16,3584]{1,0:T(8,128)(2,1)S(1)}, u32[]{:S(2)}, u32[]{:S(2)}) collective-permute-start(bf16[16,3584]{1,0:T(8,128)(2,1)S(1)} %get-tuple-element.81), channel_id=1, source_target_pairs={{0,4},{1,5},{2,6},{3,7},{4,0},{5,1},{6,2},{7,3},{8,12},{9,13},{10,... | collective-permute-start | bytes 344072 | tf_op jit(solution)/shard_map/ppermute | solution.py:252
  73.7 3.0 %inner.2.refs_5_ = f32[4,64]{1,0:T(4,128)S(1)} custom-call(s32[1]{0:T(128)} %bitcast.1.refs_0_, bf16[2,1024,1792]{2,1,0:T(8,128)(2,1)S(1)} %get-tuple-element.74.refs_1_, bf16[16,3584]{1,0:T(8,128)(2,1)S(1)} %collective-permute-done.19.refs_2_.refs_1_, bf16[16,3584]{1,0:T(8,128)(2,1)S(1)} %collective-permute-done.20.refs_3_.refs_2_, ...), custom_call_target="tpu_custom_call" | custom-call | tf_op jit(solution)/shard_map/inner/pallas_call | solution.py:270
  76.8 4.2 %basis.3 = (bf16[1024,7168]{1,0:T(8,128)(2,1)}, f32[8,128]{1,0:T(8,128)S(1)}) custom-call(bf16[1024,64]{1,0:T(8,128)(2,1)S(1)} %get-tuple-element.61.refs_0_, bf16[16,3584]{1,0:T(8,128)(2,1)S(1)} %collective-permute-done.19.refs_2_.refs_1_, bf16[16,3584]{1,0:T(8,128)(2,1)S(1)} %collective-permute-done.20.refs_3_.refs_2_, ...), custom_call_target="tpu_custom_call" | custom-call | tf_op jit(solution)/shard_map/basis/pallas_call | solution.py:270
  81.0 0.8 collective-permute-done.24.refs_3_
  81.8 3.0 %inner.3 = f32[4,64]{1,0:T(4,128)S(1)} custom-call(s32[1]{0:T(128)} %bitcast.1.refs_0_, bf16[2,1024,1792]{2,1,0:T(8,128)(2,1)S(1)} %get-tuple-element.82.refs_1_, bf16[16,3584]{1,0:T(8,128)(2,1)S(1)} %collective-permute-done.23.refs_2_, bf16[16,3584]{1,0:T(8,128)(2,1)S(1)} %collective-permute-done.24.refs_3_, ...), custom_call_target="tpu_custom_call" | custom-call | tf_op jit(solution)/shard_map/inner/pallas_call | solution.py:270
  84.9 0.2 collective-permute-start.28
  85.1 1.2 %collective-permute-start.27 = (f32[4,64]{1,0:T(4,128)S(1)}, f32[4,64]{1,0:T(4,128)S(1)}, u32[]{:S(2)}, u32[]{:S(2)}) collective-permute-start(f32[4,64]{1,0:T(4,128)S(1)} %add.74.refs_6_.refs_3_), channel_id=1, source_target_pairs={{0,2},{1,3},{2,0},{3,1},{4,6},{5,7},{6,4},{7,5},{8,10},{9,11},{10,... | collective-permute-start | bytes 3080 | tf_op jit(solution)/shard_map/ppermute | solution.py:252
  86.2 0.5 collective-permute-start.26
  86.8 2.5 %basis.4 = (bf16[1024,7168]{1,0:T(8,128)(2,1)}, f32[8,128]{1,0:T(8,128)S(1)}) custom-call(bf16[1024,64]{1,0:T(8,128)(2,1)S(1)} %get-tuple-element.61.refs_0_, bf16[1024,7168]{1,0:T(8,128)(2,1)} %get-tuple-element.78.refs_1_, bf16[16,3584]{1,0:T(8,128)(2,1)S(1)} %collective-permute-done.23.refs_2_, ...), custom_call_target="tpu_custom_call", output_to_operand_aliasing={{0}: (1, {})} | custom-call | tf_op jit(solution)/shard_map/basis/pallas_call | solution.py:270
  89.3 2.2 %collective-permute-start.31 = (f32[4,64]{1,0:T(4,128)S(1)}, f32[4,64]{1,0:T(4,128)S(1)}, u32[]{:S(2)}, u32[]{:S(2)}) collective-permute-start(f32[4,64]{1,0:T(4,128)S(1)} %add.103.refs_6_.refs_3_), channel_id=1, source_target_pairs={{0,12},{1,13},{2,14},{3,15},{4,8},{5,9},{6,10},{7,11},{8,4},{9,5},... | collective-permute-start | bytes 3080 | tf_op jit(solution)/shard_map/ppermute | solution.py:252
  91.6 2.2 %collective-permute-start.29 = (f32[4,64]{1,0:T(4,128)S(1)}, f32[4,64]{1,0:T(4,128)S(1)}, u32[]{:S(2)}, u32[]{:S(2)}) collective-permute-start(f32[4,64]{1,0:T(4,128)S(1)} %add.103.refs_6_.refs_3_), channel_id=1, source_target_pairs={{0,4},{1,5},{2,6},{3,7},{4,0},{5,1},{6,2},{7,3},{8,12},{9,13},{10,... | collective-permute-start | bytes 3080 | tf_op jit(solution)/shard_map/ppermute | solution.py:252
  93.8 2.5 %basis.5 = (bf16[1024,7168]{1,0:T(8,128)(2,1)}, f32[8,128]{1,0:T(8,128)S(1)}) custom-call(bf16[1024,64]{1,0:T(8,128)(2,1)S(1)} %get-tuple-element.61.refs_0_, bf16[1024,7168]{1,0:T(8,128)(2,1)} %get-tuple-element.84.refs_1_, bf16[16,3584]{1,0:T(8,128)(2,1)S(1)} %collective-permute-done.23.refs_2_, ...), custom_call_target="tpu_custom_call", output_to_operand_aliasing={{0}: (1, {})} | custom-call | tf_op jit(solution)/shard_map/basis/pallas_call | solution.py:270
  96.3 0.6 add.104
  (31 shorter events, 0.2 us)
Async XLA Ops:
  0.6 33.6 %copy-start = (bf16[512,256]{1,0:T(8,128)(2,1)S(1)}, bf16[512,256]{1,0:T(8,128)(2,1)}, u32[]{:S(2)}) copy-start(bf16[512,256]{1,0:T(8,128)(2,1)} %param.5) | copy-start | bytes 786436
  0.7 0.7 copy-start.2
  5.4 9.4 %collective-permute-start.3 = (bf16[16,3584]{1,0:T(8,128)(2,1)S(1)}, bf16[16,3584]{1,0:T(8,128)(2,1)S(1)}, u32[]{:S(2)}, u32[]{:S(2)}) collective-permute-start(bf16[16,3584]{1,0:T(8,128)(2,1)S(1)} %get-tuple-element.52), channel_id=1, source_target_pairs={{0,12},{1,13},{2,14},{3,15},{4,8},{5,9},{6,10},{7,11},{8,4},{9,5},... | collective-permute-start | bytes 344072 | tf_op jit(solution)/shard_map/ppermute | solution.py:252
  10.5 9.7 %collective-permute-start.4 = (bf16[16,3584]{1,0:T(8,128)(2,1)S(1)}, bf16[16,3584]{1,0:T(8,128)(2,1)S(1)}, u32[]{:S(2)}, u32[]{:S(2)}) collective-permute-start(bf16[16,3584]{1,0:T(8,128)(2,1)S(1)} %get-tuple-element.53), channel_id=1, source_target_pairs={{0,8},{1,9},{2,10},{3,11},{4,12},{5,13},{6,14},{7,15},{8,0},{9,1},... | collective-permute-start | bytes 344072 | tf_op jit(solution)/shard_map/ppermute | solution.py:252
  10.5 9.7 %collective-permute-start.5 = (bf16[16,3584]{1,0:T(8,128)(2,1)S(1)}, bf16[16,3584]{1,0:T(8,128)(2,1)S(1)}, u32[]{:S(2)}, u32[]{:S(2)}) collective-permute-start(bf16[16,3584]{1,0:T(8,128)(2,1)S(1)} %get-tuple-element.54), channel_id=1, source_target_pairs={{0,4},{1,5},{2,6},{3,7},{4,0},{5,1},{6,2},{7,3},{8,12},{9,13},{10,... | collective-permute-start | bytes 344072 | tf_op jit(solution)/shard_map/ppermute | solution.py:252
  20.2 11.6 %collective-permute-start.9 = (bf16[64,3584]{1,0:T(8,128)(2,1)S(1)}, bf16[64,3584]{1,0:T(8,128)(2,1)S(1)}, u32[]{:S(2)}, u32[]{:S(2)}) collective-permute-start(bf16[64,3584]{1,0:T(8,128)(2,1)S(1)} %join.2.refs_4_.refs_3_), channel_id=1, source_target_pairs={{0,2},{1,3},{2,0},{3,1},{4,6},{5,7},{6,4},{7,5},{8,10},{9,11},{10,... | collective-permute-start | bytes 1376264 | tf_op jit(solution)/shard_map/ppermute | solution.py:252
  21.8 10.1 %collective-permute-start = (bf16[16,3584]{1,0:T(8,128)(2,1)S(1)}, bf16[16,3584]{1,0:T(8,128)(2,1)S(1)}, u32[]{:S(2)}, u32[]{:S(2)}) collective-permute-start(bf16[16,3584]{1,0:T(8,128)(2,1)S(1)} %get-tuple-element.48), channel_id=1, source_target_pairs={{0,12},{1,13},{2,14},{3,15},{4,8},{5,9},{6,10},{7,11},{8,4},{9,5},... | collective-permute-start | bytes 344072 | tf_op jit(solution)/shard_map/ppermute | solution.py:252
  24.3 9.3 %collective-permute-start.1 = (bf16[16,3584]{1,0:T(8,128)(2,1)S(1)}, bf16[16,3584]{1,0:T(8,128)(2,1)S(1)}, u32[]{:S(2)}, u32[]{:S(2)}) collective-permute-start(bf16[16,3584]{1,0:T(8,128)(2,1)S(1)} %get-tuple-element.49), channel_id=1, source_target_pairs={{0,8},{1,9},{2,10},{3,11},{4,12},{5,13},{6,14},{7,15},{8,0},{9,1},... | collective-permute-start | bytes 344072 | tf_op jit(solution)/shard_map/ppermute | solution.py:252
  24.3 9.3 %collective-permute-start.2 = (bf16[16,3584]{1,0:T(8,128)(2,1)S(1)}, bf16[16,3584]{1,0:T(8,128)(2,1)S(1)}, u32[]{:S(2)}, u32[]{:S(2)}) collective-permute-start(bf16[16,3584]{1,0:T(8,128)(2,1)S(1)} %get-tuple-element.50), channel_id=1, source_target_pairs={{0,4},{1,5},{2,6},{3,7},{4,0},{5,1},{6,2},{7,3},{8,12},{9,13},{10,... | collective-permute-start | bytes 344072 | tf_op jit(solution)/shard_map/ppermute | solution.py:252
  26.2 8.4 %collective-permute-start.10 = (bf16[64,3584]{1,0:T(8,128)(2,1)S(1)}, bf16[64,3584]{1,0:T(8,128)(2,1)S(1)}, u32[]{:S(2)}, u32[]{:S(2)}) collective-permute-start(bf16[64,3584]{1,0:T(8,128)(2,1)S(1)} %join.2.refs_4_.refs_3_), channel_id=1, source_target_pairs={{0,1},{1,0},{2,3},{3,2},{4,5},{5,4},{6,7},{7,6},{8,9},{9,8},{10,11... | collective-permute-start | bytes 1376264 | tf_op jit(solution)/shard_map/ppermute | solution.py:252
  31.9 2.8 %collective-permute-start.11 = (bf16[64,3584]{1,0:T(8,128)(2,1)S(1)}, bf16[64,3584]{1,0:T(8,128)(2,1)S(1)}, u32[]{:S(2)}, u32[]{:S(2)}) collective-permute-start(bf16[64,3584]{1,0:T(8,128)(2,1)S(1)} %collective-permute-done.9.refs_4_), channel_id=1, source_target_pairs={{0,1},{1,0},{2,3},{3,2},{4,5},{5,4},{6,7},{7,6},{8,9},{9,8},{10,11... | collective-permute-start | bytes 1376264 | tf_op jit(solution)/shard_map/ppermute | solution.py:252
  33.6 11.6 %collective-permute-start.6 = (bf16[64,3584]{1,0:T(8,128)(2,1)S(1)}, bf16[64,3584]{1,0:T(8,128)(2,1)S(1)}, u32[]{:S(2)}, u32[]{:S(2)}) collective-permute-start(bf16[64,3584]{1,0:T(8,128)(2,1)S(1)} %join.3.refs_7_.refs_3_), channel_id=1, source_target_pairs={{0,2},{1,3},{2,0},{3,1},{4,6},{5,7},{6,4},{7,5},{8,10},{9,11},{10,... | collective-permute-start | bytes 1376264 | tf_op jit(solution)/shard_map/ppermute | solution.py:252
  39.9 5.3 %collective-permute-start.12 = (bf16[64,3584]{1,0:T(8,128)(2,1)S(1)}, bf16[64,3584]{1,0:T(8,128)(2,1)S(1)}, u32[]{:S(2)}, u32[]{:S(2)}) collective-permute-start(bf16[64,3584]{1,0:T(8,128)(2,1)S(1)} %get-tuple-element.57), channel_id=1, source_target_pairs={{0,1},{1,0},{2,3},{3,2},{4,5},{5,4},{6,7},{7,6},{8,9},{9,8},{10,11... | collective-permute-start | bytes 1376264 | tf_op jit(solution)/shard_map/ppermute | solution.py:252
  40.0 5.3 %collective-permute-start.13 = (bf16[64,3584]{1,0:T(8,128)(2,1)S(1)}, bf16[64,3584]{1,0:T(8,128)(2,1)S(1)}, u32[]{:S(2)}, u32[]{:S(2)}) collective-permute-start(bf16[64,3584]{1,0:T(8,128)(2,1)S(1)} %get-tuple-element.58), channel_id=1, source_target_pairs={{0,1},{1,0},{2,3},{3,2},{4,5},{5,4},{6,7},{7,6},{8,9},{9,8},{10,11... | collective-permute-start | bytes 1376264 | tf_op jit(solution)/shard_map/ppermute | solution.py:252
  40.5 6.6 %collective-permute-start.7 = (bf16[64,3584]{1,0:T(8,128)(2,1)S(1)}, bf16[64,3584]{1,0:T(8,128)(2,1)S(1)}, u32[]{:S(2)}, u32[]{:S(2)}) collective-permute-start(bf16[64,3584]{1,0:T(8,128)(2,1)S(1)} %join.3.refs_7_.refs_3_), channel_id=1, source_target_pairs={{0,1},{1,0},{2,3},{3,2},{4,5},{5,4},{6,7},{7,6},{8,9},{9,8},{10,11... | collective-permute-start | bytes 1376264 | tf_op jit(solution)/shard_map/ppermute | solution.py:252
  45.2 1.8 %collective-permute-start.8 = (bf16[64,3584]{1,0:T(8,128)(2,1)S(1)}, bf16[64,3584]{1,0:T(8,128)(2,1)S(1)}, u32[]{:S(2)}, u32[]{:S(2)}) collective-permute-start(bf16[64,3584]{1,0:T(8,128)(2,1)S(1)} %collective-permute-done.6.refs_4_), channel_id=1, source_target_pairs={{0,1},{1,0},{2,3},{3,2},{4,5},{5,4},{6,7},{7,6},{8,9},{9,8},{10,11... | collective-permute-start | bytes 1376264 | tf_op jit(solution)/shard_map/ppermute | solution.py:252
  45.7 14.1 %collective-permute-start.14 = (bf16[64,3584]{1,0:T(8,128)(2,1)S(1)}, bf16[64,3584]{1,0:T(8,128)(2,1)S(1)}, u32[]{:S(2)}, u32[]{:S(2)}) collective-permute-start(bf16[64,3584]{1,0:T(8,128)(2,1)S(1)} %get-tuple-element.62), channel_id=1, source_target_pairs={{0,2},{1,3},{2,0},{3,1},{4,6},{5,7},{6,4},{7,5},{8,10},{9,11},{10,... | collective-permute-start | bytes 1376264 | tf_op jit(solution)/shard_map/ppermute | solution.py:252
  52.3 1.6 %collective-permute-start.15 = (bf16[32,3584]{1,0:T(8,128)(2,1)S(1)}, bf16[32,3584]{1,0:T(8,128)(2,1)S(1)}, u32[]{:S(2)}, u32[]{:S(2)}) collective-permute-start(bf16[32,3584]{1,0:T(8,128)(2,1)S(1)} %get-tuple-element.64), channel_id=1, source_target_pairs={{0,1},{1,0},{2,3},{3,2},{4,5},{5,4},{6,7},{7,6},{8,9},{9,8},{10,11... | collective-permute-start | bytes 688136 | tf_op jit(solution)/shard_map/ppermute | solution.py:252
  52.6 1.6 %collective-permute-start.16 = (bf16[32,3584]{1,0:T(8,128)(2,1)S(1)}, bf16[32,3584]{1,0:T(8,128)(2,1)S(1)}, u32[]{:S(2)}, u32[]{:S(2)}) collective-permute-start(bf16[32,3584]{1,0:T(8,128)(2,1)S(1)} %get-tuple-element.65), channel_id=1, source_target_pairs={{0,1},{1,0},{2,3},{3,2},{4,5},{5,4},{6,7},{7,6},{8,9},{9,8},{10,11... | collective-permute-start | bytes 688136 | tf_op jit(solution)/shard_map/ppermute | solution.py:252
  52.9 1.6 %collective-permute-start.17 = (bf16[32,3584]{1,0:T(8,128)(2,1)S(1)}, bf16[32,3584]{1,0:T(8,128)(2,1)S(1)}, u32[]{:S(2)}, u32[]{:S(2)}) collective-permute-start(bf16[32,3584]{1,0:T(8,128)(2,1)S(1)} %get-tuple-element.66), channel_id=1, source_target_pairs={{0,1},{1,0},{2,3},{3,2},{4,5},{5,4},{6,7},{7,6},{8,9},{9,8},{10,11... | collective-permute-start | bytes 688136 | tf_op jit(solution)/shard_map/ppermute | solution.py:252
  53.1 1.8 %collective-permute-start.18 = (bf16[32,3584]{1,0:T(8,128)(2,1)S(1)}, bf16[32,3584]{1,0:T(8,128)(2,1)S(1)}, u32[]{:S(2)}, u32[]{:S(2)}) collective-permute-start(bf16[32,3584]{1,0:T(8,128)(2,1)S(1)} %get-tuple-element.67), channel_id=1, source_target_pairs={{0,1},{1,0},{2,3},{3,2},{4,5},{5,4},{6,7},{7,6},{8,9},{9,8},{10,11... | collective-permute-start | bytes 688136 | tf_op jit(solution)/shard_map/ppermute | solution.py:252
  55.3 13.6 %collective-permute-start.22 = (bf16[64,3584]{1,0:T(8,128)(2,1)S(1)}, bf16[64,3584]{1,0:T(8,128)(2,1)S(1)}, u32[]{:S(2)}, u32[]{:S(2)}) collective-permute-start(bf16[64,3584]{1,0:T(8,128)(2,1)S(1)} %get-tuple-element.75), channel_id=1, source_target_pairs={{0,2},{1,3},{2,0},{3,1},{4,6},{5,7},{6,4},{7,5},{8,10},{9,11},{10,... | collective-permute-start | bytes 1376264 | tf_op jit(solution)/shard_map/ppermute | solution.py:252
  60.1 11.5 %collective-permute-start.19 = (bf16[16,3584]{1,0:T(8,128)(2,1)S(1)}, bf16[16,3584]{1,0:T(8,128)(2,1)S(1)}, u32[]{:S(2)}, u32[]{:S(2)}) collective-permute-start(bf16[16,3584]{1,0:T(8,128)(2,1)S(1)} %get-tuple-element.70), channel_id=1, source_target_pairs={{0,12},{1,13},{2,14},{3,15},{4,8},{5,9},{6,10},{7,11},{8,4},{9,5},... | collective-permute-start | bytes 344072 | tf_op jit(solution)/shard_map/ppermute | solution.py:252
  63.7 10.1 %collective-permute-start.20 = (bf16[16,3584]{1,0:T(8,128)(2,1)S(1)}, bf16[16,3584]{1,0:T(8,128)(2,1)S(1)}, u32[]{:S(2)}, u32[]{:S(2)}) collective-permute-start(bf16[16,3584]{1,0:T(8,128)(2,1)S(1)} %get-tuple-element.71), channel_id=1, source_target_pairs={{0,8},{1,9},{2,10},{3,11},{4,12},{5,13},{6,14},{7,15},{8,0},{9,1},... | collective-permute-start | bytes 344072 | tf_op jit(solution)/shard_map/ppermute | solution.py:252
  63.7 10.1 %collective-permute-start.21 = (bf16[16,3584]{1,0:T(8,128)(2,1)S(1)}, bf16[16,3584]{1,0:T(8,128)(2,1)S(1)}, u32[]{:S(2)}, u32[]{:S(2)}) collective-permute-start(bf16[16,3584]{1,0:T(8,128)(2,1)S(1)} %get-tuple-element.72), channel_id=1, source_target_pairs={{0,4},{1,5},{2,6},{3,7},{4,0},{5,1},{6,2},{7,3},{8,12},{9,13},{10,... | collective-permute-start | bytes 344072 | tf_op jit(solution)/shard_map/ppermute | solution.py:252
  69.3 11.7 %collective-permute-start.23 = (bf16[16,3584]{1,0:T(8,128)(2,1)S(1)}, bf16[16,3584]{1,0:T(8,128)(2,1)S(1)}, u32[]{:S(2)}, u32[]{:S(2)}) collective-permute-start(bf16[16,3584]{1,0:T(8,128)(2,1)S(1)} %get-tuple-element.79), channel_id=1, source_target_pairs={{0,12},{1,13},{2,14},{3,15},{4,8},{5,9},{6,10},{7,11},{8,4},{9,5},... | collective-permute-start | bytes 344072 | tf_op jit(solution)/shard_map/ppermute | solution.py:252
  71.6 10.2 %collective-permute-start.24 = (bf16[16,3584]{1,0:T(8,128)(2,1)S(1)}, bf16[16,3584]{1,0:T(8,128)(2,1)S(1)}, u32[]{:S(2)}, u32[]{:S(2)}) collective-permute-start(bf16[16,3584]{1,0:T(8,128)(2,1)S(1)} %get-tuple-element.80), channel_id=1, source_target_pairs={{0,8},{1,9},{2,10},{3,11},{4,12},{5,13},{6,14},{7,15},{8,0},{9,1},... | collective-permute-start | bytes 344072 | tf_op jit(solution)/shard_map/ppermute | solution.py:252
  71.6 10.2 %collective-permute-start.25 = (bf16[16,3584]{1,0:T(8,128)(2,1)S(1)}, bf16[16,3584]{1,0:T(8,128)(2,1)S(1)}, u32[]{:S(2)}, u32[]{:S(2)}) collective-permute-start(bf16[16,3584]{1,0:T(8,128)(2,1)S(1)} %get-tuple-element.81), channel_id=1, source_target_pairs={{0,4},{1,5},{2,6},{3,7},{4,0},{5,1},{6,2},{7,3},{8,12},{9,13},{10,... | collective-permute-start | bytes 344072 | tf_op jit(solution)/shard_map/ppermute | solution.py:252
  84.9 4.5 %collective-permute-start.28 = (f32[4,64]{1,0:T(4,128)S(1)}, f32[4,64]{1,0:T(4,128)S(1)}, u32[]{:S(2)}, u32[]{:S(2)}) collective-permute-start(f32[4,64]{1,0:T(4,128)S(1)} %add.74.refs_6_.refs_3_), channel_id=1, source_target_pairs={{0,3},{1,2},{2,1},{3,0},{4,7},{5,6},{6,5},{7,4},{8,11},{9,10},{10,... | collective-permute-start | bytes 3080 | tf_op jit(solution)/shard_map/ppermute | solution.py:252
  85.1 4.3 %collective-permute-start.27 = (f32[4,64]{1,0:T(4,128)S(1)}, f32[4,64]{1,0:T(4,128)S(1)}, u32[]{:S(2)}, u32[]{:S(2)}) collective-permute-start(f32[4,64]{1,0:T(4,128)S(1)} %add.74.refs_6_.refs_3_), channel_id=1, source_target_pairs={{0,2},{1,3},{2,0},{3,1},{4,6},{5,7},{6,4},{7,5},{8,10},{9,11},{10,... | collective-permute-start | bytes 3080 | tf_op jit(solution)/shard_map/ppermute | solution.py:252
  86.2 3.1 %collective-permute-start.26 = (f32[4,64]{1,0:T(4,128)S(1)}, f32[4,64]{1,0:T(4,128)S(1)}, u32[]{:S(2)}, u32[]{:S(2)}) collective-permute-start(f32[4,64]{1,0:T(4,128)S(1)} %add.74.refs_6_.refs_3_), channel_id=1, source_target_pairs={{0,1},{1,0},{2,3},{3,2},{4,5},{5,4},{6,7},{7,6},{8,9},{9,8},{10,11... | collective-permute-start | bytes 3080 | tf_op jit(solution)/shard_map/ppermute | solution.py:252
  89.3 7.0 %collective-permute-start.31 = (f32[4,64]{1,0:T(4,128)S(1)}, f32[4,64]{1,0:T(4,128)S(1)}, u32[]{:S(2)}, u32[]{:S(2)}) collective-permute-start(f32[4,64]{1,0:T(4,128)S(1)} %add.103.refs_6_.refs_3_), channel_id=1, source_target_pairs={{0,12},{1,13},{2,14},{3,15},{4,8},{5,9},{6,10},{7,11},{8,4},{9,5},... | collective-permute-start | bytes 3080 | tf_op jit(solution)/shard_map/ppermute | solution.py:252
  91.6 4.8 %collective-permute-start.30 = (f32[4,64]{1,0:T(4,128)S(1)}, f32[4,64]{1,0:T(4,128)S(1)}, u32[]{:S(2)}, u32[]{:S(2)}) collective-permute-start(f32[4,64]{1,0:T(4,128)S(1)} %add.103.refs_6_.refs_3_), channel_id=1, source_target_pairs={{0,8},{1,9},{2,10},{3,11},{4,12},{5,13},{6,14},{7,15},{8,0},{9,1},... | collective-permute-start | bytes 3080 | tf_op jit(solution)/shard_map/ppermute | solution.py:252
  91.6 4.8 %collective-permute-start.29 = (f32[4,64]{1,0:T(4,128)S(1)}, f32[4,64]{1,0:T(4,128)S(1)}, u32[]{:S(2)}, u32[]{:S(2)}) collective-permute-start(f32[4,64]{1,0:T(4,128)S(1)} %add.103.refs_6_.refs_3_), channel_id=1, source_target_pairs={{0,4},{1,5},{2,6},{3,7},{4,0},{5,1},{6,2},{7,3},{8,12},{9,13},{10,... | collective-permute-start | bytes 3080 | tf_op jit(solution)/shard_map/ppermute | solution.py:252
  93.8 3.1 %copy-start.1 = (bf16[512,256]{1,0:T(8,128)(2,1)S(1)}, bf16[512,256]{1,0:T(8,128)(2,1)}, u32[]{:S(2)}) copy-start(bf16[512,256]{1,0:T(8,128)(2,1)} %param.5) | copy-start | bytes 786436

commit v5 on v4

--- a/solution.py
+++ b/solution.py
@@ -12,6 +12,7 @@
 HIGHEST = lax.Precision.HIGHEST
 SHARES = (1, 1)
 LAG = 1
+READY = (1, 2)
 LARGE = 2048
 FAR = (2, 4)
 FB = (0, 1)
@@ -160,25 +161,38 @@
         out_ref[...] = total[j * rows : (j + 1) * rows].astype(BF16)
 
 
-def inner_kernel(rows, experts, start, place_ref, bases_ref, *refs):
-    if start is None:
-        *sum_refs, inner_ref, acc_ref = refs
-        held = bases_ref[0]
-    else:
-        *sum_refs, inner_ref, acc_ref, held_ref, sems = refs
-        held = streamed(start, bases_ref, held_ref, sems)
+def inner_kernel(rows, experts, start, ready, steps, place_ref, bases_ref, *refs):
+    if ready:
+        ready_ref, *refs = refs
+    if ready < steps:
+        *refs, held_ref, sems = refs
+    *sum_refs, inner_ref, acc_ref = refs
     summed = jnp.concatenate([ref[...] for ref in by_place(sum_refs)], axis=0)
-    step = lax.dot_general(
-        summed, held, (((1,), (1,)), ((), ())), preferred_element_type=F32
-    )
-
-    @pl.when(pl.program_id(0) == 0)
-    def _():
-        acc_ref[...] = step
-
-    @pl.when(pl.program_id(0) > 0)
-    def _():
-        acc_ref[...] += step
+    step = pl.program_id(0)
+
+    def copy(at):
+        block = held_ref.shape[2]
+        column = start + at * block
+        return pltpu.make_async_copy(
+            bases_ref.at[:, column : column + block], held_ref.at[at - ready], sems.at[at - ready]
+        )
+
+    for at in range(steps):
+
+        @pl.when(step == at)
+        def _(at=at):
+            if at == 0:
+                for later in range(ready, steps):
+                    copy(later).start()
+            if at < ready:
+                held = ready_ref[at]
+            else:
+                copy(at).wait()
+                held = held_ref[at - ready]
+            product = lax.dot_general(
+                summed, held, (((1,), (1,)), ((), ())), preferred_element_type=F32
+            )
+            acc_ref[...] = product if at == 0 else acc_ref[...] + product
 
     @pl.when(pl.program_id(0) == pl.num_programs(0) - 1)
     def _():
@@ -289,8 +303,10 @@
         size = size or block
         return column_spec(rows_in, size, start // size)
 
-    def held(j, rows_in, size):
-        steps = widths[j] // size
+    def held(j, rows_in, size, ready=0):
+        steps = widths[j] // size - ready
+        if not steps:
+            return []
         return [pltpu.VMEM((steps, rows_in, size), BF16), pltpu.SemaphoreType.DMA((steps,))]
 
     flat = bases.reshape(wide, width)
@@ -350,14 +366,14 @@
         return FAR[min(j, len(FAR) - 1)]
 
     def fetch(j, source, after):
-        steps, rows_in = widths[j] // block, source.shape[0]
+        steps, rows_in = min(READY[j], widths[j] // block), source.shape[0]
         return call(
             functools.partial(fetch_kernel, starts[j]),
             "fetch",
             [(source, hbm)],
             [(shape(steps, rows_in, block), vmem), (shape(8, 128, dtype=F32), vmem)],
             after=after,
-            bytes_accessed=FETCH_COST * 4 * rows_in * widths[j],
+            bytes_accessed=FETCH_COST * 4 * rows_in * block * steps,
             scratch_shapes=[pltpu.SemaphoreType.DMA((steps,))],
         )
 
@@ -422,15 +438,14 @@
         return [(sums[k], col(tall // len(sums))) for k in far_first(len(sums))]
 
     def inner_chunk(j, sums, after, fetched=None):
-        there = fetched is not None
+        ready = 0 if fetched is None else fetched.shape[0]
         return call(
-            functools.partial(inner_kernel, rows, experts, None if there else starts[j]),
+            functools.partial(inner_kernel, rows, experts, starts[j], ready, widths[j] // block),
             "inner",
             [
                 (place, smem),
-                (fetched, pl.BlockSpec((1, wide, block), lambda s: (s, 0, 0)))
-                if there
-                else (flat, hbm),
+                (flat, hbm),
+                *([(fetched, vmem)] if ready else []),
                 *sums_of(sums),
             ],
             [(shape(experts, num_bases, dtype=F32), whole_spec((experts, num_bases)))],
@@ -438,7 +453,7 @@
             after,
             FLOPS * 2 * tall * wide * widths[j],
             FLOPS * 2 * wide * widths[j],
-            scratch_shapes=[pltpu.VMEM((tall, wide), F32), *([] if there else held(j, wide, block))],
+            scratch_shapes=[pltpu.VMEM((tall, wide), F32), *held(j, wide, block, ready)],
         )[0]
 
     def basis_chunk(j, sums, before, after, first=0, last=None):

time: 97.1 us -> 96.5 us (level)
  transfers between devices with their start and end apart: 32 -> 32, of which waited for: 9 -> 10; matrix products, arithmetic and copies ran while one was open for 2% -> 2% of each run, Pallas kernels for 35% -> 35%
where the time goes in v5:
time: 96.5 us; the launch traced here: 96.3 us
  Pallas kernels  41.5 us (43%)
  starting transfers between devices  31.9 us (33%)
  waiting for transfers between devices  19.6 us (20%)
  matrix products  1.48 us (2%)
    pallas_call x20, Pallas kernels, call(): pl.pallas_call(body, out_shape=[shape for shape, _ in outs], in_specs=[sp...  41.5 us
    ppermute x32, starting transfers between devices, send(): return lax.ppermute(x, 'expert', [(i, i ^ flip) for i in range(devices)])  31.9 us
    ppermute x32, waiting for transfers between devices, send(): return lax.ppermute(x, 'expert', [(i, i ^ flip) for i in range(devices)])  19.6 us
  transfers between devices with their start and end apart: 32, of which 10 were waited for; matrix products, arithmetic and copies ran while one was open for 2% of the time, Pallas kernels for 35%

profile of v5, /device:TPU:0, one launch (start us, length us, event | category | flops | bytes accessed | tf_op | source)
XLA Modules:
  0.0 96.3 jit_solution(5377157755113975434)
XLA Ops:
  0.6 0.0 copy-start
  0.7 0.7 copy-done.2
  1.4 0.3 spread.1
  1.7 3.7 %mix.2 = (bf16[16,3584]{1,0:T(8,128)(2,1)S(1)}, bf16[16,3584]{1,0:T(8,128)(2,1)S(1)}, bf16[16,3584]{1,0:T(8,128)(2,1)S(1)}, bf16[16,3584]{1,0:T(8,128)(2,1)S(1)}) custom-call(bf16[64,1024]{1,0:T(8,128)(2,1)S(1)} %get-tuple-element.46.refs_0_, bf16[1024,7168]{1,0:T(8,128)(2,1)} %bitcast.7), custom_call_target="tpu_custom_call" | custom-call | tf_op jit(solution)/shard_map/mix/pallas_call | solution.py:284
  5.4 5.1 %collective-permute-start.3 = (bf16[16,3584]{1,0:T(8,128)(2,1)S(1)}, bf16[16,3584]{1,0:T(8,128)(2,1)S(1)}, u32[]{:S(2)}, u32[]{:S(2)}) collective-permute-start(bf16[16,3584]{1,0:T(8,128)(2,1)S(1)} %get-tuple-element.52), channel_id=1, source_target_pairs={{0,12},{1,13},{2,14},{3,15},{4,8},{5,9},{6,10},{7,11},{8,4},{9,5},... | collective-permute-start | bytes 344072 | tf_op jit(solution)/shard_map/ppermute | solution.py:266
  10.5 0.6 collective-permute-start.5
  11.2 3.7 %mix.3 = (bf16[16,3584]{1,0:T(8,128)(2,1)S(1)}, bf16[16,3584]{1,0:T(8,128)(2,1)S(1)}, bf16[16,3584]{1,0:T(8,128)(2,1)S(1)}, bf16[16,3584]{1,0:T(8,128)(2,1)S(1)}) custom-call(bf16[64,1024]{1,0:T(8,128)(2,1)S(1)} %get-tuple-element.46.refs_0_, bf16[1024,7168]{1,0:T(8,128)(2,1)} %bitcast.8, bf16[16,3584]{1,0:T(8,128)(2,1)S(1)} %get-tuple-element.47.refs_2_.refs_3_), custom_call_target="tpu_custom_call" | custom-call | tf_op jit(solution)/shard_map/mix/pallas_call | solution.py:284
  14.9 0.0 collective-permute-done.3.refs_0_
  14.9 5.3 %collective-permute-done.4.refs_1_ = bf16[16,3584]{1,0:T(8,128)(2,1)S(1)} collective-permute-done((bf16[16,3584]{1,0:T(8,128)(2,1)S(1)}, bf16[16,3584]{1,0:T(8,128)(2,1)S(1)}, u32[]{:S(2)}, u32[]{:S(2)}) %collective-permute-start.4) | collective-permute-done | bytes 114720 | tf_op jit(solution)/shard_map/ppermute | solution.py:266
  20.2 1.6 %collective-permute-start.9 = (bf16[64,3584]{1,0:T(8,128)(2,1)S(1)}, bf16[64,3584]{1,0:T(8,128)(2,1)S(1)}, u32[]{:S(2)}, u32[]{:S(2)}) collective-permute-start(bf16[64,3584]{1,0:T(8,128)(2,1)S(1)} %join.2.refs_4_.refs_3_), channel_id=1, source_target_pairs={{0,2},{1,3},{2,0},{3,1},{4,6},{5,7},{6,4},{7,5},{8,10},{9,11},{10,... | collective-permute-start | bytes 1376264 | tf_op jit(solution)/shard_map/ppermute | solution.py:266
  21.8 2.5 %collective-permute-start = (bf16[16,3584]{1,0:T(8,128)(2,1)S(1)}, bf16[16,3584]{1,0:T(8,128)(2,1)S(1)}, u32[]{:S(2)}, u32[]{:S(2)}) collective-permute-start(bf16[16,3584]{1,0:T(8,128)(2,1)S(1)} %get-tuple-element.48), channel_id=1, source_target_pairs={{0,12},{1,13},{2,14},{3,15},{4,8},{5,9},{6,10},{7,11},{8,4},{9,5},... | collective-permute-start | bytes 344072 | tf_op jit(solution)/shard_map/ppermute | solution.py:266
  24.3 0.0 collective-permute-start.1
  24.3 1.9 %collective-permute-start.2 = (bf16[16,3584]{1,0:T(8,128)(2,1)S(1)}, bf16[16,3584]{1,0:T(8,128)(2,1)S(1)}, u32[]{:S(2)}, u32[]{:S(2)}) collective-permute-start(bf16[16,3584]{1,0:T(8,128)(2,1)S(1)} %get-tuple-element.50), channel_id=1, source_target_pairs={{0,4},{1,5},{2,6},{3,7},{4,0},{5,1},{6,2},{7,3},{8,12},{9,13},{10,... | collective-permute-start | bytes 344072 | tf_op jit(solution)/shard_map/ppermute | solution.py:266
  26.2 5.7 %collective-permute-done.9.refs_4_ = bf16[64,3584]{1,0:T(8,128)(2,1)S(1)} collective-permute-done((bf16[64,3584]{1,0:T(8,128)(2,1)S(1)}, bf16[64,3584]{1,0:T(8,128)(2,1)S(1)}, u32[]{:S(2)}, u32[]{:S(2)}) %collective-permute-start.9) | collective-permute-done | bytes 458784 | tf_op jit(solution)/shard_map/ppermute | solution.py:266
  31.9 0.0 collective-permute-done.refs_0_
  31.9 1.7 %collective-permute-done.1.refs_1_ = bf16[16,3584]{1,0:T(8,128)(2,1)S(1)} collective-permute-done((bf16[16,3584]{1,0:T(8,128)(2,1)S(1)}, bf16[16,3584]{1,0:T(8,128)(2,1)S(1)}, u32[]{:S(2)}, u32[]{:S(2)}) %collective-permute-start.1) | collective-permute-done | bytes 114720 | tf_op jit(solution)/shard_map/ppermute | solution.py:266
  33.6 0.6 collective-permute-start.6
  34.2 0.3 convolution_convert_fusion.refs_1_
  34.5 0.1 copy.10.refs_0_
  34.7 0.0 collective-permute-done.10.refs_5_
  34.7 0.0 collective-permute-done.11.refs_6_
  34.7 5.2 %fit.2 = (f32[128,3584]{1,0:T(8,128)S(1)}, bf16[64,3584]{1,0:T(8,128)(2,1)S(1)}, bf16[64,3584]{1,0:T(8,128)(2,1)S(1)}, f32[512,256]{1,0:T(8,128)S(1)}) custom-call(bf16[512,256]{1,0:T(8,128)(2,1)S(1)} %copy.10.refs_0_, bf16[256,512]{1,0:T(8,128)(2,1)S(1)} %convolution_convert_fusion.refs_1_, bf16[512,7168]{1,0:T(8,128)(2,1)} %refs_2_.3, ...), custom_call_target="tpu_custom_call" | custom-call | tf_op jit(solution)/shard_map/fit/pallas_call | solution.py:284
  39.9 0.1 collective-permute-start.12
  40.0 0.5 collective-permute-start.13
  40.5 0.1 collective-permute-start.7
  40.5 4.7 %collective-permute-done.6.refs_4_ = bf16[64,3584]{1,0:T(8,128)(2,1)S(1)} collective-permute-done((bf16[64,3584]{1,0:T(8,128)(2,1)S(1)}, bf16[64,3584]{1,0:T(8,128)(2,1)S(1)}, u32[]{:S(2)}, u32[]{:S(2)}) %collective-permute-start.6) | collective-permute-done | bytes 458784 | tf_op jit(solution)/shard_map/ppermute | solution.py:266
  45.2 0.5 chip_sum.2
  45.7 1.3 %collective-permute-start.14 = (bf16[64,3584]{1,0:T(8,128)(2,1)S(1)}, bf16[64,3584]{1,0:T(8,128)(2,1)S(1)}, u32[]{:S(2)}, u32[]{:S(2)}) collective-permute-start(bf16[64,3584]{1,0:T(8,128)(2,1)S(1)} %get-tuple-element.62), channel_id=1, source_target_pairs={{0,2},{1,3},{2,0},{3,1},{4,6},{5,7},{6,4},{7,5},{8,10},{9,11},{10,... | collective-permute-start | bytes 1376264 | tf_op jit(solution)/shard_map/ppermute | solution.py:266
  47.1 0.0 collective-permute-done.7.refs_5_
  47.1 0.0 collective-permute-done.8.refs_6_
  47.1 5.2 %fit.3 = (f32[128,3584]{1,0:T(8,128)S(1)}, bf16[32,3584]{1,0:T(8,128)(2,1)S(1)}, bf16[32,3584]{1,0:T(8,128)(2,1)S(1)}, bf16[32,3584]{1,0:T(8,128)(2,1)S(1)}, bf1...) custom-call(bf16[512,256]{1,0:T(8,128)(2,1)S(1)} %copy.10.refs_0_, ...), custom_call_target="tpu_custom_call" | custom-call | tf_op jit(solution)/shard_map/fit/pallas_call | solution.py:284
  52.3 0.3 collective-permute-start.15
  52.6 0.3 collective-permute-start.16
  52.9 0.2 collective-permute-start.17
  53.1 0.3 collective-permute-start.18
  53.4 0.5 collective-permute-done.15.refs_1_
  53.9 0.3 collective-permute-done.16.refs_2_
  54.2 0.3 collective-permute-done.17.refs_3_
  54.5 0.3 collective-permute-done.18.refs_4_
  54.8 0.5 chip_sum.3
  55.3 1.3 %collective-permute-start.22 = (bf16[64,3584]{1,0:T(8,128)(2,1)S(1)}, bf16[64,3584]{1,0:T(8,128)(2,1)S(1)}, u32[]{:S(2)}, u32[]{:S(2)}) collective-permute-start(bf16[64,3584]{1,0:T(8,128)(2,1)S(1)} %get-tuple-element.75), channel_id=1, source_target_pairs={{0,2},{1,3},{2,0},{3,1},{4,6},{5,7},{6,4},{7,5},{8,10},{9,11},{10,... | collective-permute-start | bytes 1376264 | tf_op jit(solution)/shard_map/ppermute | solution.py:266
  56.6 2.0 %fetch.2 = (bf16[1,1024,1792]{2,1,0:T(8,128)(2,1)S(1)}, f32[8,128]{1,0:T(8,128)S(1)}) custom-call(bf16[1024,7168]{1,0:T(8,128)(2,1)} %bitcast.9, f32[64,3584]{1,0:T(8,128)S(1)} %get-tuple-element.68.refs_1_.refs_0_), custom_call_target="tpu_custom_call" | custom-call | bytes 7340032 | tf_op jit(solution)/shard_map/fetch/pallas_call | solution.py:284
  58.7 0.4 collective-permute-done.14.refs_1_
  59.1 0.3 plane_sum.2
  59.4 2.4 %collective-permute-start.19 = (bf16[16,3584]{1,0:T(8,128)(2,1)S(1)}, bf16[16,3584]{1,0:T(8,128)(2,1)S(1)}, u32[]{:S(2)}, u32[]{:S(2)}) collective-permute-start(bf16[16,3584]{1,0:T(8,128)(2,1)S(1)} %get-tuple-element.70), channel_id=1, source_target_pairs={{0,12},{1,13},{2,14},{3,15},{4,8},{5,9},{6,10},{7,11},{8,4},{9,5},... | collective-permute-start | bytes 344072 | tf_op jit(solution)/shard_map/ppermute | solution.py:266
  61.8 1.2 %convolution_multiply_fusion.refs_2_ = f32[512,256]{1,0:T(8,128)} fusion(f32[512,256]{1,0:T(8,128)S(1)} %get-tuple-element.60, s32[256]{0:T(256)S(1)} %fusion.6), kind=kOutput, calls=%fused_computation | convolution fusion | flops 402849792 | bytes 1049600 | tf_op jit(solution)/shard_map/dot_general | solution.py:513
  63.0 0.0 collective-permute-start.20
  63.0 2.1 %collective-permute-start.21 = (bf16[16,3584]{1,0:T(8,128)(2,1)S(1)}, bf16[16,3584]{1,0:T(8,128)(2,1)S(1)}, u32[]{:S(2)}, u32[]{:S(2)}) collective-permute-start(bf16[16,3584]{1,0:T(8,128)(2,1)S(1)} %get-tuple-element.72), channel_id=1, source_target_pairs={{0,4},{1,5},{2,6},{3,7},{4,0},{5,1},{6,2},{7,3},{8,12},{9,13},{10,... | collective-permute-start | bytes 344072 | tf_op jit(solution)/shard_map/ppermute | solution.py:266
  65.1 3.2 %fetch.3 = (bf16[2,1024,1792]{2,1,0:T(8,128)(2,1)S(1)}, f32[8,128]{1,0:T(8,128)S(1)}) custom-call(bf16[1024,7168]{1,0:T(8,128)(2,1)} %bitcast.10, bf16[16,3584]{1,0:T(8,128)(2,1)S(1)} %get-tuple-element.73.refs_1_.refs_6_.refs_4_, f32[512,256]{1,0:T(8,128)} %convolution_multiply_fusion.refs_2_), custom_call_target="tpu_custom_call" | custom-call | bytes 14680064 | tf_op jit(solution)/shard_map/fetch/pallas_call | solution.py:284
  68.2 0.3 collective-permute-done.22.refs_1_
  68.5 0.3 plane_sum.3
  68.8 2.4 %collective-permute-start.23 = (bf16[16,3584]{1,0:T(8,128)(2,1)S(1)}, bf16[16,3584]{1,0:T(8,128)(2,1)S(1)}, u32[]{:S(2)}, u32[]{:S(2)}) collective-permute-start(bf16[16,3584]{1,0:T(8,128)(2,1)S(1)} %get-tuple-element.79), channel_id=1, source_target_pairs={{0,12},{1,13},{2,14},{3,15},{4,8},{5,9},{6,10},{7,11},{8,4},{9,5},... | collective-permute-start | bytes 344072 | tf_op jit(solution)/shard_map/ppermute | solution.py:266
  71.2 2.1 %collective-permute-start.25 = (bf16[16,3584]{1,0:T(8,128)(2,1)S(1)}, bf16[16,3584]{1,0:T(8,128)(2,1)S(1)}, u32[]{:S(2)}, u32[]{:S(2)}) collective-permute-start(bf16[16,3584]{1,0:T(8,128)(2,1)S(1)} %get-tuple-element.81), channel_id=1, source_target_pairs={{0,4},{1,5},{2,6},{3,7},{4,0},{5,1},{6,2},{7,3},{8,12},{9,13},{10,... | collective-permute-start | bytes 344072 | tf_op jit(solution)/shard_map/ppermute | solution.py:266
  73.3 3.8 %inner.2.refs_5_ = f32[4,64]{1,0:T(4,128)S(1)} custom-call(s32[1]{0:T(128)} %bitcast.1.refs_0_, bf16[1024,7168]{1,0:T(8,128)(2,1)} %bitcast.11, bf16[1,1024,1792]{2,1,0:T(8,128)(2,1)S(1)} %get-tuple-element.74.refs_2_, bf16[16,3584]{1,0:T(8,128)(2,1)S(1)} %collective-permute-done.19.refs_3_.refs_1_, ...), custom_call_target="tpu_custom_call" | custom-call | tf_op jit(solution)/shard_map/inner/pallas_call | solution.py:284
  77.0 4.2 %basis.3 = (bf16[1024,7168]{1,0:T(8,128)(2,1)}, f32[8,128]{1,0:T(8,128)S(1)}) custom-call(bf16[1024,64]{1,0:T(8,128)(2,1)S(1)} %get-tuple-element.61.refs_0_, bf16[16,3584]{1,0:T(8,128)(2,1)S(1)} %collective-permute-done.19.refs_3_.refs_1_, bf16[16,3584]{1,0:T(8,128)(2,1)S(1)} %collective-permute-done.20.refs_4_.refs_2_, ...), custom_call_target="tpu_custom_call" | custom-call | tf_op jit(solution)/shard_map/basis/pallas_call | solution.py:284
  81.3 2.9 %inner.3 = f32[4,64]{1,0:T(4,128)S(1)} custom-call(s32[1]{0:T(128)} %bitcast.1.refs_0_, bf16[1024,7168]{1,0:T(8,128)(2,1)} %bitcast.12, bf16[2,1024,1792]{2,1,0:T(8,128)(2,1)S(1)} %get-tuple-element.82.refs_2_, bf16[16,3584]{1,0:T(8,128)(2,1)S(1)} %collective-permute-done.23.refs_3_.refs_2_, bf16[16,3584]{1,0:T(8,128)(2,1)S(1)} %collective-permute-done.24.refs_4_.refs_3_, ...), custom_call_target="tpu_custom_call" | custom-call | tf_op jit(solution)/shard_map/inner/pallas_call | solution.py:284
  84.2 0.3 collective-permute-start.28
  84.5 1.1 %collective-permute-start.27 = (f32[4,64]{1,0:T(4,128)S(1)}, f32[4,64]{1,0:T(4,128)S(1)}, u32[]{:S(2)}, u32[]{:S(2)}) collective-permute-start(f32[4,64]{1,0:T(4,128)S(1)} %add.74.refs_6_.refs_3_), channel_id=1, source_target_pairs={{0,2},{1,3},{2,0},{3,1},{4,6},{5,7},{6,4},{7,5},{8,10},{9,11},{10,... | collective-permute-start | bytes 3080 | tf_op jit(solution)/shard_map/ppermute | solution.py:266
  85.6 0.5 collective-permute-start.26
  86.2 2.5 %basis.4 = (bf16[1024,7168]{1,0:T(8,128)(2,1)}, f32[8,128]{1,0:T(8,128)S(1)}) custom-call(bf16[1024,64]{1,0:T(8,128)(2,1)S(1)} %get-tuple-element.61.refs_0_, bf16[1024,7168]{1,0:T(8,128)(2,1)} %get-tuple-element.78.refs_1_, bf16[16,3584]{1,0:T(8,128)(2,1)S(1)} %collective-permute-done.23.refs_3_.refs_2_, ...), custom_call_target="tpu_custom_call", output_to_operand_aliasing={{0}: (1, {})} | custom-call | tf_op jit(solution)/shard_map/basis/pallas_call | solution.py:284
  88.7 2.4 %collective-permute-start.31 = (f32[4,64]{1,0:T(4,128)S(1)}, f32[4,64]{1,0:T(4,128)S(1)}, u32[]{:S(2)}, u32[]{:S(2)}) collective-permute-start(f32[4,64]{1,0:T(4,128)S(1)} %add.103.refs_6_.refs_3_), channel_id=1, source_target_pairs={{0,12},{1,13},{2,14},{3,15},{4,8},{5,9},{6,10},{7,11},{8,4},{9,5},... | collective-permute-start | bytes 3080 | tf_op jit(solution)/shard_map/ppermute | solution.py:266
  91.1 2.1 %collective-permute-start.29 = (f32[4,64]{1,0:T(4,128)S(1)}, f32[4,64]{1,0:T(4,128)S(1)}, u32[]{:S(2)}, u32[]{:S(2)}) collective-permute-start(f32[4,64]{1,0:T(4,128)S(1)} %add.103.refs_6_.refs_3_), channel_id=1, source_target_pairs={{0,4},{1,5},{2,6},{3,7},{4,0},{5,1},{6,2},{7,3},{8,12},{9,13},{10,... | collective-permute-start | bytes 3080 | tf_op jit(solution)/shard_map/ppermute | solution.py:266
  93.2 2.5 %basis.5 = (bf16[1024,7168]{1,0:T(8,128)(2,1)}, f32[8,128]{1,0:T(8,128)S(1)}) custom-call(bf16[1024,64]{1,0:T(8,128)(2,1)S(1)} %get-tuple-element.61.refs_0_, bf16[1024,7168]{1,0:T(8,128)(2,1)} %get-tuple-element.84.refs_1_, bf16[16,3584]{1,0:T(8,128)(2,1)S(1)} %collective-permute-done.23.refs_3_.refs_2_, ...), custom_call_target="tpu_custom_call", output_to_operand_aliasing={{0}: (1, {})} | custom-call | tf_op jit(solution)/shard_map/basis/pallas_call | solution.py:284
  95.7 0.6 add.104
  (31 shorter events, 0.2 us)
Async XLA Ops:
  0.6 33.6 %copy-start = (bf16[512,256]{1,0:T(8,128)(2,1)S(1)}, bf16[512,256]{1,0:T(8,128)(2,1)}, u32[]{:S(2)}) copy-start(bf16[512,256]{1,0:T(8,128)(2,1)} %param.5) | copy-start | bytes 786436
  0.7 0.7 copy-start.2
  5.4 9.4 %collective-permute-start.3 = (bf16[16,3584]{1,0:T(8,128)(2,1)S(1)}, bf16[16,3584]{1,0:T(8,128)(2,1)S(1)}, u32[]{:S(2)}, u32[]{:S(2)}) collective-permute-start(bf16[16,3584]{1,0:T(8,128)(2,1)S(1)} %get-tuple-element.52), channel_id=1, source_target_pairs={{0,12},{1,13},{2,14},{3,15},{4,8},{5,9},{6,10},{7,11},{8,4},{9,5},... | collective-permute-start | bytes 344072 | tf_op jit(solution)/shard_map/ppermute | solution.py:266
  10.5 9.7 %collective-permute-start.4 = (bf16[16,3584]{1,0:T(8,128)(2,1)S(1)}, bf16[16,3584]{1,0:T(8,128)(2,1)S(1)}, u32[]{:S(2)}, u32[]{:S(2)}) collective-permute-start(bf16[16,3584]{1,0:T(8,128)(2,1)S(1)} %get-tuple-element.53), channel_id=1, source_target_pairs={{0,8},{1,9},{2,10},{3,11},{4,12},{5,13},{6,14},{7,15},{8,0},{9,1},... | collective-permute-start | bytes 344072 | tf_op jit(solution)/shard_map/ppermute | solution.py:266
  10.5 9.7 %collective-permute-start.5 = (bf16[16,3584]{1,0:T(8,128)(2,1)S(1)}, bf16[16,3584]{1,0:T(8,128)(2,1)S(1)}, u32[]{:S(2)}, u32[]{:S(2)}) collective-permute-start(bf16[16,3584]{1,0:T(8,128)(2,1)S(1)} %get-tuple-element.54), channel_id=1, source_target_pairs={{0,4},{1,5},{2,6},{3,7},{4,0},{5,1},{6,2},{7,3},{8,12},{9,13},{10,... | collective-permute-start | bytes 344072 | tf_op jit(solution)/shard_map/ppermute | solution.py:266
  20.2 11.6 %collective-permute-start.9 = (bf16[64,3584]{1,0:T(8,128)(2,1)S(1)}, bf16[64,3584]{1,0:T(8,128)(2,1)S(1)}, u32[]{:S(2)}, u32[]{:S(2)}) collective-permute-start(bf16[64,3584]{1,0:T(8,128)(2,1)S(1)} %join.2.refs_4_.refs_3_), channel_id=1, source_target_pairs={{0,2},{1,3},{2,0},{3,1},{4,6},{5,7},{6,4},{7,5},{8,10},{9,11},{10,... | collective-permute-start | bytes 1376264 | tf_op jit(solution)/shard_map/ppermute | solution.py:266
  21.8 10.1 %collective-permute-start = (bf16[16,3584]{1,0:T(8,128)(2,1)S(1)}, bf16[16,3584]{1,0:T(8,128)(2,1)S(1)}, u32[]{:S(2)}, u32[]{:S(2)}) collective-permute-start(bf16[16,3584]{1,0:T(8,128)(2,1)S(1)} %get-tuple-element.48), channel_id=1, source_target_pairs={{0,12},{1,13},{2,14},{3,15},{4,8},{5,9},{6,10},{7,11},{8,4},{9,5},... | collective-permute-start | bytes 344072 | tf_op jit(solution)/shard_map/ppermute | solution.py:266
  24.3 9.3 %collective-permute-start.1 = (bf16[16,3584]{1,0:T(8,128)(2,1)S(1)}, bf16[16,3584]{1,0:T(8,128)(2,1)S(1)}, u32[]{:S(2)}, u32[]{:S(2)}) collective-permute-start(bf16[16,3584]{1,0:T(8,128)(2,1)S(1)} %get-tuple-element.49), channel_id=1, source_target_pairs={{0,8},{1,9},{2,10},{3,11},{4,12},{5,13},{6,14},{7,15},{8,0},{9,1},... | collective-permute-start | bytes 344072 | tf_op jit(solution)/shard_map/ppermute | solution.py:266
  24.3 9.3 %collective-permute-start.2 = (bf16[16,3584]{1,0:T(8,128)(2,1)S(1)}, bf16[16,3584]{1,0:T(8,128)(2,1)S(1)}, u32[]{:S(2)}, u32[]{:S(2)}) collective-permute-start(bf16[16,3584]{1,0:T(8,128)(2,1)S(1)} %get-tuple-element.50), channel_id=1, source_target_pairs={{0,4},{1,5},{2,6},{3,7},{4,0},{5,1},{6,2},{7,3},{8,12},{9,13},{10,... | collective-permute-start | bytes 344072 | tf_op jit(solution)/shard_map/ppermute | solution.py:266
  26.2 8.4 %collective-permute-start.10 = (bf16[64,3584]{1,0:T(8,128)(2,1)S(1)}, bf16[64,3584]{1,0:T(8,128)(2,1)S(1)}, u32[]{:S(2)}, u32[]{:S(2)}) collective-permute-start(bf16[64,3584]{1,0:T(8,128)(2,1)S(1)} %join.2.refs_4_.refs_3_), channel_id=1, source_target_pairs={{0,1},{1,0},{2,3},{3,2},{4,5},{5,4},{6,7},{7,6},{8,9},{9,8},{10,11... | collective-permute-start | bytes 1376264 | tf_op jit(solution)/shard_map/ppermute | solution.py:266
  31.9 2.8 %collective-permute-start.11 = (bf16[64,3584]{1,0:T(8,128)(2,1)S(1)}, bf16[64,3584]{1,0:T(8,128)(2,1)S(1)}, u32[]{:S(2)}, u32[]{:S(2)}) collective-permute-start(bf16[64,3584]{1,0:T(8,128)(2,1)S(1)} %collective-permute-done.9.refs_4_), channel_id=1, source_target_pairs={{0,1},{1,0},{2,3},{3,2},{4,5},{5,4},{6,7},{7,6},{8,9},{9,8},{10,11... | collective-permute-start | bytes 1376264 | tf_op jit(solution)/shard_map/ppermute | solution.py:266
  33.6 11.6 %collective-permute-start.6 = (bf16[64,3584]{1,0:T(8,128)(2,1)S(1)}, bf16[64,3584]{1,0:T(8,128)(2,1)S(1)}, u32[]{:S(2)}, u32[]{:S(2)}) collective-permute-start(bf16[64,3584]{1,0:T(8,128)(2,1)S(1)} %join.3.refs_7_.refs_3_), channel_id=1, source_target_pairs={{0,2},{1,3},{2,0},{3,1},{4,6},{5,7},{6,4},{7,5},{8,10},{9,11},{10,... | collective-permute-start | bytes 1376264 | tf_op jit(solution)/shard_map/ppermute | solution.py:266
  39.9 5.3 %collective-permute-start.12 = (bf16[64,3584]{1,0:T(8,128)(2,1)S(1)}, bf16[64,3584]{1,0:T(8,128)(2,1)S(1)}, u32[]{:S(2)}, u32[]{:S(2)}) collective-permute-start(bf16[64,3584]{1,0:T(8,128)(2,1)S(1)} %get-tuple-element.57), channel_id=1, source_target_pairs={{0,1},{1,0},{2,3},{3,2},{4,5},{5,4},{6,7},{7,6},{8,9},{9,8},{10,11... | collective-permute-start | bytes 1376264 | tf_op jit(solution)/shard_map/ppermute | solution.py:266
  40.0 5.3 %collective-permute-start.13 = (bf16[64,3584]{1,0:T(8,128)(2,1)S(1)}, bf16[64,3584]{1,0:T(8,128)(2,1)S(1)}, u32[]{:S(2)}, u32[]{:S(2)}) collective-permute-start(bf16[64,3584]{1,0:T(8,128)(2,1)S(1)} %get-tuple-element.58), channel_id=1, source_target_pairs={{0,1},{1,0},{2,3},{3,2},{4,5},{5,4},{6,7},{7,6},{8,9},{9,8},{10,11... | collective-permute-start | bytes 1376264 | tf_op jit(solution)/shard_map/ppermute | solution.py:266
  40.5 6.6 %collective-permute-start.7 = (bf16[64,3584]{1,0:T(8,128)(2,1)S(1)}, bf16[64,3584]{1,0:T(8,128)(2,1)S(1)}, u32[]{:S(2)}, u32[]{:S(2)}) collective-permute-start(bf16[64,3584]{1,0:T(8,128)(2,1)S(1)} %join.3.refs_7_.refs_3_), channel_id=1, source_target_pairs={{0,1},{1,0},{2,3},{3,2},{4,5},{5,4},{6,7},{7,6},{8,9},{9,8},{10,11... | collective-permute-start | bytes 1376264 | tf_op jit(solution)/shard_map/ppermute | solution.py:266
  45.2 1.8 %collective-permute-start.8 = (bf16[64,3584]{1,0:T(8,128)(2,1)S(1)}, bf16[64,3584]{1,0:T(8,128)(2,1)S(1)}, u32[]{:S(2)}, u32[]{:S(2)}) collective-permute-start(bf16[64,3584]{1,0:T(8,128)(2,1)S(1)} %collective-permute-done.6.refs_4_), channel_id=1, source_target_pairs={{0,1},{1,0},{2,3},{3,2},{4,5},{5,4},{6,7},{7,6},{8,9},{9,8},{10,11... | collective-permute-start | bytes 1376264 | tf_op jit(solution)/shard_map/ppermute | solution.py:266
  45.7 13.4 %collective-permute-start.14 = (bf16[64,3584]{1,0:T(8,128)(2,1)S(1)}, bf16[64,3584]{1,0:T(8,128)(2,1)S(1)}, u32[]{:S(2)}, u32[]{:S(2)}) collective-permute-start(bf16[64,3584]{1,0:T(8,128)(2,1)S(1)} %get-tuple-element.62), channel_id=1, source_target_pairs={{0,2},{1,3},{2,0},{3,1},{4,6},{5,7},{6,4},{7,5},{8,10},{9,11},{10,... | collective-permute-start | bytes 1376264 | tf_op jit(solution)/shard_map/ppermute | solution.py:266
  52.3 1.6 %collective-permute-start.15 = (bf16[32,3584]{1,0:T(8,128)(2,1)S(1)}, bf16[32,3584]{1,0:T(8,128)(2,1)S(1)}, u32[]{:S(2)}, u32[]{:S(2)}) collective-permute-start(bf16[32,3584]{1,0:T(8,128)(2,1)S(1)} %get-tuple-element.64), channel_id=1, source_target_pairs={{0,1},{1,0},{2,3},{3,2},{4,5},{5,4},{6,7},{7,6},{8,9},{9,8},{10,11... | collective-permute-start | bytes 688136 | tf_op jit(solution)/shard_map/ppermute | solution.py:266
  52.6 1.6 %collective-permute-start.16 = (bf16[32,3584]{1,0:T(8,128)(2,1)S(1)}, bf16[32,3584]{1,0:T(8,128)(2,1)S(1)}, u32[]{:S(2)}, u32[]{:S(2)}) collective-permute-start(bf16[32,3584]{1,0:T(8,128)(2,1)S(1)} %get-tuple-element.65), channel_id=1, source_target_pairs={{0,1},{1,0},{2,3},{3,2},{4,5},{5,4},{6,7},{7,6},{8,9},{9,8},{10,11... | collective-permute-start | bytes 688136 | tf_op jit(solution)/shard_map/ppermute | solution.py:266
  52.9 1.6 %collective-permute-start.17 = (bf16[32,3584]{1,0:T(8,128)(2,1)S(1)}, bf16[32,3584]{1,0:T(8,128)(2,1)S(1)}, u32[]{:S(2)}, u32[]{:S(2)}) collective-permute-start(bf16[32,3584]{1,0:T(8,128)(2,1)S(1)} %get-tuple-element.66), channel_id=1, source_target_pairs={{0,1},{1,0},{2,3},{3,2},{4,5},{5,4},{6,7},{7,6},{8,9},{9,8},{10,11... | collective-permute-start | bytes 688136 | tf_op jit(solution)/shard_map/ppermute | solution.py:266
  53.1 1.8 %collective-permute-start.18 = (bf16[32,3584]{1,0:T(8,128)(2,1)S(1)}, bf16[32,3584]{1,0:T(8,128)(2,1)S(1)}, u32[]{:S(2)}, u32[]{:S(2)}) collective-permute-start(bf16[32,3584]{1,0:T(8,128)(2,1)S(1)} %get-tuple-element.67), channel_id=1, source_target_pairs={{0,1},{1,0},{2,3},{3,2},{4,5},{5,4},{6,7},{7,6},{8,9},{9,8},{10,11... | collective-permute-start | bytes 688136 | tf_op jit(solution)/shard_map/ppermute | solution.py:266
  55.3 13.2 %collective-permute-start.22 = (bf16[64,3584]{1,0:T(8,128)(2,1)S(1)}, bf16[64,3584]{1,0:T(8,128)(2,1)S(1)}, u32[]{:S(2)}, u32[]{:S(2)}) collective-permute-start(bf16[64,3584]{1,0:T(8,128)(2,1)S(1)} %get-tuple-element.75), channel_id=1, source_target_pairs={{0,2},{1,3},{2,0},{3,1},{4,6},{5,7},{6,4},{7,5},{8,10},{9,11},{10,... | collective-permute-start | bytes 1376264 | tf_op jit(solution)/shard_map/ppermute | solution.py:266
  59.4 11.8 %collective-permute-start.19 = (bf16[16,3584]{1,0:T(8,128)(2,1)S(1)}, bf16[16,3584]{1,0:T(8,128)(2,1)S(1)}, u32[]{:S(2)}, u32[]{:S(2)}) collective-permute-start(bf16[16,3584]{1,0:T(8,128)(2,1)S(1)} %get-tuple-element.70), channel_id=1, source_target_pairs={{0,12},{1,13},{2,14},{3,15},{4,8},{5,9},{6,10},{7,11},{8,4},{9,5},... | collective-permute-start | bytes 344072 | tf_op jit(solution)/shard_map/ppermute | solution.py:266
  63.0 10.3 %collective-permute-start.20 = (bf16[16,3584]{1,0:T(8,128)(2,1)S(1)}, bf16[16,3584]{1,0:T(8,128)(2,1)S(1)}, u32[]{:S(2)}, u32[]{:S(2)}) collective-permute-start(bf16[16,3584]{1,0:T(8,128)(2,1)S(1)} %get-tuple-element.71), channel_id=1, source_target_pairs={{0,8},{1,9},{2,10},{3,11},{4,12},{5,13},{6,14},{7,15},{8,0},{9,1},... | collective-permute-start | bytes 344072 | tf_op jit(solution)/shard_map/ppermute | solution.py:266
  63.0 10.3 %collective-permute-start.21 = (bf16[16,3584]{1,0:T(8,128)(2,1)S(1)}, bf16[16,3584]{1,0:T(8,128)(2,1)S(1)}, u32[]{:S(2)}, u32[]{:S(2)}) collective-permute-start(bf16[16,3584]{1,0:T(8,128)(2,1)S(1)} %get-tuple-element.72), channel_id=1, source_target_pairs={{0,4},{1,5},{2,6},{3,7},{4,0},{5,1},{6,2},{7,3},{8,12},{9,13},{10,... | collective-permute-start | bytes 344072 | tf_op jit(solution)/shard_map/ppermute | solution.py:266
  68.8 12.4 %collective-permute-start.23 = (bf16[16,3584]{1,0:T(8,128)(2,1)S(1)}, bf16[16,3584]{1,0:T(8,128)(2,1)S(1)}, u32[]{:S(2)}, u32[]{:S(2)}) collective-permute-start(bf16[16,3584]{1,0:T(8,128)(2,1)S(1)} %get-tuple-element.79), channel_id=1, source_target_pairs={{0,12},{1,13},{2,14},{3,15},{4,8},{5,9},{6,10},{7,11},{8,4},{9,5},... | collective-permute-start | bytes 344072 | tf_op jit(solution)/shard_map/ppermute | solution.py:266
  71.2 10.1 %collective-permute-start.24 = (bf16[16,3584]{1,0:T(8,128)(2,1)S(1)}, bf16[16,3584]{1,0:T(8,128)(2,1)S(1)}, u32[]{:S(2)}, u32[]{:S(2)}) collective-permute-start(bf16[16,3584]{1,0:T(8,128)(2,1)S(1)} %get-tuple-element.80), channel_id=1, source_target_pairs={{0,8},{1,9},{2,10},{3,11},{4,12},{5,13},{6,14},{7,15},{8,0},{9,1},... | collective-permute-start | bytes 344072 | tf_op jit(solution)/shard_map/ppermute | solution.py:266
  71.2 10.1 %collective-permute-start.25 = (bf16[16,3584]{1,0:T(8,128)(2,1)S(1)}, bf16[16,3584]{1,0:T(8,128)(2,1)S(1)}, u32[]{:S(2)}, u32[]{:S(2)}) collective-permute-start(bf16[16,3584]{1,0:T(8,128)(2,1)S(1)} %get-tuple-element.81), channel_id=1, source_target_pairs={{0,4},{1,5},{2,6},{3,7},{4,0},{5,1},{6,2},{7,3},{8,12},{9,13},{10,... | collective-permute-start | bytes 344072 | tf_op jit(solution)/shard_map/ppermute | solution.py:266
  84.2 4.4 %collective-permute-start.28 = (f32[4,64]{1,0:T(4,128)S(1)}, f32[4,64]{1,0:T(4,128)S(1)}, u32[]{:S(2)}, u32[]{:S(2)}) collective-permute-start(f32[4,64]{1,0:T(4,128)S(1)} %add.74.refs_6_.refs_3_), channel_id=1, source_target_pairs={{0,3},{1,2},{2,1},{3,0},{4,7},{5,6},{6,5},{7,4},{8,11},{9,10},{10,... | collective-permute-start | bytes 3080 | tf_op jit(solution)/shard_map/ppermute | solution.py:266
  84.5 4.2 %collective-permute-start.27 = (f32[4,64]{1,0:T(4,128)S(1)}, f32[4,64]{1,0:T(4,128)S(1)}, u32[]{:S(2)}, u32[]{:S(2)}) collective-permute-start(f32[4,64]{1,0:T(4,128)S(1)} %add.74.refs_6_.refs_3_), channel_id=1, source_target_pairs={{0,2},{1,3},{2,0},{3,1},{4,6},{5,7},{6,4},{7,5},{8,10},{9,11},{10,... | collective-permute-start | bytes 3080 | tf_op jit(solution)/shard_map/ppermute | solution.py:266
  85.6 3.1 %collective-permute-start.26 = (f32[4,64]{1,0:T(4,128)S(1)}, f32[4,64]{1,0:T(4,128)S(1)}, u32[]{:S(2)}, u32[]{:S(2)}) collective-permute-start(f32[4,64]{1,0:T(4,128)S(1)} %add.74.refs_6_.refs_3_), channel_id=1, source_target_pairs={{0,1},{1,0},{2,3},{3,2},{4,5},{5,4},{6,7},{7,6},{8,9},{9,8},{10,11... | collective-permute-start | bytes 3080 | tf_op jit(solution)/shard_map/ppermute | solution.py:266
  88.7 7.0 %collective-permute-start.31 = (f32[4,64]{1,0:T(4,128)S(1)}, f32[4,64]{1,0:T(4,128)S(1)}, u32[]{:S(2)}, u32[]{:S(2)}) collective-permute-start(f32[4,64]{1,0:T(4,128)S(1)} %add.103.refs_6_.refs_3_), channel_id=1, source_target_pairs={{0,12},{1,13},{2,14},{3,15},{4,8},{5,9},{6,10},{7,11},{8,4},{9,5},... | collective-permute-start | bytes 3080 | tf_op jit(solution)/shard_map/ppermute | solution.py:266
  91.1 4.6 %collective-permute-start.30 = (f32[4,64]{1,0:T(4,128)S(1)}, f32[4,64]{1,0:T(4,128)S(1)}, u32[]{:S(2)}, u32[]{:S(2)}) collective-permute-start(f32[4,64]{1,0:T(4,128)S(1)} %add.103.refs_6_.refs_3_), channel_id=1, source_target_pairs={{0,8},{1,9},{2,10},{3,11},{4,12},{5,13},{6,14},{7,15},{8,0},{9,1},... | collective-permute-start | bytes 3080 | tf_op jit(solution)/shard_map/ppermute | solution.py:266
  91.1 4.6 %collective-permute-start.29 = (f32[4,64]{1,0:T(4,128)S(1)}, f32[4,64]{1,0:T(4,128)S(1)}, u32[]{:S(2)}, u32[]{:S(2)}) collective-permute-start(f32[4,64]{1,0:T(4,128)S(1)} %add.103.refs_6_.refs_3_), channel_id=1, source_target_pairs={{0,4},{1,5},{2,6},{3,7},{4,0},{5,1},{6,2},{7,3},{8,12},{9,13},{10,... | collective-permute-start | bytes 3080 | tf_op jit(solution)/shard_map/ppermute | solution.py:266
  93.2 3.1 %copy-start.1 = (bf16[512,256]{1,0:T(8,128)(2,1)S(1)}, bf16[512,256]{1,0:T(8,128)(2,1)}, u32[]{:S(2)}) copy-start(bf16[512,256]{1,0:T(8,128)(2,1)} %param.5) | copy-start | bytes 786436

commit v6 on v5

--- a/solution.py
+++ b/solution.py
@@ -20,7 +20,7 @@
 P_ORDER = (1, 2, 3)
 FETCH_COST = 1
 FLOPS = 0
-VMEM_LIMIT = 26 * 2**20
+VMEM_LIMIT = 20 * 2**20
 
 
 def iota(shape, dim):

time: 96.5 us -> 96.5 us (level)
  no operation moved by 1% of the time
where the time goes in v6:
time: 96.5 us; the launch traced here: 96.3 us
  Pallas kernels  41.5 us (43%)
  starting transfers between devices  31.9 us (33%)
  waiting for transfers between devices  19.6 us (20%)
  matrix products  1.48 us (2%)
    pallas_call x20, Pallas kernels, call(): pl.pallas_call(body, out_shape=[shape for shape, _ in outs], in_specs=[sp...  41.5 us
    ppermute x32, starting transfers between devices, send(): return lax.ppermute(x, 'expert', [(i, i ^ flip) for i in range(devices)])  31.9 us
    ppermute x32, waiting for transfers between devices, send(): return lax.ppermute(x, 'expert', [(i, i ^ flip) for i in range(devices)])  19.6 us
  transfers between devices with their start and end apart: 32, of which 10 were waited for; matrix products, arithmetic and copies ran while one was open for 2% of the time, Pallas kernels for 35%

profile of v6, /device:TPU:0, one launch (start us, length us, event | category | flops | bytes accessed | tf_op | source)
XLA Modules:
  0.0 96.3 jit_solution(6412442971226817811)
XLA Ops:
  0.6 0.0 copy-start
  0.7 0.7 copy-done.2
  1.4 0.3 spread.1
  1.7 3.7 %mix.2 = (bf16[16,3584]{1,0:T(8,128)(2,1)S(1)}, bf16[16,3584]{1,0:T(8,128)(2,1)S(1)}, bf16[16,3584]{1,0:T(8,128)(2,1)S(1)}, bf16[16,3584]{1,0:T(8,128)(2,1)S(1)}) custom-call(bf16[64,1024]{1,0:T(8,128)(2,1)S(1)} %get-tuple-element.46.refs_0_, bf16[1024,7168]{1,0:T(8,128)(2,1)} %bitcast.7), custom_call_target="tpu_custom_call" | custom-call | tf_op jit(solution)/shard_map/mix/pallas_call | solution.py:284
  5.4 5.1 %collective-permute-start.3 = (bf16[16,3584]{1,0:T(8,128)(2,1)S(1)}, bf16[16,3584]{1,0:T(8,128)(2,1)S(1)}, u32[]{:S(2)}, u32[]{:S(2)}) collective-permute-start(bf16[16,3584]{1,0:T(8,128)(2,1)S(1)} %get-tuple-element.52), channel_id=1, source_target_pairs={{0,12},{1,13},{2,14},{3,15},{4,8},{5,9},{6,10},{7,11},{8,4},{9,5},... | collective-permute-start | bytes 344072 | tf_op jit(solution)/shard_map/ppermute | solution.py:266
  10.5 0.6 collective-permute-start.5
  11.2 3.7 %mix.3 = (bf16[16,3584]{1,0:T(8,128)(2,1)S(1)}, bf16[16,3584]{1,0:T(8,128)(2,1)S(1)}, bf16[16,3584]{1,0:T(8,128)(2,1)S(1)}, bf16[16,3584]{1,0:T(8,128)(2,1)S(1)}) custom-call(bf16[64,1024]{1,0:T(8,128)(2,1)S(1)} %get-tuple-element.46.refs_0_, bf16[1024,7168]{1,0:T(8,128)(2,1)} %bitcast.8, bf16[16,3584]{1,0:T(8,128)(2,1)S(1)} %get-tuple-element.47.refs_2_.refs_3_), custom_call_target="tpu_custom_call" | custom-call | tf_op jit(solution)/shard_map/mix/pallas_call | solution.py:284
  14.9 0.0 collective-permute-done.3.refs_0_
  14.9 5.3 %collective-permute-done.4.refs_1_ = bf16[16,3584]{1,0:T(8,128)(2,1)S(1)} collective-permute-done((bf16[16,3584]{1,0:T(8,128)(2,1)S(1)}, bf16[16,3584]{1,0:T(8,128)(2,1)S(1)}, u32[]{:S(2)}, u32[]{:S(2)}) %collective-permute-start.4) | collective-permute-done | bytes 114720 | tf_op jit(solution)/shard_map/ppermute | solution.py:266
  20.2 1.6 %collective-permute-start.9 = (bf16[64,3584]{1,0:T(8,128)(2,1)S(1)}, bf16[64,3584]{1,0:T(8,128)(2,1)S(1)}, u32[]{:S(2)}, u32[]{:S(2)}) collective-permute-start(bf16[64,3584]{1,0:T(8,128)(2,1)S(1)} %join.2.refs_4_.refs_3_), channel_id=1, source_target_pairs={{0,2},{1,3},{2,0},{3,1},{4,6},{5,7},{6,4},{7,5},{8,10},{9,11},{10,... | collective-permute-start | bytes 1376264 | tf_op jit(solution)/shard_map/ppermute | solution.py:266
  21.8 2.5 %collective-permute-start = (bf16[16,3584]{1,0:T(8,128)(2,1)S(1)}, bf16[16,3584]{1,0:T(8,128)(2,1)S(1)}, u32[]{:S(2)}, u32[]{:S(2)}) collective-permute-start(bf16[16,3584]{1,0:T(8,128)(2,1)S(1)} %get-tuple-element.48), channel_id=1, source_target_pairs={{0,12},{1,13},{2,14},{3,15},{4,8},{5,9},{6,10},{7,11},{8,4},{9,5},... | collective-permute-start | bytes 344072 | tf_op jit(solution)/shard_map/ppermute | solution.py:266
  24.3 0.0 collective-permute-start.1
  24.3 1.9 %collective-permute-start.2 = (bf16[16,3584]{1,0:T(8,128)(2,1)S(1)}, bf16[16,3584]{1,0:T(8,128)(2,1)S(1)}, u32[]{:S(2)}, u32[]{:S(2)}) collective-permute-start(bf16[16,3584]{1,0:T(8,128)(2,1)S(1)} %get-tuple-element.50), channel_id=1, source_target_pairs={{0,4},{1,5},{2,6},{3,7},{4,0},{5,1},{6,2},{7,3},{8,12},{9,13},{10,... | collective-permute-start | bytes 344072 | tf_op jit(solution)/shard_map/ppermute | solution.py:266
  26.2 5.7 %collective-permute-done.9.refs_4_ = bf16[64,3584]{1,0:T(8,128)(2,1)S(1)} collective-permute-done((bf16[64,3584]{1,0:T(8,128)(2,1)S(1)}, bf16[64,3584]{1,0:T(8,128)(2,1)S(1)}, u32[]{:S(2)}, u32[]{:S(2)}) %collective-permute-start.9) | collective-permute-done | bytes 458784 | tf_op jit(solution)/shard_map/ppermute | solution.py:266
  31.9 0.0 collective-permute-done.refs_0_
  31.9 1.7 %collective-permute-done.1.refs_1_ = bf16[16,3584]{1,0:T(8,128)(2,1)S(1)} collective-permute-done((bf16[16,3584]{1,0:T(8,128)(2,1)S(1)}, bf16[16,3584]{1,0:T(8,128)(2,1)S(1)}, u32[]{:S(2)}, u32[]{:S(2)}) %collective-permute-start.1) | collective-permute-done | bytes 114720 | tf_op jit(solution)/shard_map/ppermute | solution.py:266
  33.6 0.6 collective-permute-start.6
  34.2 0.3 convolution_convert_fusion.refs_1_
  34.5 0.1 copy.10.refs_0_
  34.7 0.0 collective-permute-done.10.refs_5_
  34.7 0.0 collective-permute-done.11.refs_6_
  34.7 5.2 %fit.2 = (f32[128,3584]{1,0:T(8,128)S(1)}, bf16[64,3584]{1,0:T(8,128)(2,1)S(1)}, bf16[64,3584]{1,0:T(8,128)(2,1)S(1)}, f32[512,256]{1,0:T(8,128)S(1)}) custom-call(bf16[512,256]{1,0:T(8,128)(2,1)S(1)} %copy.10.refs_0_, bf16[256,512]{1,0:T(8,128)(2,1)S(1)} %convolution_convert_fusion.refs_1_, bf16[512,7168]{1,0:T(8,128)(2,1)} %refs_2_.3, ...), custom_call_target="tpu_custom_call" | custom-call | tf_op jit(solution)/shard_map/fit/pallas_call | solution.py:284
  39.9 0.1 collective-permute-start.12
  40.0 0.5 collective-permute-start.13
  40.5 0.1 collective-permute-start.7
  40.5 4.7 %collective-permute-done.6.refs_4_ = bf16[64,3584]{1,0:T(8,128)(2,1)S(1)} collective-permute-done((bf16[64,3584]{1,0:T(8,128)(2,1)S(1)}, bf16[64,3584]{1,0:T(8,128)(2,1)S(1)}, u32[]{:S(2)}, u32[]{:S(2)}) %collective-permute-start.6) | collective-permute-done | bytes 458784 | tf_op jit(solution)/shard_map/ppermute | solution.py:266
  45.2 0.5 chip_sum.2
  45.7 1.3 %collective-permute-start.14 = (bf16[64,3584]{1,0:T(8,128)(2,1)S(1)}, bf16[64,3584]{1,0:T(8,128)(2,1)S(1)}, u32[]{:S(2)}, u32[]{:S(2)}) collective-permute-start(bf16[64,3584]{1,0:T(8,128)(2,1)S(1)} %get-tuple-element.62), channel_id=1, source_target_pairs={{0,2},{1,3},{2,0},{3,1},{4,6},{5,7},{6,4},{7,5},{8,10},{9,11},{10,... | collective-permute-start | bytes 1376264 | tf_op jit(solution)/shard_map/ppermute | solution.py:266
  47.1 0.0 collective-permute-done.7.refs_5_
  47.1 0.0 collective-permute-done.8.refs_6_
  47.1 5.2 %fit.3 = (f32[128,3584]{1,0:T(8,128)S(1)}, bf16[32,3584]{1,0:T(8,128)(2,1)S(1)}, bf16[32,3584]{1,0:T(8,128)(2,1)S(1)}, bf16[32,3584]{1,0:T(8,128)(2,1)S(1)}, bf1...) custom-call(bf16[512,256]{1,0:T(8,128)(2,1)S(1)} %copy.10.refs_0_, ...), custom_call_target="tpu_custom_call" | custom-call | tf_op jit(solution)/shard_map/fit/pallas_call | solution.py:284
  52.3 0.3 collective-permute-start.15
  52.6 0.3 collective-permute-start.16
  52.9 0.2 collective-permute-start.17
  53.1 0.3 collective-permute-start.18
  53.4 0.5 collective-permute-done.15.refs_1_
  53.9 0.3 collective-permute-done.16.refs_2_
  54.2 0.3 collective-permute-done.17.refs_3_
  54.5 0.3 collective-permute-done.18.refs_4_
  54.8 0.5 chip_sum.3
  55.3 1.3 %collective-permute-start.22 = (bf16[64,3584]{1,0:T(8,128)(2,1)S(1)}, bf16[64,3584]{1,0:T(8,128)(2,1)S(1)}, u32[]{:S(2)}, u32[]{:S(2)}) collective-permute-start(bf16[64,3584]{1,0:T(8,128)(2,1)S(1)} %get-tuple-element.75), channel_id=1, source_target_pairs={{0,2},{1,3},{2,0},{3,1},{4,6},{5,7},{6,4},{7,5},{8,10},{9,11},{10,... | collective-permute-start | bytes 1376264 | tf_op jit(solution)/shard_map/ppermute | solution.py:266
  56.6 2.0 %fetch.2 = (bf16[1,1024,1792]{2,1,0:T(8,128)(2,1)S(1)}, f32[8,128]{1,0:T(8,128)S(1)}) custom-call(bf16[1024,7168]{1,0:T(8,128)(2,1)} %bitcast.9, f32[64,3584]{1,0:T(8,128)S(1)} %get-tuple-element.68.refs_1_.refs_0_), custom_call_target="tpu_custom_call" | custom-call | bytes 7340032 | tf_op jit(solution)/shard_map/fetch/pallas_call | solution.py:284
  58.7 0.4 collective-permute-done.14.refs_1_
  59.1 0.3 plane_sum.2
  59.4 2.4 %collective-permute-start.19 = (bf16[16,3584]{1,0:T(8,128)(2,1)S(1)}, bf16[16,3584]{1,0:T(8,128)(2,1)S(1)}, u32[]{:S(2)}, u32[]{:S(2)}) collective-permute-start(bf16[16,3584]{1,0:T(8,128)(2,1)S(1)} %get-tuple-element.70), channel_id=1, source_target_pairs={{0,12},{1,13},{2,14},{3,15},{4,8},{5,9},{6,10},{7,11},{8,4},{9,5},... | collective-permute-start | bytes 344072 | tf_op jit(solution)/shard_map/ppermute | solution.py:266
  61.8 1.2 %convolution_multiply_fusion.refs_2_ = f32[512,256]{1,0:T(8,128)} fusion(f32[512,256]{1,0:T(8,128)S(1)} %get-tuple-element.60, s32[256]{0:T(256)S(1)} %fusion.6), kind=kOutput, calls=%fused_computation | convolution fusion | flops 402849792 | bytes 1049600 | tf_op jit(solution)/shard_map/dot_general | solution.py:513
  63.0 0.0 collective-permute-start.20
  63.0 2.1 %collective-permute-start.21 = (bf16[16,3584]{1,0:T(8,128)(2,1)S(1)}, bf16[16,3584]{1,0:T(8,128)(2,1)S(1)}, u32[]{:S(2)}, u32[]{:S(2)}) collective-permute-start(bf16[16,3584]{1,0:T(8,128)(2,1)S(1)} %get-tuple-element.72), channel_id=1, source_target_pairs={{0,4},{1,5},{2,6},{3,7},{4,0},{5,1},{6,2},{7,3},{8,12},{9,13},{10,... | collective-permute-start | bytes 344072 | tf_op jit(solution)/shard_map/ppermute | solution.py:266
  65.1 3.2 %fetch.3 = (bf16[2,1024,1792]{2,1,0:T(8,128)(2,1)S(1)}, f32[8,128]{1,0:T(8,128)S(1)}) custom-call(bf16[1024,7168]{1,0:T(8,128)(2,1)} %bitcast.10, bf16[16,3584]{1,0:T(8,128)(2,1)S(1)} %get-tuple-element.73.refs_1_.refs_6_.refs_4_, f32[512,256]{1,0:T(8,128)} %convolution_multiply_fusion.refs_2_), custom_call_target="tpu_custom_call" | custom-call | bytes 14680064 | tf_op jit(solution)/shard_map/fetch/pallas_call | solution.py:284
  68.2 0.3 collective-permute-done.22.refs_1_
  68.5 0.3 plane_sum.3
  68.8 2.4 %collective-permute-start.23 = (bf16[16,3584]{1,0:T(8,128)(2,1)S(1)}, bf16[16,3584]{1,0:T(8,128)(2,1)S(1)}, u32[]{:S(2)}, u32[]{:S(2)}) collective-permute-start(bf16[16,3584]{1,0:T(8,128)(2,1)S(1)} %get-tuple-element.79), channel_id=1, source_target_pairs={{0,12},{1,13},{2,14},{3,15},{4,8},{5,9},{6,10},{7,11},{8,4},{9,5},... | collective-permute-start | bytes 344072 | tf_op jit(solution)/shard_map/ppermute | solution.py:266
  71.2 2.1 %collective-permute-start.25 = (bf16[16,3584]{1,0:T(8,128)(2,1)S(1)}, bf16[16,3584]{1,0:T(8,128)(2,1)S(1)}, u32[]{:S(2)}, u32[]{:S(2)}) collective-permute-start(bf16[16,3584]{1,0:T(8,128)(2,1)S(1)} %get-tuple-element.81), channel_id=1, source_target_pairs={{0,4},{1,5},{2,6},{3,7},{4,0},{5,1},{6,2},{7,3},{8,12},{9,13},{10,... | collective-permute-start | bytes 344072 | tf_op jit(solution)/shard_map/ppermute | solution.py:266
  73.3 3.8 %inner.2.refs_5_ = f32[4,64]{1,0:T(4,128)S(1)} custom-call(s32[1]{0:T(128)} %bitcast.1.refs_0_, bf16[1024,7168]{1,0:T(8,128)(2,1)} %bitcast.11, bf16[1,1024,1792]{2,1,0:T(8,128)(2,1)S(1)} %get-tuple-element.74.refs_2_, bf16[16,3584]{1,0:T(8,128)(2,1)S(1)} %collective-permute-done.19.refs_3_.refs_1_, ...), custom_call_target="tpu_custom_call" | custom-call | tf_op jit(solution)/shard_map/inner/pallas_call | solution.py:284
  77.0 4.2 %basis.3 = (bf16[1024,7168]{1,0:T(8,128)(2,1)}, f32[8,128]{1,0:T(8,128)S(1)}) custom-call(bf16[1024,64]{1,0:T(8,128)(2,1)S(1)} %get-tuple-element.61.refs_0_, bf16[16,3584]{1,0:T(8,128)(2,1)S(1)} %collective-permute-done.19.refs_3_.refs_1_, bf16[16,3584]{1,0:T(8,128)(2,1)S(1)} %collective-permute-done.20.refs_4_.refs_2_, ...), custom_call_target="tpu_custom_call" | custom-call | tf_op jit(solution)/shard_map/basis/pallas_call | solution.py:284
  81.3 2.9 %inner.3 = f32[4,64]{1,0:T(4,128)S(1)} custom-call(s32[1]{0:T(128)} %bitcast.1.refs_0_, bf16[1024,7168]{1,0:T(8,128)(2,1)} %bitcast.12, bf16[2,1024,1792]{2,1,0:T(8,128)(2,1)S(1)} %get-tuple-element.82.refs_2_, bf16[16,3584]{1,0:T(8,128)(2,1)S(1)} %collective-permute-done.23.refs_3_.refs_2_, bf16[16,3584]{1,0:T(8,128)(2,1)S(1)} %collective-permute-done.24.refs_4_.refs_3_, ...), custom_call_target="tpu_custom_call" | custom-call | tf_op jit(solution)/shard_map/inner/pallas_call | solution.py:284
  84.2 0.3 collective-permute-start.28
  84.5 1.1 %collective-permute-start.27 = (f32[4,64]{1,0:T(4,128)S(1)}, f32[4,64]{1,0:T(4,128)S(1)}, u32[]{:S(2)}, u32[]{:S(2)}) collective-permute-start(f32[4,64]{1,0:T(4,128)S(1)} %add.74.refs_6_.refs_3_), channel_id=1, source_target_pairs={{0,2},{1,3},{2,0},{3,1},{4,6},{5,7},{6,4},{7,5},{8,10},{9,11},{10,... | collective-permute-start | bytes 3080 | tf_op jit(solution)/shard_map/ppermute | solution.py:266
  85.6 0.5 collective-permute-start.26
  86.2 2.5 %basis.4 = (bf16[1024,7168]{1,0:T(8,128)(2,1)}, f32[8,128]{1,0:T(8,128)S(1)}) custom-call(bf16[1024,64]{1,0:T(8,128)(2,1)S(1)} %get-tuple-element.61.refs_0_, bf16[1024,7168]{1,0:T(8,128)(2,1)} %get-tuple-element.78.refs_1_, bf16[16,3584]{1,0:T(8,128)(2,1)S(1)} %collective-permute-done.23.refs_3_.refs_2_, ...), custom_call_target="tpu_custom_call", output_to_operand_aliasing={{0}: (1, {})} | custom-call | tf_op jit(solution)/shard_map/basis/pallas_call | solution.py:284
  88.7 2.4 %collective-permute-start.31 = (f32[4,64]{1,0:T(4,128)S(1)}, f32[4,64]{1,0:T(4,128)S(1)}, u32[]{:S(2)}, u32[]{:S(2)}) collective-permute-start(f32[4,64]{1,0:T(4,128)S(1)} %add.103.refs_6_.refs_3_), channel_id=1, source_target_pairs={{0,12},{1,13},{2,14},{3,15},{4,8},{5,9},{6,10},{7,11},{8,4},{9,5},... | collective-permute-start | bytes 3080 | tf_op jit(solution)/shard_map/ppermute | solution.py:266
  91.1 2.1 %collective-permute-start.29 = (f32[4,64]{1,0:T(4,128)S(1)}, f32[4,64]{1,0:T(4,128)S(1)}, u32[]{:S(2)}, u32[]{:S(2)}) collective-permute-start(f32[4,64]{1,0:T(4,128)S(1)} %add.103.refs_6_.refs_3_), channel_id=1, source_target_pairs={{0,4},{1,5},{2,6},{3,7},{4,0},{5,1},{6,2},{7,3},{8,12},{9,13},{10,... | collective-permute-start | bytes 3080 | tf_op jit(solution)/shard_map/ppermute | solution.py:266
  93.2 2.5 %basis.5 = (bf16[1024,7168]{1,0:T(8,128)(2,1)}, f32[8,128]{1,0:T(8,128)S(1)}) custom-call(bf16[1024,64]{1,0:T(8,128)(2,1)S(1)} %get-tuple-element.61.refs_0_, bf16[1024,7168]{1,0:T(8,128)(2,1)} %get-tuple-element.84.refs_1_, bf16[16,3584]{1,0:T(8,128)(2,1)S(1)} %collective-permute-done.23.refs_3_.refs_2_, ...), custom_call_target="tpu_custom_call", output_to_operand_aliasing={{0}: (1, {})} | custom-call | tf_op jit(solution)/shard_map/basis/pallas_call | solution.py:284
  95.7 0.6 add.104
  (31 shorter events, 0.2 us)
Async XLA Ops:
  0.6 33.6 %copy-start = (bf16[512,256]{1,0:T(8,128)(2,1)S(1)}, bf16[512,256]{1,0:T(8,128)(2,1)}, u32[]{:S(2)}) copy-start(bf16[512,256]{1,0:T(8,128)(2,1)} %param.5) | copy-start | bytes 786436
  0.7 0.7 copy-start.2
  5.4 9.4 %collective-permute-start.3 = (bf16[16,3584]{1,0:T(8,128)(2,1)S(1)}, bf16[16,3584]{1,0:T(8,128)(2,1)S(1)}, u32[]{:S(2)}, u32[]{:S(2)}) collective-permute-start(bf16[16,3584]{1,0:T(8,128)(2,1)S(1)} %get-tuple-element.52), channel_id=1, source_target_pairs={{0,12},{1,13},{2,14},{3,15},{4,8},{5,9},{6,10},{7,11},{8,4},{9,5},... | collective-permute-start | bytes 344072 | tf_op jit(solution)/shard_map/ppermute | solution.py:266
  10.5 9.7 %collective-permute-start.4 = (bf16[16,3584]{1,0:T(8,128)(2,1)S(1)}, bf16[16,3584]{1,0:T(8,128)(2,1)S(1)}, u32[]{:S(2)}, u32[]{:S(2)}) collective-permute-start(bf16[16,3584]{1,0:T(8,128)(2,1)S(1)} %get-tuple-element.53), channel_id=1, source_target_pairs={{0,8},{1,9},{2,10},{3,11},{4,12},{5,13},{6,14},{7,15},{8,0},{9,1},... | collective-permute-start | bytes 344072 | tf_op jit(solution)/shard_map/ppermute | solution.py:266
  10.5 9.7 %collective-permute-start.5 = (bf16[16,3584]{1,0:T(8,128)(2,1)S(1)}, bf16[16,3584]{1,0:T(8,128)(2,1)S(1)}, u32[]{:S(2)}, u32[]{:S(2)}) collective-permute-start(bf16[16,3584]{1,0:T(8,128)(2,1)S(1)} %get-tuple-element.54), channel_id=1, source_target_pairs={{0,4},{1,5},{2,6},{3,7},{4,0},{5,1},{6,2},{7,3},{8,12},{9,13},{10,... | collective-permute-start | bytes 344072 | tf_op jit(solution)/shard_map/ppermute | solution.py:266
  20.2 11.6 %collective-permute-start.9 = (bf16[64,3584]{1,0:T(8,128)(2,1)S(1)}, bf16[64,3584]{1,0:T(8,128)(2,1)S(1)}, u32[]{:S(2)}, u32[]{:S(2)}) collective-permute-start(bf16[64,3584]{1,0:T(8,128)(2,1)S(1)} %join.2.refs_4_.refs_3_), channel_id=1, source_target_pairs={{0,2},{1,3},{2,0},{3,1},{4,6},{5,7},{6,4},{7,5},{8,10},{9,11},{10,... | collective-permute-start | bytes 1376264 | tf_op jit(solution)/shard_map/ppermute | solution.py:266
  21.8 10.1 %collective-permute-start = (bf16[16,3584]{1,0:T(8,128)(2,1)S(1)}, bf16[16,3584]{1,0:T(8,128)(2,1)S(1)}, u32[]{:S(2)}, u32[]{:S(2)}) collective-permute-start(bf16[16,3584]{1,0:T(8,128)(2,1)S(1)} %get-tuple-element.48), channel_id=1, source_target_pairs={{0,12},{1,13},{2,14},{3,15},{4,8},{5,9},{6,10},{7,11},{8,4},{9,5},... | collective-permute-start | bytes 344072 | tf_op jit(solution)/shard_map/ppermute | solution.py:266
  24.3 9.3 %collective-permute-start.1 = (bf16[16,3584]{1,0:T(8,128)(2,1)S(1)}, bf16[16,3584]{1,0:T(8,128)(2,1)S(1)}, u32[]{:S(2)}, u32[]{:S(2)}) collective-permute-start(bf16[16,3584]{1,0:T(8,128)(2,1)S(1)} %get-tuple-element.49), channel_id=1, source_target_pairs={{0,8},{1,9},{2,10},{3,11},{4,12},{5,13},{6,14},{7,15},{8,0},{9,1},... | collective-permute-start | bytes 344072 | tf_op jit(solution)/shard_map/ppermute | solution.py:266
  24.3 9.3 %collective-permute-start.2 = (bf16[16,3584]{1,0:T(8,128)(2,1)S(1)}, bf16[16,3584]{1,0:T(8,128)(2,1)S(1)}, u32[]{:S(2)}, u32[]{:S(2)}) collective-permute-start(bf16[16,3584]{1,0:T(8,128)(2,1)S(1)} %get-tuple-element.50), channel_id=1, source_target_pairs={{0,4},{1,5},{2,6},{3,7},{4,0},{5,1},{6,2},{7,3},{8,12},{9,13},{10,... | collective-permute-start | bytes 344072 | tf_op jit(solution)/shard_map/ppermute | solution.py:266
  26.2 8.4 %collective-permute-start.10 = (bf16[64,3584]{1,0:T(8,128)(2,1)S(1)}, bf16[64,3584]{1,0:T(8,128)(2,1)S(1)}, u32[]{:S(2)}, u32[]{:S(2)}) collective-permute-start(bf16[64,3584]{1,0:T(8,128)(2,1)S(1)} %join.2.refs_4_.refs_3_), channel_id=1, source_target_pairs={{0,1},{1,0},{2,3},{3,2},{4,5},{5,4},{6,7},{7,6},{8,9},{9,8},{10,11... | collective-permute-start | bytes 1376264 | tf_op jit(solution)/shard_map/ppermute | solution.py:266
  31.9 2.8 %collective-permute-start.11 = (bf16[64,3584]{1,0:T(8,128)(2,1)S(1)}, bf16[64,3584]{1,0:T(8,128)(2,1)S(1)}, u32[]{:S(2)}, u32[]{:S(2)}) collective-permute-start(bf16[64,3584]{1,0:T(8,128)(2,1)S(1)} %collective-permute-done.9.refs_4_), channel_id=1, source_target_pairs={{0,1},{1,0},{2,3},{3,2},{4,5},{5,4},{6,7},{7,6},{8,9},{9,8},{10,11... | collective-permute-start | bytes 1376264 | tf_op jit(solution)/shard_map/ppermute | solution.py:266
  33.6 11.6 %collective-permute-start.6 = (bf16[64,3584]{1,0:T(8,128)(2,1)S(1)}, bf16[64,3584]{1,0:T(8,128)(2,1)S(1)}, u32[]{:S(2)}, u32[]{:S(2)}) collective-permute-start(bf16[64,3584]{1,0:T(8,128)(2,1)S(1)} %join.3.refs_7_.refs_3_), channel_id=1, source_target_pairs={{0,2},{1,3},{2,0},{3,1},{4,6},{5,7},{6,4},{7,5},{8,10},{9,11},{10,... | collective-permute-start | bytes 1376264 | tf_op jit(solution)/shard_map/ppermute | solution.py:266
  39.9 5.3 %collective-permute-start.12 = (bf16[64,3584]{1,0:T(8,128)(2,1)S(1)}, bf16[64,3584]{1,0:T(8,128)(2,1)S(1)}, u32[]{:S(2)}, u32[]{:S(2)}) collective-permute-start(bf16[64,3584]{1,0:T(8,128)(2,1)S(1)} %get-tuple-element.57), channel_id=1, source_target_pairs={{0,1},{1,0},{2,3},{3,2},{4,5},{5,4},{6,7},{7,6},{8,9},{9,8},{10,11... | collective-permute-start | bytes 1376264 | tf_op jit(solution)/shard_map/ppermute | solution.py:266
  40.0 5.3 %collective-permute-start.13 = (bf16[64,3584]{1,0:T(8,128)(2,1)S(1)}, bf16[64,3584]{1,0:T(8,128)(2,1)S(1)}, u32[]{:S(2)}, u32[]{:S(2)}) collective-permute-start(bf16[64,3584]{1,0:T(8,128)(2,1)S(1)} %get-tuple-element.58), channel_id=1, source_target_pairs={{0,1},{1,0},{2,3},{3,2},{4,5},{5,4},{6,7},{7,6},{8,9},{9,8},{10,11... | collective-permute-start | bytes 1376264 | tf_op jit(solution)/shard_map/ppermute | solution.py:266
  40.5 6.6 %collective-permute-start.7 = (bf16[64,3584]{1,0:T(8,128)(2,1)S(1)}, bf16[64,3584]{1,0:T(8,128)(2,1)S(1)}, u32[]{:S(2)}, u32[]{:S(2)}) collective-permute-start(bf16[64,3584]{1,0:T(8,128)(2,1)S(1)} %join.3.refs_7_.refs_3_), channel_id=1, source_target_pairs={{0,1},{1,0},{2,3},{3,2},{4,5},{5,4},{6,7},{7,6},{8,9},{9,8},{10,11... | collective-permute-start | bytes 1376264 | tf_op jit(solution)/shard_map/ppermute | solution.py:266
  45.2 1.8 %collective-permute-start.8 = (bf16[64,3584]{1,0:T(8,128)(2,1)S(1)}, bf16[64,3584]{1,0:T(8,128)(2,1)S(1)}, u32[]{:S(2)}, u32[]{:S(2)}) collective-permute-start(bf16[64,3584]{1,0:T(8,128)(2,1)S(1)} %collective-permute-done.6.refs_4_), channel_id=1, source_target_pairs={{0,1},{1,0},{2,3},{3,2},{4,5},{5,4},{6,7},{7,6},{8,9},{9,8},{10,11... | collective-permute-start | bytes 1376264 | tf_op jit(solution)/shard_map/ppermute | solution.py:266
  45.7 13.4 %collective-permute-start.14 = (bf16[64,3584]{1,0:T(8,128)(2,1)S(1)}, bf16[64,3584]{1,0:T(8,128)(2,1)S(1)}, u32[]{:S(2)}, u32[]{:S(2)}) collective-permute-start(bf16[64,3584]{1,0:T(8,128)(2,1)S(1)} %get-tuple-element.62), channel_id=1, source_target_pairs={{0,2},{1,3},{2,0},{3,1},{4,6},{5,7},{6,4},{7,5},{8,10},{9,11},{10,... | collective-permute-start | bytes 1376264 | tf_op jit(solution)/shard_map/ppermute | solution.py:266
  52.3 1.6 %collective-permute-start.15 = (bf16[32,3584]{1,0:T(8,128)(2,1)S(1)}, bf16[32,3584]{1,0:T(8,128)(2,1)S(1)}, u32[]{:S(2)}, u32[]{:S(2)}) collective-permute-start(bf16[32,3584]{1,0:T(8,128)(2,1)S(1)} %get-tuple-element.64), channel_id=1, source_target_pairs={{0,1},{1,0},{2,3},{3,2},{4,5},{5,4},{6,7},{7,6},{8,9},{9,8},{10,11... | collective-permute-start | bytes 688136 | tf_op jit(solution)/shard_map/ppermute | solution.py:266
  52.6 1.6 %collective-permute-start.16 = (bf16[32,3584]{1,0:T(8,128)(2,1)S(1)}, bf16[32,3584]{1,0:T(8,128)(2,1)S(1)}, u32[]{:S(2)}, u32[]{:S(2)}) collective-permute-start(bf16[32,3584]{1,0:T(8,128)(2,1)S(1)} %get-tuple-element.65), channel_id=1, source_target_pairs={{0,1},{1,0},{2,3},{3,2},{4,5},{5,4},{6,7},{7,6},{8,9},{9,8},{10,11... | collective-permute-start | bytes 688136 | tf_op jit(solution)/shard_map/ppermute | solution.py:266
  52.9 1.6 %collective-permute-start.17 = (bf16[32,3584]{1,0:T(8,128)(2,1)S(1)}, bf16[32,3584]{1,0:T(8,128)(2,1)S(1)}, u32[]{:S(2)}, u32[]{:S(2)}) collective-permute-start(bf16[32,3584]{1,0:T(8,128)(2,1)S(1)} %get-tuple-element.66), channel_id=1, source_target_pairs={{0,1},{1,0},{2,3},{3,2},{4,5},{5,4},{6,7},{7,6},{8,9},{9,8},{10,11... | collective-permute-start | bytes 688136 | tf_op jit(solution)/shard_map/ppermute | solution.py:266
  53.1 1.8 %collective-permute-start.18 = (bf16[32,3584]{1,0:T(8,128)(2,1)S(1)}, bf16[32,3584]{1,0:T(8,128)(2,1)S(1)}, u32[]{:S(2)}, u32[]{:S(2)}) collective-permute-start(bf16[32,3584]{1,0:T(8,128)(2,1)S(1)} %get-tuple-element.67), channel_id=1, source_target_pairs={{0,1},{1,0},{2,3},{3,2},{4,5},{5,4},{6,7},{7,6},{8,9},{9,8},{10,11... | collective-permute-start | bytes 688136 | tf_op jit(solution)/shard_map/ppermute | solution.py:266
  55.3 13.2 %collective-permute-start.22 = (bf16[64,3584]{1,0:T(8,128)(2,1)S(1)}, bf16[64,3584]{1,0:T(8,128)(2,1)S(1)}, u32[]{:S(2)}, u32[]{:S(2)}) collective-permute-start(bf16[64,3584]{1,0:T(8,128)(2,1)S(1)} %get-tuple-element.75), channel_id=1, source_target_pairs={{0,2},{1,3},{2,0},{3,1},{4,6},{5,7},{6,4},{7,5},{8,10},{9,11},{10,... | collective-permute-start | bytes 1376264 | tf_op jit(solution)/shard_map/ppermute | solution.py:266
  59.4 11.8 %collective-permute-start.19 = (bf16[16,3584]{1,0:T(8,128)(2,1)S(1)}, bf16[16,3584]{1,0:T(8,128)(2,1)S(1)}, u32[]{:S(2)}, u32[]{:S(2)}) collective-permute-start(bf16[16,3584]{1,0:T(8,128)(2,1)S(1)} %get-tuple-element.70), channel_id=1, source_target_pairs={{0,12},{1,13},{2,14},{3,15},{4,8},{5,9},{6,10},{7,11},{8,4},{9,5},... | collective-permute-start | bytes 344072 | tf_op jit(solution)/shard_map/ppermute | solution.py:266
  63.0 10.3 %collective-permute-start.20 = (bf16[16,3584]{1,0:T(8,128)(2,1)S(1)}, bf16[16,3584]{1,0:T(8,128)(2,1)S(1)}, u32[]{:S(2)}, u32[]{:S(2)}) collective-permute-start(bf16[16,3584]{1,0:T(8,128)(2,1)S(1)} %get-tuple-element.71), channel_id=1, source_target_pairs={{0,8},{1,9},{2,10},{3,11},{4,12},{5,13},{6,14},{7,15},{8,0},{9,1},... | collective-permute-start | bytes 344072 | tf_op jit(solution)/shard_map/ppermute | solution.py:266
  63.0 10.3 %collective-permute-start.21 = (bf16[16,3584]{1,0:T(8,128)(2,1)S(1)}, bf16[16,3584]{1,0:T(8,128)(2,1)S(1)}, u32[]{:S(2)}, u32[]{:S(2)}) collective-permute-start(bf16[16,3584]{1,0:T(8,128)(2,1)S(1)} %get-tuple-element.72), channel_id=1, source_target_pairs={{0,4},{1,5},{2,6},{3,7},{4,0},{5,1},{6,2},{7,3},{8,12},{9,13},{10,... | collective-permute-start | bytes 344072 | tf_op jit(solution)/shard_map/ppermute | solution.py:266
  68.8 12.4 %collective-permute-start.23 = (bf16[16,3584]{1,0:T(8,128)(2,1)S(1)}, bf16[16,3584]{1,0:T(8,128)(2,1)S(1)}, u32[]{:S(2)}, u32[]{:S(2)}) collective-permute-start(bf16[16,3584]{1,0:T(8,128)(2,1)S(1)} %get-tuple-element.79), channel_id=1, source_target_pairs={{0,12},{1,13},{2,14},{3,15},{4,8},{5,9},{6,10},{7,11},{8,4},{9,5},... | collective-permute-start | bytes 344072 | tf_op jit(solution)/shard_map/ppermute | solution.py:266
  71.2 10.1 %collective-permute-start.24 = (bf16[16,3584]{1,0:T(8,128)(2,1)S(1)}, bf16[16,3584]{1,0:T(8,128)(2,1)S(1)}, u32[]{:S(2)}, u32[]{:S(2)}) collective-permute-start(bf16[16,3584]{1,0:T(8,128)(2,1)S(1)} %get-tuple-element.80), channel_id=1, source_target_pairs={{0,8},{1,9},{2,10},{3,11},{4,12},{5,13},{6,14},{7,15},{8,0},{9,1},... | collective-permute-start | bytes 344072 | tf_op jit(solution)/shard_map/ppermute | solution.py:266
  71.2 10.1 %collective-permute-start.25 = (bf16[16,3584]{1,0:T(8,128)(2,1)S(1)}, bf16[16,3584]{1,0:T(8,128)(2,1)S(1)}, u32[]{:S(2)}, u32[]{:S(2)}) collective-permute-start(bf16[16,3584]{1,0:T(8,128)(2,1)S(1)} %get-tuple-element.81), channel_id=1, source_target_pairs={{0,4},{1,5},{2,6},{3,7},{4,0},{5,1},{6,2},{7,3},{8,12},{9,13},{10,... | collective-permute-start | bytes 344072 | tf_op jit(solution)/shard_map/ppermute | solution.py:266
  84.2 4.4 %collective-permute-start.28 = (f32[4,64]{1,0:T(4,128)S(1)}, f32[4,64]{1,0:T(4,128)S(1)}, u32[]{:S(2)}, u32[]{:S(2)}) collective-permute-start(f32[4,64]{1,0:T(4,128)S(1)} %add.74.refs_6_.refs_3_), channel_id=1, source_target_pairs={{0,3},{1,2},{2,1},{3,0},{4,7},{5,6},{6,5},{7,4},{8,11},{9,10},{10,... | collective-permute-start | bytes 3080 | tf_op jit(solution)/shard_map/ppermute | solution.py:266
  84.5 4.2 %collective-permute-start.27 = (f32[4,64]{1,0:T(4,128)S(1)}, f32[4,64]{1,0:T(4,128)S(1)}, u32[]{:S(2)}, u32[]{:S(2)}) collective-permute-start(f32[4,64]{1,0:T(4,128)S(1)} %add.74.refs_6_.refs_3_), channel_id=1, source_target_pairs={{0,2},{1,3},{2,0},{3,1},{4,6},{5,7},{6,4},{7,5},{8,10},{9,11},{10,... | collective-permute-start | bytes 3080 | tf_op jit(solution)/shard_map/ppermute | solution.py:266
  85.6 3.1 %collective-permute-start.26 = (f32[4,64]{1,0:T(4,128)S(1)}, f32[4,64]{1,0:T(4,128)S(1)}, u32[]{:S(2)}, u32[]{:S(2)}) collective-permute-start(f32[4,64]{1,0:T(4,128)S(1)} %add.74.refs_6_.refs_3_), channel_id=1, source_target_pairs={{0,1},{1,0},{2,3},{3,2},{4,5},{5,4},{6,7},{7,6},{8,9},{9,8},{10,11... | collective-permute-start | bytes 3080 | tf_op jit(solution)/shard_map/ppermute | solution.py:266
  88.7 7.0 %collective-permute-start.31 = (f32[4,64]{1,0:T(4,128)S(1)}, f32[4,64]{1,0:T(4,128)S(1)}, u32[]{:S(2)}, u32[]{:S(2)}) collective-permute-start(f32[4,64]{1,0:T(4,128)S(1)} %add.103.refs_6_.refs_3_), channel_id=1, source_target_pairs={{0,12},{1,13},{2,14},{3,15},{4,8},{5,9},{6,10},{7,11},{8,4},{9,5},... | collective-permute-start | bytes 3080 | tf_op jit(solution)/shard_map/ppermute | solution.py:266
  91.1 4.6 %collective-permute-start.30 = (f32[4,64]{1,0:T(4,128)S(1)}, f32[4,64]{1,0:T(4,128)S(1)}, u32[]{:S(2)}, u32[]{:S(2)}) collective-permute-start(f32[4,64]{1,0:T(4,128)S(1)} %add.103.refs_6_.refs_3_), channel_id=1, source_target_pairs={{0,8},{1,9},{2,10},{3,11},{4,12},{5,13},{6,14},{7,15},{8,0},{9,1},... | collective-permute-start | bytes 3080 | tf_op jit(solution)/shard_map/ppermute | solution.py:266
  91.1 4.6 %collective-permute-start.29 = (f32[4,64]{1,0:T(4,128)S(1)}, f32[4,64]{1,0:T(4,128)S(1)}, u32[]{:S(2)}, u32[]{:S(2)}) collective-permute-start(f32[4,64]{1,0:T(4,128)S(1)} %add.103.refs_6_.refs_3_), channel_id=1, source_target_pairs={{0,4},{1,5},{2,6},{3,7},{4,0},{5,1},{6,2},{7,3},{8,12},{9,13},{10,... | collective-permute-start | bytes 3080 | tf_op jit(solution)/shard_map/ppermute | solution.py:266
  93.2 3.1 %copy-start.1 = (bf16[512,256]{1,0:T(8,128)(2,1)S(1)}, bf16[512,256]{1,0:T(8,128)(2,1)}, u32[]{:S(2)}) copy-start(bf16[512,256]{1,0:T(8,128)(2,1)} %param.5) | copy-start | bytes 786436
